TPU v7x, 32 devices: a whole 2x2x4 slice. The times are simulated.
32 devices in a mesh: section: 2 (over core), dp: 4 (over z), seq: 4 (over y, x).
Axes of the slice: x: 2, y: 2, z: 4, core: 2. Of those that a mesh axis runs over, the one named last changes fastest.
Arguments:
- inputs: bfloat16 [12, 1024, 1600], P('dp', 'seq'), may hold values from -6 to 6
- cotangent: bfloat16 [12, 1024, 1600], P('dp', 'seq'), may hold values from -6 to 6
- lengths: int32 [12], replicated, may hold values from 256 to 1024, as said below
- dealing: int32 [12], replicated, may hold values from 0 to 11, as said below
- query_key_value_weight: bfloat16 [2, 1600, 4800], P('section', ('dp', 'seq')), may hold values from -0.15625 to 0.15625
- b_qv: bfloat16 [2, 3200], P('section', ('dp', 'seq')), may hold values from -3 to 3
- attention_out_weight: bfloat16 [2, 1600, 1600], P('section', ('dp', 'seq')), may hold values from -0.625 to 0.625
- attention_out_bias: bfloat16 [2, 1600], P('section', ('dp', 'seq')), may hold values from -3 to 3
- up_weight: bfloat16 [2, 1600, 6400], P('section', ('dp', 'seq')), may hold values from -0.15625 to 0.15625
- up_bias: bfloat16 [2, 6400], P('section', ('dp', 'seq')), may hold values from -3 to 3
- down_weight: bfloat16 [2, 6400, 1600], P('section', ('dp', 'seq')), may hold values from -0.078125 to 0.078125
- down_bias: bfloat16 [2, 1600], P('section', ('dp', 'seq')), may hold values from -3 to 3
- gain_one: bfloat16 [2, 1600], P('section', ('dp', 'seq')), may hold values from 0.099609375 to 1.8984375
- shift_one: bfloat16 [2, 1600], P('section', ('dp', 'seq')), may hold values from -3 to 3
- gain_two: bfloat16 [2, 1600], P('section', ('dp', 'seq')), may hold values from 0.099609375 to 1.8984375
- shift_two: bfloat16 [2, 1600], P('section', ('dp', 'seq')), may hold values from -3 to 3
Outputs:
- acts: bfloat16 [2, 12, 1024, 1600], P('section', 'dp', 'seq')
- input_grad: bfloat16 [2, 12, 1024, 1600], P('section', 'dp', 'seq')
- grad_w_qkv: float32 [2, 1600, 4800], P('section', ('dp', 'seq'))
- grad_b_qv: float32 [2, 3200], P('section', ('dp', 'seq'))
- grad_w_out: float32 [2, 1600, 1600], P('section', ('dp', 'seq'))
- grad_b_out: float32 [2, 1600], P('section', ('dp', 'seq'))
- grad_w_up: float32 [2, 1600, 6400], P('section', ('dp', 'seq'))
- grad_b_up: float32 [2, 6400], P('section', ('dp', 'seq'))
- grad_w_down: float32 [2, 6400, 1600], P('section', ('dp', 'seq'))
- grad_b_down: float32 [2, 1600], P('section', ('dp', 'seq'))
- grad_gain_one: float32 [2, 1600], P('section', ('dp', 'seq'))
- grad_shift_one: float32 [2, 1600], P('section', ('dp', 'seq'))
- grad_gain_two: float32 [2, 1600], P('section', ('dp', 'seq'))
- grad_shift_two: float32 [2, 1600], P('section', ('dp', 'seq'))
Inputs may be any that keep to these rules, and one draw needn't show every extreme that they name: dealing is a permutation; the 3 sequences of one group come from 3 different aligned blocks of 3 input sequences, and the sequences of one block go to different groups. `lengths`: every group takes one sequence of length 1024.
All inputs are finite; a program needn't handle non-finite values.
Results may differ from a plain program's by a relative error of at most 0.018.
Values may be sent and summed in bfloat16 or wider, within the bound.
No kernel may reach another device: no remote copies, remote signals or barrier semaphores. Data moves between devices by JAX's collectives and lax.ppermute only.
A program may use at most 448 MiB of HBM per device.

v0:
```python
import jax
import jax.numpy as jnp
from jax import lax
from jax.sharding import PartitionSpec as P

H = 25
HD = 64


def passed_along(value, axis, by):
    count = lax.axis_size(axis)
    pairs = [(i, i + by) for i in range(count) if 0 <= i + by < count]
    return lax.ppermute(value, axis, pairs)


def shortened(value):

    def short(part):
        return part.astype(jnp.bfloat16) if part.dtype == jnp.float32 else part

    return jax.tree.map(short, value)


def normalize(row_block, gain_vec, shift_vec):
    average = jnp.mean(row_block, axis=-1, keepdims=True)
    centered = row_block - average
    variance = jnp.mean(centered * centered, axis=-1, keepdims=True)
    return centered * lax.rsqrt(variance + 1e-05) * gain_vec + shift_vec


def smooth(up_projected):
    return jax.nn.gelu(up_projected, approximate=True)


def score_block(attention_projected, context, first_row, length):
    model_width = context.shape[1] // 2
    query_count = attention_projected.shape[0]
    key_count = context.shape[0]
    queries = attention_projected[:, :model_width].reshape(query_count, H, HD)
    key_rows = context[:, :model_width].reshape(key_count, H, HD)
    value_rows = context[:, model_width:].reshape(key_count, H, HD)
    scores = jnp.einsum(
        "qhd,khd->hqk", queries, key_rows, preferred_element_type=jnp.float32
    ) * HD ** (-0.5)
    query_pos = first_row + jnp.arange(query_count, dtype=jnp.int32)
    key_pos = jnp.arange(key_count, dtype=jnp.int32)
    allowed = (key_pos[None, :] <= query_pos[:, None]) & (key_pos[None, :] < length)
    scores = jnp.where(allowed[None], scores, -1e30)
    return (queries, key_rows, value_rows, scores)


def layer_forward(row_block, gathered, length, first_row):
    (
        query_key_value_weight,
        b_qv,
        attention_out_weight,
        attention_out_bias,
        up_weight,
        up_bias,
        down_weight,
        down_bias,
        gain_one,
        shift_one,
        gain_two,
        shift_two,
    ) = gathered
    model_width = row_block.shape[1]
    normalized_first = normalize(
        row_block, gain_one.astype(jnp.float32), shift_one.astype(jnp.float32)
    ).astype(jnp.bfloat16)
    bias_full = b_qv.astype(jnp.float32)
    query_key_value_bias = jnp.concatenate(
        [bias_full[:model_width], jnp.zeros((model_width,), jnp.float32), bias_full[model_width:]]
    )
    attention_projected = (
        jnp.dot(normalized_first, query_key_value_weight, preferred_element_type=jnp.float32)
        + query_key_value_bias
    ).astype(jnp.bfloat16)
    context = lax.all_gather(attention_projected[:, model_width:], "seq", axis=0, tiled=True)
    queries, key_rows, value_rows, scores = score_block(
        attention_projected, context, first_row, length
    )
    maxima = jnp.max(scores, axis=-1, keepdims=True)
    weights = jnp.exp(scores - maxima)
    denominator = jnp.sum(weights, axis=-1, keepdims=True)
    probabilities = (weights / denominator).astype(jnp.bfloat16)
    attention_result = jnp.einsum(
        "hqk,khd->qhd", probabilities, value_rows, preferred_element_type=jnp.float32
    )
    attention_result = attention_result.reshape(row_block.shape[0], model_width).astype(
        jnp.bfloat16
    )
    middle = (
        row_block
        + jnp.dot(attention_result, attention_out_weight, preferred_element_type=jnp.float32)
        + attention_out_bias.astype(jnp.float32)
    )
    normalized_second = normalize(
        middle, gain_two.astype(jnp.float32), shift_two.astype(jnp.float32)
    ).astype(jnp.bfloat16)
    up_projected = jnp.dot(
        normalized_second, up_weight, preferred_element_type=jnp.float32
    ) + up_bias.astype(jnp.float32)
    hidden_units = smooth(up_projected).astype(jnp.bfloat16)
    output = (
        middle
        + jnp.dot(hidden_units, down_weight, preferred_element_type=jnp.float32)
        + down_bias.astype(jnp.float32)
    )
    stored = (
        row_block,
        normalized_first,
        attention_projected,
        context,
        maxima,
        denominator,
        attention_result,
        middle,
        normalized_second,
        up_projected,
        hidden_units,
    )
    return (output, stored)


def layer_backward(grad_out, stored, gathered, length, first_row):
    (
        query_key_value_weight,
        b_qv,
        attention_out_weight,
        attention_out_bias,
        up_weight,
        up_bias,
        down_weight,
        down_bias,
        gain_one,
        shift_one,
        gain_two,
        shift_two,
    ) = gathered
    (
        row_block,
        normalized_first,
        attention_projected,
        kept_context,
        maxima,
        denominator,
        attention_result,
        middle,
        normalized_second,
        up_projected,
        hidden_units,
    ) = stored
    model_width = row_block.shape[1]
    row_count = row_block.shape[0]
    grad_down = grad_out.astype(jnp.bfloat16)
    grad_b_down = jnp.sum(grad_down.astype(jnp.float32), axis=0)
    grad_hidden = jnp.einsum(
        "rd,fd->rf", grad_down, down_weight, preferred_element_type=jnp.float32
    )
    unused_value, gelu_back = jax.vjp(smooth, up_projected)
    grad_up = gelu_back(grad_hidden)[0].astype(jnp.bfloat16)
    grad_b_up = jnp.sum(grad_up.astype(jnp.float32), axis=0)
    grad_normed_two = jnp.einsum(
        "rf,df->rd", grad_up, up_weight, preferred_element_type=jnp.float32
    )
    unused_norm, norm_back_two = jax.vjp(
        normalize, middle, gain_two.astype(jnp.float32), shift_two.astype(jnp.float32)
    )
    grad_middle, grad_gain_two, grad_shift_two = norm_back_two(grad_normed_two)
    grad_middle = grad_middle + grad_out
    grad_branch = grad_middle.astype(jnp.bfloat16)
    grad_b_out = jnp.sum(grad_branch.astype(jnp.float32), axis=0)
    grad_attended = jnp.einsum(
        "re,de->rd", grad_branch, attention_out_weight, preferred_element_type=jnp.float32
    ).astype(jnp.bfloat16)
    queries, key_rows, value_rows, scores = score_block(
        attention_projected, kept_context, first_row, length
    )
    probabilities = jnp.exp(scores - maxima) / denominator
    probs_low = probabilities.astype(jnp.bfloat16)
    grad_heads = grad_attended.reshape(row_count, H, HD)
    grad_probs = jnp.einsum(
        "qhd,khd->hqk", grad_heads, value_rows, preferred_element_type=jnp.float32
    )
    grad_scores = probabilities * (
        grad_probs - jnp.sum(probabilities * grad_probs, axis=-1, keepdims=True)
    )
    grad_scores = grad_scores.astype(jnp.bfloat16)
    score_scale = HD ** (-0.5)
    grad_queries = (
        jnp.einsum("hqk,khd->qhd", grad_scores, key_rows, preferred_element_type=jnp.float32)
        * score_scale
    )
    grad_keys = (
        jnp.einsum("hqk,qhd->khd", grad_scores, queries, preferred_element_type=jnp.float32)
        * score_scale
    )
    grad_values = jnp.einsum(
        "hqk,qhd->khd", probs_low, grad_heads, preferred_element_type=jnp.float32
    )
    key_count = kept_context.shape[0]
    grad_context = jnp.concatenate(
        [grad_keys.reshape(key_count, model_width), grad_values.reshape(key_count, model_width)],
        axis=1,
    )
    grad_context = lax.psum_scatter(
        grad_context.astype(jnp.bfloat16), "seq", scatter_dimension=0, tiled=True
    ).astype(jnp.float32)
    grad_projected = jnp.concatenate(
        [grad_queries.reshape(row_count, model_width), grad_context], axis=1
    ).astype(jnp.bfloat16)
    column_sums = jnp.sum(grad_projected.astype(jnp.float32), axis=0)
    grad_b_qv = jnp.concatenate([column_sums[:model_width], column_sums[2 * model_width :]])
    grad_normed = jnp.einsum(
        "re,de->rd", grad_projected, query_key_value_weight, preferred_element_type=jnp.float32
    )
    unused_first, norm_back_one = jax.vjp(
        normalize, row_block, gain_one.astype(jnp.float32), shift_one.astype(jnp.float32)
    )
    grad_rows, grad_gain_one, grad_shift_one = norm_back_one(grad_normed)
    grad_rows = grad_rows + grad_middle
    small_terms = (
        grad_b_qv,
        grad_b_out,
        grad_b_up,
        grad_b_down,
        grad_gain_one,
        grad_shift_one,
        grad_gain_two,
        grad_shift_two,
    )
    operands = (
        normalized_first,
        grad_projected,
        attention_result,
        grad_branch,
        normalized_second,
        grad_up,
        hidden_units,
        grad_down,
    )
    return (grad_rows, small_terms, operands)


def per_device(
    inputs,
    cotangent,
    lengths,
    dealing,
    query_key_value_weight,
    b_qv,
    attention_out_weight,
    attention_out_bias,
    up_weight,
    up_bias,
    down_weight,
    down_bias,
    gain_one,
    shift_one,
    gain_two,
    shift_two,
):
    micro_count, block_rows, model_width = inputs.shape
    group_count = lax.axis_size("dp")
    group_index = lax.axis_index("dp")
    seq_index = lax.axis_index("seq")
    section_index = lax.axis_index("section")
    is_first = section_index == 0
    total_seqs = dealing.shape[0]
    numbers = jnp.arange(total_seqs, dtype=jnp.int32)
    position = jnp.sum(jnp.where(dealing[:, None] == numbers[None, :], numbers[:, None], 0), axis=0)
    own_ids = group_index * micro_count + jnp.arange(micro_count, dtype=jnp.int32)
    own_position = jnp.sum(
        jnp.where(numbers[None, :] == own_ids[:, None], position[None, :], 0), axis=1
    )
    target = own_position // micro_count
    group_ids = jnp.arange(group_count, dtype=jnp.int32)
    sending = (group_ids[:, None] == target[None, :]).astype(jnp.bfloat16)
    slot_ids = lax.dynamic_slice_in_dim(dealing, group_index * micro_count, micro_count)
    anchor = slot_ids // micro_count
    picking = (anchor[:, None] == group_ids[None, :]).astype(jnp.bfloat16)
    slot_lengths = jnp.sum(
        jnp.where(slot_ids[:, None] == numbers[None, :], lengths[None, :], 0), axis=1
    )
    packed_inputs = jnp.einsum(
        "gi,icd->gcd", sending, inputs, preferred_element_type=jnp.float32
    ).astype(jnp.bfloat16)
    packed_grads = jnp.einsum(
        "gi,icd->gcd", sending, cotangent, preferred_element_type=jnp.float32
    ).astype(jnp.bfloat16)
    arrived = (
        lax.all_to_all(packed_inputs, "dp", split_axis=0, concat_axis=0, tiled=True),
        lax.all_to_all(packed_grads, "dp", split_axis=0, concat_axis=0, tiled=True),
    )
    local_inputs = jnp.einsum(
        "jg,gcd->jcd", picking, arrived[0], preferred_element_type=jnp.float32
    ).astype(jnp.bfloat16)
    local_grads = jnp.einsum("jg,gcd->jcd", picking, arrived[1], preferred_element_type=jnp.float32)
    first_row = seq_index * block_rows
    row_pos = first_row + jnp.arange(block_rows, dtype=jnp.int32)
    valid = (row_pos[None, :] < slot_lengths[:, None]).astype(jnp.float32)
    local_grads = local_grads * valid[:, :, None]
    shards = (
        query_key_value_weight[0],
        b_qv[0],
        attention_out_weight[0],
        attention_out_bias[0],
        up_weight[0],
        up_bias[0],
        down_weight[0],
        down_bias[0],
        gain_one[0],
        shift_one[0],
        gain_two[0],
        shift_two[0],
    )
    gathered = (
        lax.all_gather(shards[0], ("dp", "seq"), axis=0, tiled=True),
        lax.all_gather(shards[1], ("dp", "seq"), axis=0, tiled=True),
        lax.all_gather(shards[2], ("dp", "seq"), axis=0, tiled=True),
        lax.all_gather(shards[3], ("dp", "seq"), axis=0, tiled=True),
        lax.all_gather(shards[4], ("dp", "seq"), axis=0, tiled=True),
        lax.all_gather(shards[5], ("dp", "seq"), axis=0, tiled=True),
        lax.all_gather(shards[6], ("dp", "seq"), axis=0, tiled=True),
        lax.all_gather(shards[7], ("dp", "seq"), axis=0, tiled=True),
        lax.all_gather(shards[8], ("dp", "seq"), axis=0, tiled=True),
        lax.all_gather(shards[9], ("dp", "seq"), axis=0, tiled=True),
        lax.all_gather(shards[10], ("dp", "seq"), axis=0, tiled=True),
        lax.all_gather(shards[11], ("dp", "seq"), axis=0, tiled=True),
    )
    zeros_rows = jnp.zeros((block_rows, model_width), jnp.bfloat16)
    incoming = zeros_rows
    outputs = []
    stored_list = []
    for moment in range(micro_count + 1):
        own_rows = local_inputs[min(moment, micro_count - 1)]
        row_block = jnp.where(is_first, own_rows, incoming).astype(jnp.float32)
        length = jnp.where(
            is_first, slot_lengths[min(moment, micro_count - 1)], slot_lengths[max(moment - 1, 0)]
        )
        output, stored = layer_forward(row_block, gathered, length, first_row)
        handed = output.astype(jnp.bfloat16)
        outputs.append(handed)
        stored_list.append(stored)
        if moment < micro_count:
            incoming = passed_along(handed, "section", 1)
    acts = jnp.stack(
        [jnp.where(is_first, outputs[index], outputs[index + 1]) for index in range(micro_count)]
    )
    received = zeros_rows
    small_totals = None
    sent_back = []
    operand_list = []
    for moment in range(micro_count + 1):
        former = stored_list[max(moment - 1, 0)]
        latter = stored_list[min(moment + 1, micro_count)]
        stored = jax.tree.map(
            lambda early_part, late_part: jnp.where(is_first, early_part, late_part), former, latter
        )
        if moment < micro_count:
            start_grad = local_grads[moment]
        else:
            start_grad = jnp.zeros((block_rows, model_width), jnp.float32)
        grad_out = jnp.where(is_first, received.astype(jnp.float32), start_grad)
        length = jnp.where(
            is_first, slot_lengths[max(moment - 1, 0)], slot_lengths[min(moment, micro_count - 1)]
        )
        grad_rows, small_terms, operands = layer_backward(
            grad_out, stored, gathered, length, first_row
        )
        returned = grad_rows.astype(jnp.bfloat16)
        sent_back.append(returned)
        operand_list.append(operands)
        if small_totals is None:
            small_totals = small_terms
        else:
            small_totals = jax.tree.map(jnp.add, small_totals, small_terms)
        if moment < micro_count:
            received = passed_along(returned, "section", -1)
    chosen = [
        jax.tree.map(
            lambda early_part, late_part: jnp.where(is_first, early_part, late_part),
            operand_list[index + 1],
            operand_list[index],
        )
        for index in range(micro_count)
    ]
    joined = [jnp.concatenate([picked[member] for picked in chosen], axis=0) for member in range(8)]
    grad_w_qkv = jnp.einsum("rd,re->de", joined[0], joined[1], preferred_element_type=jnp.float32)
    grad_w_out = jnp.einsum("rd,re->de", joined[2], joined[3], preferred_element_type=jnp.float32)
    grad_w_up = jnp.einsum("rd,rf->df", joined[4], joined[5], preferred_element_type=jnp.float32)
    grad_w_down = jnp.einsum("rf,rd->fd", joined[6], joined[7], preferred_element_type=jnp.float32)
    (
        grad_b_qv,
        grad_b_out,
        grad_b_up,
        grad_b_down,
        grad_gain_one,
        grad_shift_one,
        grad_gain_two,
        grad_shift_two,
    ) = small_totals
    totals = (
        grad_w_qkv,
        grad_b_qv,
        grad_w_out,
        grad_b_out,
        grad_w_up,
        grad_b_up,
        grad_w_down,
        grad_b_down,
        grad_gain_one,
        grad_shift_one,
        grad_gain_two,
        grad_shift_two,
    )
    grad_local = jnp.stack(
        [
            jnp.where(is_first, sent_back[index + 1], sent_back[index])
            for index in range(micro_count)
        ]
    )
    outgoing = jnp.einsum(
        "jg,jcd->gcd", picking, grad_local, preferred_element_type=jnp.float32
    ).astype(jnp.bfloat16)
    returned_all = lax.all_to_all(outgoing, "dp", split_axis=0, concat_axis=0, tiled=True)
    input_grad = jnp.einsum(
        "gi,gcd->icd", sending, returned_all, preferred_element_type=jnp.float32
    ).astype(jnp.bfloat16)
    folded = tuple(
        (
            gradient.reshape((group_count, gradient.shape[0] // group_count) + gradient.shape[1:])
            for gradient in totals
        )
    )
    inside = jax.tree.map(
        lambda part: part.astype(jnp.float32),
        lax.psum_scatter(shortened(folded), "seq", scatter_dimension=1, tiled=True),
    )
    results = jax.tree.map(
        lambda part: part.astype(jnp.float32),
        lax.psum_scatter(shortened(inside), "dp", scatter_dimension=0, tiled=True),
    )
    return (
        acts[None],
        input_grad[None],
        results[0],
        results[1],
        results[2],
        results[3],
        results[4],
        results[5],
        results[6],
        results[7],
        results[8],
        results[9],
        results[10],
        results[11],
    )


def solution(mesh):
    in_specs = (
        P("dp", "seq", None),
        P("dp", "seq", None),
        P(),
        P(),
        P("section", ("dp", "seq"), None),
        P("section", ("dp", "seq")),
        P("section", ("dp", "seq"), None),
        P("section", ("dp", "seq")),
        P("section", ("dp", "seq"), None),
        P("section", ("dp", "seq")),
        P("section", ("dp", "seq"), None),
        P("section", ("dp", "seq")),
        P("section", ("dp", "seq")),
        P("section", ("dp", "seq")),
        P("section", ("dp", "seq")),
        P("section", ("dp", "seq")),
    )
    out_specs = (
        P("section", "dp", "seq", None),
        P("section", "dp", "seq", None),
        P("section", ("dp", "seq"), None),
        P("section", ("dp", "seq")),
        P("section", ("dp", "seq"), None),
        P("section", ("dp", "seq")),
        P("section", ("dp", "seq"), None),
        P("section", ("dp", "seq")),
        P("section", ("dp", "seq"), None),
        P("section", ("dp", "seq")),
        P("section", ("dp", "seq")),
        P("section", ("dp", "seq")),
        P("section", ("dp", "seq")),
        P("section", ("dp", "seq")),
    )
    return jax.shard_map(
        per_device, mesh=mesh, in_specs=in_specs, out_specs=out_specs, check_vma=False
    )
```

profile of v0, /device:TPU:1, one launch (start us, length us, event | category | flops | bytes accessed | tf_op | source)
XLA Modules:
  0.0 4020.9 jit_solution(16818658656332709122)
XLA Ops:
  39.2 192.0 %all-reduce.28 = (bf16[3200]{0:T(1024)(128)(2,1)S(1)}, bf16[1600]{0:T(1024)(128)(2,1)S(1)}, bf16[1600]{0:T(1024)(128)(2,1)S(1)}, bf16[1600]{0:T(1024)(128)(2,1)S...) all-reduce(bf16[3200]{0:T(1024)(128)(2,1)S(1)} %dynamic-update-slic, ...), channel_id=5, replica_groups=mesh['section'=2,'dp'=4,'seq'=4] {'dp','seq'}, use_global_device_ids=true, to_apply=%add.2 | all-reduce | flops 19200 | bytes 76800
  247.9 154.5 %all-gather.29.cloned.1.call-done = bf16[1,1600,4800]{2,0,1:T(2,128)(2,1)} async-done(((bf16[1,100,4800]{2,0,1:T(2,128)(2,1)}), bf16[1,1600,4800]{2,0,1:T(2,128)(2,1)}) %all-gather.29.cloned.1.call-update) | async-done | bytes 15360016 | tf_op jit(solution)/shard_map/all_gather | solution.py:319
  402.5 20.5 copy.172
  423.0 14.3 fusion.184
  449.9 87.7 %all-gather.31.cloned.1.call-done = bf16[1,1600,1600]{2,0,1:T(2,128)(2,1)} async-done(((bf16[1,100,1600]{2,0,1:T(2,128)(2,1)}), bf16[1,1600,1600]{2,0,1:T(2,128)(2,1)}) %all-gather.31.cloned.1.call-update) | async-done | bytes 5120016 | tf_op jit(solution)/shard_map/all_gather | solution.py:321
  544.9 415.0 %all-gather.33.cloned.1.call-done = bf16[1,1600,6400]{2,0,1:T(2,128)(2,1)} async-done(((bf16[1,100,6400]{2,0,1:T(2,128)(2,1)}), bf16[1,1600,6400]{2,0,1:T(2,128)(2,1)}) %all-gather.33.cloned.1.call-update) | async-done | bytes 20480016 | tf_op jit(solution)/shard_map/all_gather | solution.py:323
  960.0 25.8 copy.174
  985.7 47.3 %all-gather.21.cloned.1.call-done = bf16[1024,3200]{0,1:T(8,128)(2,1)} async-done(((bf16[256,3200]{0,1:T(8,128)(2,1)}), bf16[1024,3200]{0,1:T(8,128)(2,1)}) %all-gather.21.cloned.1.call-update) | async-done | bytes 6553616 | tf_op jit(solution)/shard_map/all_gather | solution.py:79
  1050.5 13.3 fusion.36
  1063.8 13.3 fusion.354
  1083.2 13.3 fusion.78
  1096.5 173.3 %all-gather.35.cloned.1.call-done = bf16[1,6400,1600]{2,1,0:T(8,128)(2,1)} async-done(((bf16[1,400,1600]{2,1,0:T(8,128)(2,1)}), bf16[1,6400,1600]{2,1,0:T(8,128)(2,1)}) %all-gather.35.cloned.1.call-update) | async-done | bytes 20480016 | tf_op jit(solution)/shard_map/all_gather | solution.py:325
  1269.8 16.5 fusion.265
  1298.0 14.2 fusion.181
  1315.0 71.5 %all-gather.23.cloned.1.call-done = bf16[1024,3200]{0,1:T(8,128)(2,1)} async-done(((bf16[256,3200]{0,1:T(8,128)(2,1)}), bf16[1024,3200]{0,1:T(8,128)(2,1)}) %all-gather.23.cloned.1.call-update) | async-done | bytes 6553616 | tf_op jit(solution)/shard_map/all_gather | solution.py:79
  1403.2 13.8 fusion.37
  1417.0 13.4 fusion.353
  1436.1 18.9 fusion.150
  1455.0 15.3 fusion.262
  1478.6 14.2 fusion.178
  1495.6 71.8 %all-gather.25.cloned.1.call-done = bf16[1024,3200]{0,1:T(8,128)(2,1)} async-done(((bf16[256,3200]{0,1:T(8,128)(2,1)}), bf16[1024,3200]{0,1:T(8,128)(2,1)}) %all-gather.25.cloned.1.call-update) | async-done | bytes 6553616 | tf_op jit(solution)/shard_map/all_gather | solution.py:79
  1584.1 13.2 fusion.38
  1597.4 13.2 fusion.352
  1618.8 18.8 select_select_fusion.1
  1637.6 14.9 fusion.259
  1675.7 14.2 fusion.175
  1693.0 52.1 %all-to-all-done.1 = bf16[4,256,1600]{1,2,0:T(8,128)(2,1)} async-done(((bf16[4,256,1600]{1,2,0:T(8,128)(2,1)}), bf16[4,256,1600]{1,2,0:T(8,128)(2,1)}, u32[]{:S(2)}, u32[]{:S(2)}) %all-to-all-start.1) | async-done | bytes 3276832 | tf_op jit(solution)/shard_map/all_to_all | solution.py:294
  1757.8 23.1 convert_reduce_fusion.3
  1801.0 13.4 fusion.39
  1815.3 14.0 fusion.351
  1840.7 13.2 multiply_reduce_fusion.7
  1892.2 23.4 multiply_reduce_fusion.3
  1928.1 16.8 multiply_convert_fusion.3
  1964.9 60.5 %reduce-scatter.20.cloned.1.call-done = bf16[256,3200]{0,1:T(8,128)(2,1)} async-done(((bf16[1024,3200]{0,1:T(8,128)(2,1)}), bf16[256,3200]{0,1:T(8,128)(2,1)}) %reduce-scatter.20.cloned.1.call-update) | async-done | bytes 1638416 | tf_op jit(solution)/shard_map/reduce_scatter | solution.py:207
  2044.7 20.5 convert_reduce_fusion.2
  2065.3 13.8 multiply_reduce_fusion.6
  2096.0 23.8 multiply_reduce_fusion.2
  2119.7 12.6 fusion.314
  2132.3 16.6 multiply_convert_fusion.2
  2165.5 20.3 broadcast_select_fusion.5
  2194.9 35.3 reduce-scatter.22.cloned.1.call-done
  2254.6 21.7 convert_reduce_fusion.1
  2276.3 13.6 multiply_reduce_fusion.5
  2306.7 23.5 multiply_reduce_fusion.1
  2342.8 16.6 multiply_convert_fusion.1
  2379.8 60.6 %reduce-scatter.24.cloned.1.call-done = bf16[256,3200]{0,1:T(8,128)(2,1)} async-done(((bf16[1024,3200]{0,1:T(8,128)(2,1)}), bf16[256,3200]{0,1:T(8,128)(2,1)}) %reduce-scatter.24.cloned.1.call-update) | async-done | bytes 1638416 | tf_op jit(solution)/shard_map/reduce_scatter | solution.py:207
  2461.0 25.0 broadcast_select_fusion.10
  2486.0 13.7 multiply_reduce_fusion.4
  2516.7 23.8 multiply_reduce_fusion
  2540.4 12.5 fusion.320
  2553.0 16.6 multiply_convert_fusion
  2587.5 22.4 convolution_convert_fusion.1
  2610.0 39.9 copy.139
  2676.8 19.1 convolution_convert_fusion.2
  2695.9 34.0 copy.135
  2745.7 23.1 convolution_convert_fusion
  2768.8 30.4 copy.154
  2801.1 636.4 %all-reduce.34.cloned.1.call-done = (bf16[4,400,4800]{2,0,1:T(4,128)(2,1)}, bf16[4,400,1600]{2,0,1:T(4,128)(2,1)}, bf16[4,400,6400]{2,0,1:T(4,128)(2,1)}) async-done(((bf16[4,400,4800]{2,0,1:T(4,128)(2,1)}, bf16[4,400,1600]{2,0,1:T(4,128)(2,1)}, bf16[4,400,6400]{2,0,1:T(4,128)(2,1)}), (bf16[4,400,4800]{2,0,1:T(4,128)(2,1)}, bf16[4,400,1600]{2,0,1:T(4,128)(2,1)}, ...) | async-done | bytes 40960016
  3446.7 186.9 %reduce-scatter.32.cloned.1.call-done = bf16[4,400,1600]{2,1,0:T(8,128)(2,1)} async-done(((bf16[4,1600,1600]{2,1,0:T(8,128)(2,1)}), bf16[4,400,1600]{2,1,0:T(8,128)(2,1)}) %reduce-scatter.32.cloned.1.call-update) | async-done | bytes 5120016 | tf_op jit(solution)/shard_map/reduce_scatter | solution.py:439
  3645.6 17.4 fusion.308
  3688.3 13.6 all-reduce.29
  3702.5 118.4 %all-reduce.31 = (bf16[4,200]{1,0:T(4,128)(2,1)S(1)}, bf16[4,100]{1,0:T(4,128)(2,1)S(1)}, bf16[4,400]{1,0:T(4,128)(2,1)S(1)}, bf16[4,100]{1,0:T(4,128)(2,1)S(1)}...) all-reduce(bf16[4,200]{1,0:T(4,128)(2,1)S(1)} %constant_dynamic-sli, ...), channel_id=21, replica_groups=mesh['section'=2,'dp'=4,'seq'=4] {'dp'}, use_global_device_ids=true, to_apply=%region_74.75.clone | all-reduce | flops 4800 | bytes 19200
  3843.6 67.3 %reduce-scatter.34.cloned.1.call-done = bf16[1,400,1600]{2,1,0:T(8,128)(2,1)} async-done(((bf16[4,400,1600]{2,1,0:T(8,128)(2,1)}), bf16[1,400,1600]{2,1,0:T(8,128)(2,1)}) %reduce-scatter.34.cloned.1.call-update) | async-done | bytes 1280016 | tf_op jit(solution)/shard_map/reduce_scatter | solution.py:443
  3913.9 95.0 %reduce-scatter.30.cloned.1.call-done = bf16[1,100,6400]{2,1,0:T(8,128)(2,1)} async-done(((bf16[4,100,6400]{2,1,0:T(8,128)(2,1)}), bf16[1,100,6400]{2,1,0:T(8,128)(2,1)}) %reduce-scatter.30.cloned.1.call-update) | async-done | bytes 1280016 | tf_op jit(solution)/shard_map/reduce_scatter | solution.py:443
  (911 shorter events, 607.9 us)
Async XLA Ops:
  7.2 395.3 %all-gather.29.cloned.1.call-start = ((), (), s32[]{:S(2)}) async-start(), calls=%async_computation.24 | async-start | bytes 33075200 | tf_op jit(solution)/shard_map/all_gather | solution.py:319
  11.4 526.3 %all-gather.31.cloned.1.call-start = ((), (), s32[]{:S(2)}) async-start(), calls=%async_computation.25 | async-start | bytes 11315200 | tf_op jit(solution)/shard_map/all_gather | solution.py:321
  12.9 947.1 %all-gather.33.cloned.1.call-start = ((), (), s32[]{:S(2)}) async-start(), calls=%async_computation.26 | async-start | bytes 43520000 | tf_op jit(solution)/shard_map/all_gather | solution.py:323
  29.1 202.5 %all-to-all-start = ((bf16[4,256,1600]{1,2,0:T(8,128)(2,1)}), bf16[4,256,1600]{1,2,0:T(8,128)(2,1)}, u32[]{:S(2)}, u32[]{:S(2)}) async-start(bf16[4,256,1600]{1,2,0:T(8,128)(2,1)} %copy.119), calls=%async_computation | async-start | bytes 6553600 | tf_op jit(solution)/shard_map/all_to_all | solution.py:293
  34.6 998.4 %all-gather.21.cloned.1.call-start = ((), (), s32[]{:S(2)}) async-start(), calls=%async_computation.12 | async-start | bytes 8192000 | tf_op jit(solution)/shard_map/all_gather | solution.py:79
  231.3 1444.0 %copy-start.134 = (f32[1600]{0:T(1024)}, f32[1600]{0:T(1024)S(1)}, u32[]{:S(2)}) copy-start(f32[1600]{0:T(1024)S(1)} %convert_element_type.632) | copy-start | bytes 19204
  231.3 1066.7 %copy-start.168 = (f32[1600]{0:T(1024)}, f32[1600]{0:T(1024)S(1)}, u32[]{:S(2)}) copy-start(f32[1600]{0:T(1024)S(1)} %convert_element_type.633) | copy-start | bytes 19204
  231.5 1066.5 %copy-start.194 = (f32[4800]{0:T(1024)}, f32[4800]{0:T(1024)S(1)}, u32[]{:S(2)}) copy-start(f32[4800]{0:T(1024)S(1)} %concatenate.94) | copy-start | bytes 57604
  247.7 175.4 %copy-start.10 = (f32[1,256,1600]{1,0,2:T(1,128)}, f32[1,256,1600]{1,0,2:T(1,128)S(1)}, u32[]{:S(2)}) copy-start(f32[1,256,1600]{1,0,2:T(1,128)S(1)} %get-tuple-element.209) | copy-start | bytes 4915204
  247.7 175.3 %copy-start.207 = (f32[256]{0:T(256)}, f32[256]{0:T(256)S(1)}, u32[]{:S(2)}) copy-start(f32[256]{0:T(256)S(1)} %broadcast_multiply_fusion.15) | copy-start | bytes 3076
  247.9 175.1 %copy-start.245 = (f32[256]{0:T(256)}, f32[256]{0:T(256)S(1)}, u32[]{:S(2)}) copy-start(f32[256]{0:T(256)S(1)} %add_rsqrt_fusion.7) | copy-start | bytes 3076
  440.0 829.7 %all-gather.35.cloned.1.call-start = ((), (), s32[]{:S(2)}) async-start(), calls=%async_computation.27 | async-start | bytes 22630400 | tf_op jit(solution)/shard_map/all_gather | solution.py:325
  440.6 945.9 %all-gather.23.cloned.1.call-start = ((), (), s32[]{:S(2)}) async-start(), calls=%async_computation.13 | async-start | bytes 8192000 | tf_op jit(solution)/shard_map/all_gather | solution.py:79
  440.9 104.0 %copy-start.227 = (s32[3]{0:T(128)}, s32[3]{0:T(128)S(1)}, u32[]{:S(2)}) copy-start(s32[3]{0:T(128)S(1)} %select_reduce_fusion.1) | copy-start | bytes 40
  446.7 630.5 %copy-start.224 = (f32[1600]{0:T(1024)}, f32[1600]{0:T(1024)S(1)}, u32[]{:S(2)}) copy-start(f32[1600]{0:T(1024)S(1)} %convert_element_type.635) | copy-start | bytes 19204
  446.7 1169.5 %copy-start.112 = (f32[1600]{0:T(1024)}, f32[1600]{0:T(1024)S(1)}, u32[]{:S(2)}) copy-start(f32[1600]{0:T(1024)S(1)} %convert_element_type.636) | copy-start | bytes 19204
  446.7 636.4 %copy-start.139 = (f32[1600]{0:T(1024)}, f32[1600]{0:T(1024)S(1)}, u32[]{:S(2)}) copy-start(f32[1600]{0:T(1024)S(1)} %convert_element_type.637) | copy-start | bytes 19204
  446.7 636.4 %copy-start.159 = (f32[6400]{0:T(1024)}, f32[6400]{0:T(1024)S(1)}, u32[]{:S(2)}) copy-start(f32[6400]{0:T(1024)S(1)} %convert_element_type.638) | copy-start | bytes 76804
  446.7 823.0 %copy-start.221 = (f32[1600]{0:T(1024)}, f32[1600]{0:T(1024)S(1)}, u32[]{:S(2)}) copy-start(f32[1600]{0:T(1024)S(1)} %convert_element_type.639) | copy-start | bytes 19204
  448.2 96.7 %copy-start.243 = (s32[256]{0:T(256)}, s32[256]{0:T(256)S(1)}, u32[]{:S(2)}) copy-start(s32[256]{0:T(256)S(1)} %iota_add_fusion) | copy-start | bytes 3076
  449.9 613.9 %copy-start.109 = (pred[256,1024]{1,0:T(8,128)(4,1)}, pred[256,1024]{1,0:T(8,128)(4,1)S(1)}, u32[]{:S(2)}) copy-start(pred[256,1024]{1,0:T(8,128)(4,1)S(1)} %get-tuple-element.295) | copy-start | bytes 786436
  985.7 52.6 %slice-start.12 = ((bf16[256,4800]{0,1:T(8,128)(2,1)}), bf16[256,1600]{0,1:T(8,128)(2,1)S(1)}, s32[]{:S(2)}) async-start(bf16[256,4800]{0,1:T(8,128)(2,1)} %fusion.184), calls=%async_computation.42 | async-start | bytes 1638400 | tf_op jit(solution)/shard_map/slice | solution.py:39
  1082.9 186.9 %copy-start.7 = (f32[256,1600]{0,1:T(8,128)}, f32[256,1600]{0,1:T(8,128)S(1)}, u32[]{:S(2)}) copy-start(f32[256,1600]{0,1:T(8,128)S(1)} %get-tuple-element.306) | copy-start | bytes 4915204
  1286.4 8.9 collective-permute-start
  1297.4 133.0 %copy-start.18 = (bf16[256,1600]{0,1:T(8,128)(2,1)}, bf16[256,1600]{0,1:T(8,128)(2,1)S(1)}, u32[]{:S(2)}) copy-start(bf16[256,1600]{0,1:T(8,128)(2,1)S(1)} %get-tuple-element.201) | copy-start | bytes 2457604
  1314.9 252.5 %all-gather.25.cloned.1.call-start = ((), (), s32[]{:S(2)}) async-start(), calls=%async_computation.14 | async-start | bytes 8192000 | tf_op jit(solution)/shard_map/all_gather | solution.py:79
  1315.0 76.8 %slice-start.13 = ((bf16[256,4800]{0,1:T(8,128)(2,1)}), bf16[256,1600]{0,1:T(8,128)(2,1)S(1)}, s32[]{:S(2)}) async-start(bf16[256,4800]{0,1:T(8,128)(2,1)} %fusion.181), calls=%async_computation.43 | async-start | bytes 1638400 | tf_op jit(solution)/shard_map/slice | solution.py:39
  1435.8 180.4 %copy-start.191 = (f32[256]{0:T(256)}, f32[256]{0:T(256)S(1)}, u32[]{:S(2)}) copy-start(f32[256]{0:T(256)S(1)} %broadcast_multiply_fusion.12) | copy-start | bytes 3076
  1436.1 180.2 %copy-start.196 = (f32[256]{0:T(256)}, f32[256]{0:T(256)S(1)}, u32[]{:S(2)}) copy-start(f32[256]{0:T(256)S(1)} %add_rsqrt_fusion.4) | copy-start | bytes 3076
  1470.3 4.2 collective-permute-start.1
  1478.1 132.5 %copy-start.22 = (bf16[256,1600]{0,1:T(8,128)(2,1)}, bf16[256,1600]{0,1:T(8,128)(2,1)S(1)}, u32[]{:S(2)}) copy-start(bf16[256,1600]{0,1:T(8,128)(2,1)S(1)} %get-tuple-element.194) | copy-start | bytes 2457604
  1495.6 77.2 %slice-start.14 = ((bf16[256,4800]{0,1:T(8,128)(2,1)}), bf16[256,1600]{0,1:T(8,128)(2,1)S(1)}, s32[]{:S(2)}) async-start(bf16[256,4800]{0,1:T(8,128)(2,1)} %fusion.178), calls=%async_computation.44 | async-start | bytes 1638400 | tf_op jit(solution)/shard_map/slice | solution.py:39
  1495.6 77.2 %copy-start.111 = (pred[256,1024]{1,0:T(8,128)(4,1)S(1)}, pred[256,1024]{1,0:T(8,128)(4,1)}, u32[]{:S(2)}) copy-start(pred[256,1024]{1,0:T(8,128)(4,1)} %get-tuple-element.293) | copy-start | bytes 786436
  1652.5 19.6 collective-permute-start.2
  1667.4 77.7 %all-to-all-start.1 = ((bf16[4,256,1600]{1,2,0:T(8,128)(2,1)}), bf16[4,256,1600]{1,2,0:T(8,128)(2,1)}, u32[]{:S(2)}, u32[]{:S(2)}) async-start(bf16[4,256,1600]{1,2,0:T(8,128)(2,1)} %copy.128), calls=%async_computation.1 | async-start | bytes 6553600 | tf_op jit(solution)/shard_map/all_to_all | solution.py:294
  1672.1 112.3 %all-gather.27.cloned.1.call-start = ((), (), s32[]{:S(2)}) async-start(), calls=%async_computation.15 | async-start | bytes 8192000 | tf_op jit(solution)/shard_map/all_gather | solution.py:79
  1674.2 155.0 %copy-start.25 = (bf16[256,1600]{0,1:T(8,128)(2,1)}, bf16[256,1600]{0,1:T(8,128)(2,1)S(1)}, u32[]{:S(2)}) copy-start(bf16[256,1600]{0,1:T(8,128)(2,1)S(1)} %get-tuple-element.207) | copy-start | bytes 2457604
  1689.9 55.2 %copy-start.258 = (s32[3]{0:T(128)S(1)}, s32[3]{0:T(128)}, u32[]{:S(2)}) copy-start(s32[3]{0:T(128)} %copy-done.257) | copy-start | bytes 40
  1692.7 332.7 %reduce-scatter.20.cloned.1.call-start = ((), (), s32[]{:S(2)}) async-start(), calls=%async_computation.16 | async-start | bytes 8192000 | tf_op jit(solution)/shard_map/reduce_scatter | solution.py:207
  1953.9 276.3 %reduce-scatter.22.cloned.1.call-start = ((), (), s32[]{:S(2)}) async-start(), calls=%async_computation.17 | async-start | bytes 8192000 | tf_op jit(solution)/shard_map/reduce_scatter | solution.py:207
  1954.6 70.8 %copy-start.31 = (f32[256,1600]{0,1:T(8,128)S(1)}, f32[256,1600]{0,1:T(8,128)}, u32[]{:S(2)}) copy-start(f32[256,1600]{0,1:T(8,128)} %get-tuple-element.200) | copy-start | bytes 4915204
  1954.6 70.8 %copy-start.135 = (f32[1600]{0:T(1024)S(1)}, f32[1600]{0:T(1024)}, u32[]{:S(2)}) copy-start(f32[1600]{0:T(1024)} %copy-done.134) | copy-start | bytes 19204
  1964.9 71.1 %copy-start.68 = (bf16[25,64,256]{2,1,0:T(8,128)(2,1)}, bf16[25,64,256]{2,1,0:T(8,128)(2,1)S(1)}, u32[]{:S(2)}) copy-start(bf16[25,64,256]{2,1,0:T(8,128)(2,1)S(1)} %multiply_convert_fusion.11) | copy-start | bytes 2457604
  2038.9 4.5 collective-permute-start.3
  2158.1 282.3 %reduce-scatter.24.cloned.1.call-start = ((), (), s32[]{:S(2)}) async-start(), calls=%async_computation.18 | async-start | bytes 8192000 | tf_op jit(solution)/shard_map/reduce_scatter | solution.py:207
  2185.7 44.5 %copy-start.30 = (f32[256,1600]{0,1:T(8,128)S(1)}, f32[256,1600]{0,1:T(8,128)}, u32[]{:S(2)}) copy-start(f32[256,1600]{0,1:T(8,128)} %get-tuple-element.193) | copy-start | bytes 4915204
  2185.8 44.4 %copy-start.136 = (f32[1600]{0:T(1024)S(1)}, f32[1600]{0:T(1024)}, u32[]{:S(2)}) copy-start(f32[1600]{0:T(1024)} %copy-done.134) | copy-start | bytes 19204
  2244.8 8.6 collective-permute-start.4
  2368.4 302.6 %reduce-scatter.26.cloned.1.call-start = ((), (), s32[]{:S(2)}) async-start(), calls=%async_computation.19 | async-start | bytes 8192000 | tf_op jit(solution)/shard_map/reduce_scatter | solution.py:207
  2369.0 71.4 %copy-start.20 = (bf16[256,1600]{0,1:T(8,128)(2,1)S(1)}, bf16[256,1600]{0,1:T(8,128)(2,1)}, u32[]{:S(2)}) copy-start(bf16[256,1600]{0,1:T(8,128)(2,1)} %copy-done.18) | copy-start | bytes 2457604
  2369.0 71.4 %copy-start.26 = (bf16[256,1600]{0,1:T(8,128)(2,1)S(1)}, bf16[256,1600]{0,1:T(8,128)(2,1)}, u32[]{:S(2)}) copy-start(bf16[256,1600]{0,1:T(8,128)(2,1)} %copy-done.25) | copy-start | bytes 2457604
  2369.0 71.4 %copy-start.137 = (f32[1600]{0:T(1024)S(1)}, f32[1600]{0:T(1024)}, u32[]{:S(2)}) copy-start(f32[1600]{0:T(1024)} %copy-done.134) | copy-start | bytes 19204
  2456.5 4.5 collective-permute-start.5
  2578.8 858.8 %all-reduce.34.cloned.1.call-start = ((), (), s32[]{:S(2)}) async-start(), calls=%async_computation.29 | async-start | bytes 82739200
  2609.9 39.9 copy-start.95
  2609.9 39.9 copy-start.99
  2730.0 903.6 %reduce-scatter.32.cloned.1.call-start = ((), (), s32[]{:S(2)}) async-start(), calls=%async_computation.22 | async-start | bytes 26624000 | tf_op jit(solution)/shard_map/reduce_scatter | solution.py:439
  2799.2 1037.9 %reduce-scatter.36.cloned.1.call-start = ((), (), s32[]{:S(2)}) async-start(), calls=%async_computation.28 | async-start | bytes 1730560
  3440.6 398.9 %reduce-scatter.28.cloned.1.call-start = ((), (), s32[]{:S(2)}) async-start(), calls=%async_computation.20 | async-start | bytes 5058560 | tf_op jit(solution)/shard_map/reduce_scatter | solution.py:443
  3446.6 464.3 %reduce-scatter.34.cloned.1.call-start = ((), (), s32[]{:S(2)}) async-start(), calls=%async_computation.23 | async-start | bytes 6656000 | tf_op jit(solution)/shard_map/reduce_scatter | solution.py:443
  3633.6 375.2 %reduce-scatter.30.cloned.1.call-start = ((), (), s32[]{:S(2)}) async-start(), calls=%async_computation.21 | async-start | bytes 6656000 | tf_op jit(solution)/shard_map/reduce_scatter | solution.py:443
  3673.6 157.1 %all-to-all-start.2 = ((bf16[4,256,1600]{1,2,0:T(8,128)(2,1)}), bf16[4,256,1600]{1,2,0:T(8,128)(2,1)}, u32[]{:S(2)}, u32[]{:S(2)}) async-start(bf16[4,256,1600]{1,2,0:T(8,128)(2,1)} %copy.133), calls=%async_computation.6 | async-start | bytes 6553600 | tf_op jit(solution)/shard_map/all_to_all | solution.py:427
  3683.9 146.8 %copy-start.265 = (s32[3]{0:T(128)S(1)}, s32[3]{0:T(128)}, u32[]{:S(2)}) copy-start(s32[3]{0:T(128)} %copy-done.263) | copy-start | bytes 40
  3839.5 174.2 %copy-start.1 = (bf16[3,256,1600]{1,2,0:T(8,128)(2,1)S(1)}, bf16[3,256,1600]{1,2,0:T(8,128)(2,1)}, u32[]{:S(2)}) copy-start(bf16[3,256,1600]{1,2,0:T(8,128)(2,1)} %param.16) | copy-start | bytes 7372804
  (257 other events, 2001.2 us)
Sparse Core Ops, SparseCore 0:
  11.6 390.8 all-gather.28
  405.7 131.9 all-gather.30
  541.0 418.9 all-gather.32
  962.2 70.7 all-gather.20
  1035.6 234.1 all-gather.34
  1315.1 71.3 all-gather.22
  1495.7 71.6 all-gather.24
  1692.8 73.6 all-gather.26
  1954.0 71.3 reduce-scatter.19
  2158.1 72.0 reduce-scatter.21
  2368.5 71.8 reduce-scatter.23
  2578.8 71.8 reduce-scatter.25
  2730.1 707.3 all-reduce.33
  3440.5 193.0 reduce-scatter.31
  3636.4 31.7 reduce-scatter.35
  3670.4 126.6 reduce-scatter.27
  3799.3 111.5 reduce-scatter.33
  3913.1 95.7 reduce-scatter.29
where the time goes:
time: 4030 us; the launch traced here: 4020 us
  waiting for transfers between devices  2220 us (55%)
  matrix products  876 us (22%)
  blocking collectives  324 us (8%)
  local copies, waits for them, and re-layouts  295 us (7%)
  other arithmetic  247 us (6%)
    unnamed x20, waiting for transfers between devices  637 us
    all_gather x1, waiting for transfers between devices, per_device(): lax.all_gather(shards[4], ('dp', 'seq'), axis=0, tiled=True)  415 us
    unnamed x3, blocking collectives  324 us
    all_gather x4, waiting for transfers between devices, layer_forward(): lax.all_gather(attention_projected[:, model_width:], 'seq', axis=0, tiled...  191 us
    reduce_scatter x1, waiting for transfers between devices, per_device(): lax.psum_scatter(shortened(folded), 'seq', scatter_dimension=1, tiled=True)  187 us
    all_gather x1, waiting for transfers between devices, per_device(): lax.all_gather(shards[6], ('dp', 'seq'), axis=0, tiled=True)  173 us
    reduce_scatter x3, waiting for transfers between devices, per_device(): lax.psum_scatter(shortened(inside), 'dp', scatter_dimension=0, tiled=True)  162 us
    reduce_scatter x4, waiting for transfers between devices, layer_backward(): lax.psum_scatter(grad_context.astype(jnp.bfloat16), 'seq', scatter_dimens...  156 us
  transfers between devices with their start and end apart: 27, of which 18 were waited for; matrix products, arithmetic and copies ran while one was open for 14% of the time, Pallas kernels for 0%

commit v1 on v0

v1 whole, which is shorter than its diff:
```python
import functools

import jax
import jax.numpy as jnp
from jax import lax
from jax.experimental import pallas as pl
from jax.experimental.pallas import tpu as pltpu
from jax.sharding import PartitionSpec as P

H = 25
HD = 64
QUARTERS = 4
HL = -(-H // QUARTERS)
HSTEP = (H - HL) // (QUARTERS - 1)
PAIRS = -(-HL // 2)
QK_LANES = HL * 2 * HD
V_LANES = PAIRS * 2 * HD
P_LANES = QK_LANES + V_LANES
ROW_BLOCK = 256
F32 = jnp.float32
BF16 = jnp.bfloat16


def round_up(value, by):
    return -(-value // by) * by


def masked_probs(q, k, first, length):
    scores = lax.dot_general(q, k, (((1,), (1,)), ((), ())), preferred_element_type=F32)
    rows = first + lax.broadcasted_iota(jnp.int32, scores.shape, 0)
    cols = lax.broadcasted_iota(jnp.int32, scores.shape, 1)
    scores = jnp.where((cols <= rows) & (cols < length), scores, -1e30)
    top = jnp.max(scores, axis=1, keepdims=True)
    weights = jnp.exp(scores - top)
    return weights * (1.0 / jnp.sum(weights, axis=1, keepdims=True))


def attn_fwd_kernel(len_ref, qk_ref, v_ref, o_ref):
    total = qk_ref.shape[0]
    block = min(ROW_BLOCK, total)
    length = len_ref[0]
    lower = lax.broadcasted_iota(jnp.int32, (block, 2 * HD), 1) < HD

    def rows_of(i, both):
        first, end = i * block, (i + 1) * block
        parts = []
        for a in range(2 if both else 1):
            q = qk_ref[first:end, 2 * HD * a : 2 * HD * a + HD] * jnp.asarray(HD**-0.5, BF16)
            k = qk_ref[:end, 2 * HD * a + HD : 2 * HD * (a + 1)]
            probs = masked_probs(q, k, first, length).astype(BF16)
            parts.append(jnp.dot(probs, v_ref[:end, :], preferred_element_type=F32))
        upper = parts[1] if both else jnp.zeros_like(parts[0])
        o_ref[first:end, :] = jnp.where(lower, parts[0], upper).astype(BF16)

    if HL % 2 == 0:
        for i in range(total // block):
            rows_of(i, True)
        return
    last = pl.program_id(0) == PAIRS - 1

    @pl.when(jnp.logical_not(last))
    def _():
        for i in range(total // block):
            rows_of(i, True)

    @pl.when(last)
    def _():
        for i in range(total // block):
            rows_of(i, False)


def attn_forward(packed, length):
    total = packed.shape[0]
    return pl.pallas_call(
        attn_fwd_kernel,
        grid=(PAIRS,),
        in_specs=[
            pl.BlockSpec(memory_space=pltpu.SMEM),
            pl.BlockSpec((total, 4 * HD), lambda j: (0, j)),
            pl.BlockSpec((total, 2 * HD), lambda j: (0, j + QK_LANES // (2 * HD))),
        ],
        out_specs=pl.BlockSpec((total, 2 * HD), lambda j: (0, j)),
        out_shape=jax.ShapeDtypeStruct((total, V_LANES), BF16),
        compiler_params=pltpu.CompilerParams(vmem_limit_bytes=40 * 2**20),
        cost_estimate=pl.CostEstimate(
            flops=2 * 2 * HL * total * total * 256, bytes_accessed=4 * total * P_LANES, transcendentals=HL * total * total
        ),
        name="attn_fwd",
    )(length, packed, packed)


def attn_bwd_kernel(len_ref, qk_ref, v_ref, g_ref, out_ref, dk_ref, dv_ref):
    total = qk_ref.shape[0]
    block = min(ROW_BLOCK, total)
    length = len_ref[0]
    pair = pl.program_id(0)
    scale = jnp.asarray(HD**-0.5, BF16)
    lane = lax.broadcasted_iota(jnp.int32, (block, 2 * HD), 1)
    lane_all = lax.broadcasted_iota(jnp.int32, (total, 2 * HD), 1)

    def head(a):
        dk_ref[...] = jnp.zeros_like(dk_ref)
        mine = (lane < HD) if a == 0 else (lane >= HD)
        dq_parts = []
        for i in range(total // block):
            first, end = i * block, (i + 1) * block
            q = qk_ref[first:end, 2 * HD * a : 2 * HD * a + HD] * scale
            k = qk_ref[:end, 2 * HD * a + HD : 2 * HD * (a + 1)]
            g = g_ref[first:end, :]
            g_mine = jnp.where(mine, g, jnp.zeros_like(g))
            probs = masked_probs(q, k, first, length)
            gprobs = lax.dot_general(g_mine, v_ref[:end, :], (((1,), (1,)), ((), ())), preferred_element_type=F32)
            inner = jnp.sum(probs * gprobs, axis=1, keepdims=True)
            gscores = (probs * (gprobs - inner)).astype(BF16)
            dq_parts.append((jnp.dot(gscores, k, preferred_element_type=F32) * HD**-0.5).astype(BF16))
            dk_ref[:end, :] += lax.dot_general(gscores, q, (((0,), (0,)), ((), ())), preferred_element_type=F32)
            dv_ref[:end, :] += lax.dot_general(
                probs.astype(BF16), g_mine, (((0,), (0,)), ((), ())), preferred_element_type=F32
            )
        return jnp.concatenate([jnp.concatenate(dq_parts, axis=0), dk_ref[...].astype(BF16)], axis=1)

    dv_ref[...] = jnp.zeros_like(dv_ref)
    out_ref[:, pl.ds(pl.multiple_of(pair * 4 * HD, 2 * HD), 2 * HD)] = head(0)

    @pl.when(2 * pair + 1 < HL)
    def _():
        out_ref[:, pl.ds(pl.multiple_of(pair * 4 * HD + 2 * HD, 2 * HD), 2 * HD)] = head(1)

    out_ref[:, pl.ds(pl.multiple_of(QK_LANES + pair * 2 * HD, 2 * HD), 2 * HD)] = dv_ref[...].astype(BF16)


def attn_backward(packed, grad, length):
    total = packed.shape[0]
    return pl.pallas_call(
        attn_bwd_kernel,
        grid=(PAIRS,),
        in_specs=[
            pl.BlockSpec(memory_space=pltpu.SMEM),
            pl.BlockSpec((total, 4 * HD), lambda j: (0, j)),
            pl.BlockSpec((total, 2 * HD), lambda j: (0, j + QK_LANES // (2 * HD))),
            pl.BlockSpec((total, 2 * HD), lambda j: (0, j)),
        ],
        out_specs=pl.BlockSpec((total, P_LANES), lambda j: (0, 0)),
        out_shape=jax.ShapeDtypeStruct((total, P_LANES), BF16),
        scratch_shapes=[pltpu.VMEM((total, HD), F32), pltpu.VMEM((total, 2 * HD), F32)],
        compiler_params=pltpu.CompilerParams(vmem_limit_bytes=48 * 2**20),
        cost_estimate=pl.CostEstimate(
            flops=5 * 2 * HL * total * total * 256, bytes_accessed=6 * total * P_LANES, transcendentals=HL * total * total
        ),
        name="attn_bwd",
    )(length, packed, packed, grad)


def flip(value, axis, bit):
    count = lax.axis_size(axis)
    return lax.ppermute(value, axis, [(i, i ^ (1 << bit)) for i in range(count)])


def bit_of(axis, bit):
    return (lax.axis_index(axis) >> bit) & 1


def bits_in(axis):
    return (lax.axis_size(axis) - 1).bit_length()


def group_bits():
    z = [("dp", b) for b in reversed(range(bits_in("dp")))]
    y = [("seq", b) for b in reversed(range(1, bits_in("seq")))]
    return z, y


X_BIT = ("seq", 0)


def swap_cores(value):
    return lax.ppermute(value, "section", [(0, 1), (1, 0)])


def in_core_order(mine, other, axis):
    core = lax.axis_index("section")
    low = jnp.where(core == 0, mine, other)
    high = jnp.where(core == 0, other, mine)
    return jnp.concatenate([low, high], axis=axis)


def gather_step(value, bit, axis):
    other = flip(value, *bit)
    mine_low = bit_of(*bit) == 0
    low = jnp.where(mine_low, value, other)
    high = jnp.where(mine_low, other, value)
    return jnp.concatenate([low, high], axis=axis)


def gather_blocks(value, order, places):
    value = value.reshape((1,) * len(places) + value.shape)
    before_last = value
    for bit in order:
        before_last = value
        value = gather_step(value, bit, places.index(bit))
    return value.reshape((-1,) + value.shape[len(places) :]), before_last


def scatter_step(value, bit, axis):
    mine_low = bit_of(*bit) == 0
    low = lax.slice_in_dim(value, 0, 1, axis=axis)
    high = lax.slice_in_dim(value, 1, 2, axis=axis)
    keep = jnp.where(mine_low, low, high)
    send = jnp.where(mine_low, high, low)
    return (keep.astype(F32) + flip(send, *bit).astype(F32)).astype(BF16)


def scatter_blocks(value, order, places):
    value = value.reshape((2,) * len(places) + value.shape[1:])
    for bit in order:
        value = scatter_step(value, bit, places.index(bit))
    return value.reshape(value.shape[len(places) :])


def after(value, token):
    return lax.optimization_barrier((value, token))[0]


def rows_of_both(own):
    return in_core_order(own, swap_cores(own), 0)


def summed_rows(partial):
    half = partial.shape[0] // 2
    core = lax.axis_index("section")
    low, high = partial[:half], partial[half:]
    own = jnp.where(core == 0, low, high)
    other = jnp.where(core == 0, high, low)
    chip = (own.astype(F32) + swap_cores(other).astype(F32)).astype(BF16)
    return chip.astype(F32) + flip(chip, *X_BIT).astype(F32)


def dot(a, b):
    return jnp.dot(a, b, preferred_element_type=F32)


def dot_t(a, b):
    return lax.dot_general(a, b, (((1,), (1,)), ((), ())), preferred_element_type=F32)


def dot_0(a, b):
    return lax.dot_general(a, b, (((0,), (0,)), ((), ())), preferred_element_type=F32)


def gelu_parts(u):
    t = jnp.tanh(0.7978845608 * (u + 0.044715 * u * u * u))
    return t


def gelu(u):
    return 0.5 * u * (1.0 + gelu_parts(u))


def gelu_slope(u):
    t = gelu_parts(u)
    return 0.5 * (1.0 + t) + 0.5 * u * (1.0 - t * t) * 0.7978845608 * (1.0 + 3 * 0.044715 * u * u)


def norm_stats(rows, mask, width):
    average = jnp.sum(rows, axis=-1, keepdims=True) / width
    centered = (rows - average) * mask
    variance = jnp.sum(centered * centered, axis=-1, keepdims=True) / width
    scale = lax.rsqrt(variance + 1e-05)
    return centered * scale, scale


def norm_back(grad, rows, gain, mask, width):
    hat, scale = norm_stats(rows, mask, width)
    inner = grad * gain
    mean_one = jnp.sum(inner, axis=-1, keepdims=True) / width
    mean_two = jnp.sum(inner * hat, axis=-1, keepdims=True) / width
    back = scale * (inner - mean_one - hat * mean_two) * mask
    return back, jnp.sum(grad * hat, axis=0), jnp.sum(grad * mask, axis=0)


def layer_forward(rows, w, length, mask, width):
    hat, _ = norm_stats(rows, mask, width)
    normed = rows_of_both((hat * w["gain_one"] + w["shift_one"]).astype(BF16))
    packed = (dot(normed, w["qkv"]) + w["qkv_bias"]).astype(BF16)
    attended = attn_forward(packed, length)
    branch = summed_rows(dot(attended, w["out"]).astype(BF16))
    middle = rows + branch + w["out_bias"]
    hat_two, _ = norm_stats(middle, mask, width)
    normed_two = rows_of_both((hat_two * w["gain_two"] + w["shift_two"]).astype(BF16))
    upward = dot(normed_two, w["up"]) + w["up_bias"]
    hidden = gelu(upward).astype(BF16)
    branch_two = summed_rows(dot(hidden, w["down"]).astype(BF16))
    result = middle + branch_two + w["down_bias"]
    stored = (rows, normed, packed, attended, middle, normed_two, upward.astype(BF16), hidden)
    return result, stored


def ffn_backward(grad_out, stored, w, mask, width):
    rows, normed, packed, attended, middle, normed_two, upward, hidden = stored
    grad_down = grad_out.astype(BF16)
    b_down = jnp.sum(grad_down.astype(F32), axis=0)
    grad_down = rows_of_both(grad_down)
    grad_up = (dot_t(grad_down, w["down"]) * gelu_slope(upward.astype(F32))).astype(BF16)
    b_up = jnp.sum(grad_up.astype(F32), axis=0)
    grad_normed = summed_rows(dot_t(grad_up, w["up"]).astype(BF16))
    back, gain, shift = norm_back(grad_normed, middle, w["gain_two"], mask, width)
    grad_middle = grad_out + back
    small = {"down_bias": b_down, "up_bias": b_up, "gain_two": gain, "shift_two": shift}
    return grad_middle, small, {"down": (hidden, grad_down), "up": (normed_two, grad_up)}


def attn_layer_backward(grad_middle, stored, w, length, mask, width):
    rows, normed, packed, attended, middle, normed_two, upward, hidden = stored
    grad_branch = grad_middle.astype(BF16)
    b_out = jnp.sum(grad_branch.astype(F32), axis=0)
    grad_branch = rows_of_both(grad_branch)
    grad_attended = dot_t(grad_branch, w["out"]).astype(BF16)
    grad_packed = attn_backward(packed, grad_attended, length)
    b_packed = jnp.sum(grad_packed.astype(F32), axis=0)
    grad_normed = summed_rows(dot_t(grad_packed, w["qkv"]).astype(BF16))
    back, gain, shift = norm_back(grad_normed, rows.astype(F32), w["gain_one"], mask, width)
    small = {"out_bias": b_out, "packed": b_packed, "gain_one": gain, "shift_one": shift}
    return grad_middle + back, small, {"out": (attended, grad_branch), "qkv": (normed, grad_packed)}


SMALL = ("b_qv", "out_bias", "up_bias", "down_bias", "gain_one", "shift_one", "gain_two", "shift_two")


def per_device(
    inputs,
    cotangent,
    lengths,
    dealing,
    query_key_value_weight,
    b_qv,
    attention_out_weight,
    attention_out_bias,
    up_weight,
    up_bias,
    down_weight,
    down_bias,
    gain_one,
    shift_one,
    gain_two,
    shift_two,
):
    micro, block_rows, width = inputs.shape
    dp_count, seq_count = lax.axis_size("dp"), lax.axis_size("seq")
    chips = dp_count * seq_count
    dp_index, seq_index, core = lax.axis_index("dp"), lax.axis_index("seq"), lax.axis_index("section")
    x_index, y_index = seq_index & 1, seq_index >> 1
    groups = seq_count // 2
    rounds = -(-micro // groups)
    half_blocks = seq_count // 2
    half_rows = half_blocks * block_rows
    part = query_key_value_weight.shape[1]
    part_pad = round_up(part + 1, 8)
    width_pad = chips * part_pad
    hid = down_weight.shape[1] // 2
    hid_pad = round_up(hid, 8)
    all_groups = dp_count * groups
    z_bits, y_bits = group_bits()
    places = z_bits + y_bits
    places_all = places + [X_BIT]
    quarter = 2 * x_index + core

    lane = lax.broadcasted_iota(jnp.int32, (1, width_pad), 1)
    mask = (lane % part_pad < part).astype(F32)
    plain = lax.broadcasted_iota(jnp.int32, (width, width_pad), 0)
    padded = lax.broadcasted_iota(jnp.int32, (width, width_pad), 1)
    spread = (padded == plain // part * part_pad + plain % part).astype(BF16)

    def widen(value):
        return lax.dot_general(
            value, spread, (((value.ndim - 1,), (0,)), ((), ())), preferred_element_type=F32
        ).astype(BF16)

    def narrow(value):
        return lax.dot_general(
            value.astype(BF16), spread, (((value.ndim - 1,), (1,)), ((), ())), preferred_element_type=F32
        )

    def pad_rows(value, rows):
        return jnp.pad(value, ((0, rows - value.shape[0]), (0, 0)))

    small_in = dict(
        zip(SMALL, (b_qv, attention_out_bias, up_bias, down_bias, gain_one, shift_one, gain_two, shift_two))
    )
    small_sizes = {name: value.shape[1] for name, value in small_in.items()}
    small_row = jnp.concatenate([small_in[name][0] for name in SMALL])
    small_total = small_row.shape[0]

    shard = query_key_value_weight[0].reshape(part, 3, H, HD)

    def qkv_piece(q):
        from_head = HSTEP * q
        heads = shard[:, :, from_head : from_head + HL]
        qk = jnp.concatenate([heads[:, 0], heads[:, 1]], axis=-1).reshape(part, QK_LANES)
        v = heads[:, 2].reshape(part, HL * HD)
        body = jnp.concatenate([qk, v, jnp.zeros((part, V_LANES - HL * HD), BF16)], axis=1)
        row = jnp.pad(small_row, (0, P_LANES - small_total))[None]
        return pad_rows(jnp.concatenate([body, row], axis=0), part_pad)

    up_shard = up_weight[0].reshape(part, all_groups, 2, 2, hid)

    def up_piece(q):
        body = up_shard[:, :, q // 2, q % 2]
        body = jnp.pad(body, ((0, 0), (0, 0), (0, hid_pad - hid))).reshape(part, all_groups * hid_pad)
        return pad_rows(body, part_pad)

    qkv_pieces = jnp.stack([jnp.stack([qkv_piece(2 * x + c) for x in range(2)]) for c in range(2)])
    up_pieces = jnp.stack([jnp.stack([up_piece(2 * x + c) for x in range(2)]) for c in range(2)])
    out_wide = pad_rows(widen(attention_out_weight[0]), part_pad)
    out_pieces = jnp.stack([out_wide[:, : width_pad // 2], out_wide[:, width_pad // 2 :]])
    down_wide = widen(down_weight[0]).reshape(2, hid, width_pad)
    down_pieces = jnp.pad(down_wide, ((0, 0), (0, hid_pad - hid), (0, 0)))

    def by_layer(pieces):
        mine = jnp.where(core == 0, pieces[0], pieces[1])
        other = swap_cores(jnp.where(core == 0, pieces[1], pieces[0]))
        return [jnp.where(core == 0, mine, other), jnp.where(core == 0, other, mine)]

    def across_x(pieces):
        mine = jnp.where(x_index == 0, pieces[0], pieces[1])
        other = flip(jnp.where(x_index == 0, pieces[1], pieces[0]), *X_BIT)
        return jnp.stack([jnp.where(x_index == 0, mine, other), jnp.where(x_index == 0, other, mine)])

    qkv_l, up_l, out_l, down_l = by_layer(qkv_pieces), by_layer(up_pieces), by_layer(out_pieces), by_layer(down_pieces)

    order_zy = z_bits + y_bits
    order_yz = y_bits + z_bits
    layers = []
    token = None
    for l in range(2):
        start = (qkv_l[l], out_l[l], up_l[l], down_l[l])
        if token is not None:
            start = after(start, token)
        qkv_x = across_x(start[0])
        qkv_all, _ = gather_blocks(qkv_x, order_zy, places)
        out_all, _ = gather_blocks(start[1], [X_BIT] + order_zy, places_all)
        up_all, up_mid = gather_blocks(across_x(start[2]), order_zy, places)
        down_all, _ = gather_blocks(start[3], order_zy if l == 0 else order_yz, places)
        token = up_mid
        small_all = qkv_all.reshape(chips, part_pad, P_LANES)[:, part, :small_total]
        pieces, at = {}, 0
        for name in SMALL:
            pieces[name] = small_all[:, at : at + small_sizes[name]]
            at += small_sizes[name]

        def feature(name):
            return jnp.pad(pieces[name].astype(F32), ((0, 0), (0, part_pad - part))).reshape(1, width_pad)

        qv = pieces["b_qv"].astype(F32).reshape(2, H * HD)
        q_bias = lax.dynamic_slice_in_dim(qv[0], quarter * HSTEP * HD, HL * HD).reshape(HL, HD)
        v_bias = lax.dynamic_slice_in_dim(qv[1], quarter * HSTEP * HD, HL * HD)
        qkv_bias = jnp.concatenate(
            [
                jnp.concatenate([q_bias, jnp.zeros_like(q_bias)], axis=1).reshape(QK_LANES),
                v_bias,
                jnp.zeros((V_LANES - HL * HD,), F32),
            ]
        )[None]
        ups = pieces["up_bias"].astype(F32).reshape(all_groups, 2, 2, hid)
        up_mine = lax.dynamic_index_in_dim(
            lax.dynamic_index_in_dim(ups, x_index, 1, keepdims=False), core, 1, keepdims=False
        )
        up_bias_row = jnp.pad(up_mine, ((0, 0), (0, hid_pad - hid))).reshape(1, all_groups * hid_pad)
        out_both = in_core_order(out_all, swap_cores(out_all), 2)[:, :part].reshape(width, width_pad)
        out_mine = lax.dynamic_slice_in_dim(out_both, quarter * HSTEP * HD, HL * HD, axis=0)
        head_row = lax.broadcasted_iota(jnp.int32, (HL * HD, 1), 0) // HD
        own_head = (head_row > 0) | (quarter == 0)
        out_mine = pad_rows(jnp.where(own_head, out_mine, jnp.zeros_like(out_mine)), V_LANES)
        layers.append(
            {
                "qkv": qkv_all.reshape(width_pad, P_LANES),
                "qkv_bias": qkv_bias,
                "out": out_mine,
                "out_bias": feature("out_bias"),
                "up": up_all.reshape(width_pad, all_groups * hid_pad),
                "up_bias": up_bias_row,
                "down": down_all.reshape(all_groups * hid_pad, width_pad),
                "down_bias": feature("down_bias"),
                "gain_one": feature("gain_one"),
                "shift_one": feature("shift_one"),
                "gain_two": feature("gain_two"),
                "shift_two": feature("shift_two"),
            }
        )

    def sequence_of(group, turn):
        return group + groups * turn

    def to_groups(value):
        arrived = []
        for d in range(seq_count):
            target = (seq_index ^ d) >> 1
            send = []
            for turn in range(rounds):
                number = sequence_of(target, turn)
                taken = lax.dynamic_index_in_dim(value, jnp.minimum(number, micro - 1), 0, keepdims=False)
                send.append(jnp.where(number < micro, taken, jnp.zeros_like(taken)))
            send = jnp.stack(send)
            if d:
                pairs = [
                    (c * seq_count + s, c * seq_count + (s ^ d))
                    for c in range(2)
                    for s in range(seq_count)
                    if s // half_blocks == c
                ]
                send = lax.ppermute(send, ("section", "seq"), pairs)
            arrived.append(send)
        slots = []
        for i in range(half_blocks):
            offset = (core * half_blocks + i) ^ seq_index
            chosen = arrived[0]
            for d in range(1, seq_count):
                chosen = jnp.where(offset == d, arrived[d], chosen)
            slots.append(chosen)
        return jnp.concatenate(slots, axis=1)

    def to_blocks(value, layer):
        value = jnp.stack(value).reshape(rounds, half_blocks, block_rows, width)
        arrived = []
        for e in range(groups):
            wanted = (seq_index ^ (2 * e)) % half_blocks
            send = lax.dynamic_index_in_dim(value, wanted, 1, keepdims=False)
            pairs = [
                (c * seq_count + s, layer * seq_count + (s ^ (2 * e)))
                for c in range(2)
                for s in range(seq_count)
                if (s ^ (2 * e)) // half_blocks == c
            ]
            arrived.append(lax.ppermute(send, ("section", "seq"), pairs))
        result = []
        for number in range(micro):
            offset = (number % groups) ^ y_index
            turn = number // groups
            chosen = arrived[0][turn]
            for e in range(1, groups):
                chosen = jnp.where(offset == e, arrived[e][turn], chosen)
            result.append(chosen)
        return jnp.stack(result)

    positions = core * half_rows + jnp.arange(half_rows, dtype=jnp.int32)
    turn_lengths, live = [], []
    for turn in range(rounds):
        number = sequence_of(y_index, turn)
        at = dp_index * micro + jnp.minimum(number, micro - 1)
        turn_lengths.append(lax.dynamic_slice_in_dim(lengths, at, 1))
        live.append(number < micro)

    start_rows = widen(to_groups(inputs))
    grad_rows = widen(to_groups(cotangent))

    stored = [[None] * rounds for _ in range(2)]
    outputs = [[None] * rounds for _ in range(2)]
    rows_now = [start_rows[turn] for turn in range(rounds)]
    for l in range(2):
        for turn in range(rounds):
            result, kept = layer_forward(
                rows_now[turn].astype(F32), layers[l], turn_lengths[turn], mask, width
            )
            stored[l][turn] = (rows_now[turn],) + kept[1:]
            outputs[l][turn] = result.astype(BF16)
            rows_now[turn] = outputs[l][turn]

    acts_local = [to_blocks([narrow(o).astype(BF16) for o in outputs[l]], l) for l in range(2)]
    acts_local = jnp.where(core == 0, acts_local[0], acts_local[1])
    total_seqs = dealing.shape[0]
    numbers = jnp.arange(total_seqs, dtype=jnp.int32)
    position = jnp.sum(jnp.where(dealing[:, None] == numbers[None, :], numbers[:, None], 0), axis=0)
    target = lax.dynamic_slice_in_dim(position, dp_index * micro, micro) // micro
    anchor = lax.dynamic_slice_in_dim(dealing, dp_index * micro, micro) // micro
    dealt = []
    for d in range(dp_count):
        dest = dp_index ^ d
        send = acts_local[0]
        for i in range(1, micro):
            send = jnp.where(target[i] == dest, acts_local[i], send)
        if d:
            send = lax.ppermute(send, "dp", [(i, i ^ d) for i in range(dp_count)])
        dealt.append(send)
    acts = []
    for j in range(micro):
        offset = anchor[j] ^ dp_index
        chosen = dealt[0]
        for d in range(1, dp_count):
            chosen = jnp.where(offset == d, dealt[d], chosen)
        acts.append(chosen)
    acts = jnp.stack(acts)

    def total(values):
        return functools.reduce(jnp.add, values)

    def product(operands):
        return total([dot_0(a, b) for a, b in operands]).astype(BF16)

    once = (x_index == 0).astype(F32)
    grads = []
    for turn in range(rounds):
        valid = (positions < turn_lengths[turn]) & live[turn]
        grads.append(jnp.where(valid[:, None], grad_rows[turn].astype(F32), 0.0))

    finished = [None, None]
    sent_back = [None, None]
    for l in (1, 0):
        w = layers[l]
        smalls, operands = [], []
        middles = []
        for turn in range(rounds):
            grad_middle, small, ops = ffn_backward(grads[turn], stored[l][turn], w, mask, width)
            middles.append(grad_middle)
            smalls.append(small)
            operands.append(ops)
        d_down = product([ops["down"] for ops in operands])
        d_up = product([ops["up"] for ops in operands])
        down_done = scatter_blocks(d_down.reshape(all_groups, hid_pad, width_pad), list(reversed(order_zy)), places)
        up_done = scatter_blocks(
            d_up.reshape(all_groups, 2 * part_pad, all_groups * hid_pad), list(reversed(order_zy)), places
        )
        returned = []
        for turn in range(rounds):
            grad_in, small, ops = attn_layer_backward(
                middles[turn], stored[l][turn], w, turn_lengths[turn], mask, width
            )
            returned.append(grad_in.astype(BF16))
            smalls[turn].update(small)
            operands[turn].update(ops)
        sent_back[l] = returned
        if l == 1:
            grads = [r.astype(F32) for r in returned]
        d_out = product([ops["out"] for ops in operands])[: HL * HD]
        d_out = jnp.where(own_head, d_out, jnp.zeros_like(d_out))
        d_out_full = lax.dynamic_update_slice_in_dim(
            jnp.zeros((width, width_pad), BF16), d_out, quarter * HSTEP * HD, axis=0
        )
        d_out_full = jnp.pad(
            d_out_full.reshape(chips, part, 2, width_pad // 2), ((0, 0), (0, part_pad - part), (0, 0), (0, 0))
        )
        mine = jnp.where(core == 0, d_out_full[:, :, 0], d_out_full[:, :, 1])
        other = jnp.where(core == 0, d_out_full[:, :, 1], d_out_full[:, :, 0])
        d_out_half = (mine.astype(F32) + swap_cores(other).astype(F32)).astype(BF16)
        out_done = scatter_blocks(d_out_half, list(reversed([X_BIT] + order_zy)), places_all)

        sums = {name: total([small[name] for small in smalls]) for name in smalls[0]}

        def feature_sum(name):
            return sums[name].reshape(chips, part_pad)[:, :part] * once

        q_sum = sums["packed"][:QK_LANES].reshape(HL, 2, HD)[:, 0].reshape(HL * HD)
        v_sum = sums["packed"][QK_LANES : QK_LANES + HL * HD]
        qv_sum = jnp.stack(
            [
                lax.dynamic_update_slice_in_dim(
                    jnp.zeros((H * HD,), F32), jnp.where(own_head[:, 0], s, 0.0), quarter * HSTEP * HD, axis=0
                )
                for s in (q_sum, v_sum)
            ]
        ).reshape(chips, -1)
        up_sum = sums["up_bias"].reshape(all_groups, 1, 1, hid_pad)[..., :hid]
        at_x = jnp.arange(2)[None, :, None, None] == x_index
        at_c = jnp.arange(2)[None, None, :, None] == core
        up_sum = jnp.where(at_x & at_c, up_sum, 0.0).reshape(chips, -1)
        small_cols = jnp.concatenate(
            [qv_sum, feature_sum("out_bias"), up_sum]
            + [feature_sum(name) for name in ("down_bias", "gain_one", "shift_one", "gain_two", "shift_two")],
            axis=1,
        ).astype(BF16)
        small_cols = jnp.pad(small_cols, ((0, 0), (0, P_LANES - small_total)))[:, None, :]
        d_qkv = product([ops["qkv"] for ops in operands]).reshape(chips, part_pad, P_LANES)
        at_row = lax.broadcasted_iota(jnp.int32, (1, part_pad, 1), 1) == part
        d_qkv = jnp.where(at_row, small_cols, d_qkv)
        qkv_done = scatter_blocks(
            d_qkv.reshape(all_groups, 2 * part_pad, P_LANES), list(reversed(order_zy)), places
        )
        finished[l] = (qkv_done, out_done, up_done, down_done)

    def back_across_x(value):
        low, high = value[:part_pad], value[part_pad:]
        mine = jnp.where(x_index == 0, low, high)
        other = flip(jnp.where(x_index == 0, high, low), *X_BIT)
        return jnp.stack([jnp.where(x_index == 0, mine, other), jnp.where(x_index == 0, other, mine)])

    def own_layer(first, second):
        mine = jnp.where(core == 0, first, second)
        other = swap_cores(jnp.where(core == 0, second, first))
        return [jnp.where(core == 0, mine, other), jnp.where(core == 0, other, mine)]

    qkv_c = own_layer(*[back_across_x(finished[l][0]) for l in range(2)])
    up_c = own_layer(*[back_across_x(finished[l][2]) for l in range(2)])
    out_c = own_layer(finished[0][1], finished[1][1])
    down_c = own_layer(finished[0][3], finished[1][3])

    def heads_sum(lanes_of):
        parts = []
        for x in range(2):
            for c in range(2):
                q = 2 * x + c
                piece = lanes_of(qkv_c[c][x, :part].astype(F32))
                own = jnp.arange(HL * HD) >= (0 if q == 0 else HD)
                piece = jnp.where(own[None], piece, 0.0)
                parts.append(jnp.pad(piece, ((0, 0), (HSTEP * q * HD, (H - HL - HSTEP * q) * HD))))
        return total(parts)

    def qk_half(which):
        return lambda piece: piece[:, :QK_LANES].reshape(part, HL, 2, HD)[:, :, which].reshape(part, HL * HD)

    grad_w_qkv = jnp.concatenate(
        [heads_sum(qk_half(0)), heads_sum(qk_half(1)), heads_sum(lambda p: p[:, QK_LANES : QK_LANES + HL * HD])],
        axis=1,
    )
    grad_w_out = narrow(jnp.concatenate([out_c[0][:part], out_c[1][:part]], axis=1))
    up_parts = jnp.stack(
        [
            jnp.stack(
                [up_c[c][x, :part].reshape(part, all_groups, hid_pad)[..., :hid] for c in range(2)], axis=2
            )
            for x in range(2)
        ],
        axis=2,
    )
    grad_w_up = up_parts.astype(F32).reshape(part, -1)
    grad_w_down = narrow(jnp.concatenate([down_c[0][:hid], down_c[1][:hid]], axis=0))
    small_sum = total([qkv_c[c][x, part, :small_total].astype(F32) for x in range(2) for c in range(2)])
    small_out, at = {}, 0
    for name in SMALL:
        small_out[name] = small_sum[at : at + small_sizes[name]]
        at += small_sizes[name]

    grads_local = [to_blocks([narrow(r).astype(BF16) for r in sent_back[l]], l) for l in range(2)]
    input_grad = jnp.where(core == 0, grads_local[0], grads_local[1])
    return (
        acts[None],
        input_grad[None],
        grad_w_qkv[None],
        small_out["b_qv"][None],
        grad_w_out[None],
        small_out["out_bias"][None],
        grad_w_up[None],
        small_out["up_bias"][None],
        grad_w_down[None],
        small_out["down_bias"][None],
        small_out["gain_one"][None],
        small_out["shift_one"][None],
        small_out["gain_two"][None],
        small_out["shift_two"][None],
    )


def solution(mesh):
    wide = P("section", ("dp", "seq"), None)
    thin = P("section", ("dp", "seq"))
    in_specs = (
        P("dp", "seq", None),
        P("dp", "seq", None),
        P(),
        P(),
        wide,
        thin,
        wide,
        thin,
        wide,
        thin,
        wide,
        thin,
        thin,
        thin,
        thin,
        thin,
    )
    out_specs = (
        P("section", "dp", "seq", None),
        P("section", "dp", "seq", None),
        wide,
        thin,
        wide,
        thin,
        wide,
        thin,
        wide,
        thin,
        thin,
        thin,
        thin,
        thin,
    )
    return jax.shard_map(per_device, mesh=mesh, in_specs=in_specs, out_specs=out_specs, check_vma=False)
```

time: 4030 us -> 2550 us (0.63)
  waiting for transfers between devices: 2220 us -> 905 us
  matrix products: 876 us -> 478 us
  blocking collectives: 324 us -> 0 us
  other arithmetic: 247 us -> 506 us
  starting transfers between devices: 28.3 us -> 208 us
  Pallas kernels: 0 us -> 175 us
  local copies, waits for them, and re-layouts: 295 us -> 248 us
    all_gather x8 -> x0, waiting for transfers between devices: 1020 us -> none  [the longest x1 415 us: per_device(): lax.all_gather(shards[4], ('dp', 'seq'), axis=0, tiled=True)]
    ppermute x6 -> x137, waiting for transfers between devices: 6.62 us -> 905 us  [the longest x76 874 us: flip(): return lax.ppermute(value, axis, [(i, i ^ 1 << bit) for i in range(count)])]
    unnamed x20 -> x0, waiting for transfers between devices: 637 us -> none
    reduce_scatter x8 -> x0, waiting for transfers between devices: 506 us -> none  [the longest x1 187 us: per_device(): lax.psum_scatter(shortened(folded), 'seq', scatter_dimension=1, tiled=True)]
    dot_general x70 -> x62, matrix products: 876 us -> 478 us  [the longest x16 142 us: dot_0(): lax.dot_general(a, b, (((0,), (0,)), ((), ())), preferred_element_type=F32)]
    unnamed x3 -> x0, blocking collectives: 324 us -> none
    ppermute x6 -> x137, starting transfers between devices: 12 us -> 208 us  [the longest x76 97.4 us: flip(): return lax.ppermute(value, axis, [(i, i ^ 1 << bit) for i in range(count)])]
    select_n x14 -> x130, other arithmetic: 38.1 us -> 232 us  [the longest x2 65.9 us: per_device(): other = jnp.where(core == 0, d_out_full[:, :, 1], d_out_full[:, :, 0])]
  transfers between devices with their start and end apart: 27 -> 137, of which waited for: 18 -> 45; matrix products, arithmetic and copies ran while one was open for 14% -> 45% of each run, Pallas kernels for 0% -> 7%
where the time goes in v1:
time: 2550 us; the launch traced here: 2530 us
  waiting for transfers between devices  905 us (35%)
  other arithmetic  506 us (20%)
  matrix products  478 us (19%)
  local copies, waits for them, and re-layouts  248 us (10%)
  starting transfers between devices  208 us (8%)
  Pallas kernels  175 us (7%)
    ppermute x76, waiting for transfers between devices, flip(): return lax.ppermute(value, axis, [(i, i ^ 1 << bit) for i in range(count)])  874 us
    dot_general x16, matrix products, dot_0(): lax.dot_general(a, b, (((0,), (0,)), ((), ())), preferred_element_type=F32)  142 us
    dot_general x16, matrix products, dot_t(): lax.dot_general(a, b, (((1,), (1,)), ((), ())), preferred_element_type=F32)  132 us
    dot_general x16, matrix products, dot(): return jnp.dot(a, b, preferred_element_type=F32)  116 us
    pallas_call x4, Pallas kernels, attn_backward(): pl.pallas_call(attn_bwd_kernel, grid=(PAIRS,), in_specs=[pl.BlockSpec(mem...  111 us
    ppermute x76, starting transfers between devices, flip(): return lax.ppermute(value, axis, [(i, i ^ 1 << bit) for i in range(count)])  97.4 us
    dot_general x10, matrix products, narrow(): lax.dot_general(value.astype(BF16), spread, (((value.ndim - 1,), (1,)), (...  66.9 us
    select_n x2, other arithmetic, per_device(): other = jnp.where(core == 0, d_out_full[:, :, 1], d_out_full[:, :, 0])  65.9 us
  transfers between devices with their start and end apart: 137, of which 45 were waited for; matrix products, arithmetic and copies ran while one was open for 45% of the time, Pallas kernels for 7%

profile of v1, /device:TPU:1, one launch (start us, length us, event | category | flops | bytes accessed | tf_op | source)
XLA Modules:
  0.0 2534.8 jit_solution(11049696781811852623)
XLA Ops:
  96.6 11.5 collective-permute-done.11
  123.5 14.7 collective-permute-done.24
  152.3 12.8 collective-permute-done.5
  212.8 22.0 collective-permute-done.6
  236.6 11.9 collective-permute-start.7
  293.9 11.9 collective-permute-start.14
  310.2 12.2 collective-permute-start.54
  326.3 12.2 collective-permute-start.45
  363.9 38.0 %collective-permute-done.45 = bf16[2,2,1,2,104,832]{5,4,3,2,1,0:T(8,128)(2,1)} collective-permute-done((bf16[2,2,1,2,104,832]{5,4,3,2,1,0:T(8,128)(2,1)}, bf16[2,2,1,2,104,832]{5,4,3,2,1,0:T(8,128)(2,1)}, u32[]{:S(2)}, u32[]{:S(2)}) %collective-permute-start.45) | collective-permute-done | bytes 1384480 | tf_op jit(solution)/shard_map/ppermute | solution.py:156
  419.9 16.4 attn_fwd.5
  443.2 16.2 attn_fwd.4
  497.5 16.9 collective-permute-done.39
  516.5 10.8 collective-permute-done.31
  527.3 36.5 %collective-permute-done.16 = bf16[512,1664]{1,0:T(8,128)(2,1)} collective-permute-done((bf16[512,1664]{1,0:T(8,128)(2,1)}, bf16[512,1664]{1,0:T(8,128)(2,1)}, u32[]{:S(2)}, u32[]{:S(2)}) %collective-permute-start.16) | collective-permute-done | bytes 1703968 | tf_op jit(solution)/shard_map/ppermute | solution.py:156
  593.2 10.1 fusion.195
  603.3 10.2 convolution_convert_fusion.12
  627.5 10.2 convolution_convert_fusion.14
  659.2 34.4 %collective-permute-done.40 = bf16[2,2,1,2,104,1408]{5,4,3,2,1,0:T(8,128)(2,1)} collective-permute-done((bf16[2,2,1,2,104,1408]{5,4,3,2,1,0:T(8,128)(2,1)}, bf16[2,2,1,2,104,1408]{5,4,3,2,1,0:T(8,128)(2,1)}, u32[]{:S(2)}, u32[]{:S(2)}) %collective-permute-start.40) | collective-permute-done | bytes 2342944 | tf_op jit(solution)/shard_map/ppermute | solution.py:156
  698.9 28.4 %collective-permute-done.28 = bf16[512,1664]{1,0:T(8,128)(2,1)} collective-permute-done((bf16[512,1664]{1,0:T(8,128)(2,1)}, bf16[512,1664]{1,0:T(8,128)(2,1)}, u32[]{:S(2)}, u32[]{:S(2)}) %collective-permute-start.28) | collective-permute-done | bytes 1703968 | tf_op jit(solution)/shard_map/ppermute | solution.py:156
  760.1 16.1 attn_fwd.7
  786.3 16.0 attn_fwd.6
  859.1 36.5 %collective-permute-done.48 = bf16[512,1664]{1,0:T(8,128)(2,1)} collective-permute-done((bf16[512,1664]{1,0:T(8,128)(2,1)}, bf16[512,1664]{1,0:T(8,128)(2,1)}, u32[]{:S(2)}, u32[]{:S(2)}) %collective-permute-start.48) | collective-permute-done | bytes 1703968 | tf_op jit(solution)/shard_map/ppermute | solution.py:156
  932.5 12.6 fusion.185
  945.2 14.7 convert_reduce_fusion
  977.7 10.0 convolution_convert_fusion.8
  998.3 10.0 convolution_convert_fusion.10
  1012.7 13.8 convert_reduce_fusion.1
  1038.2 12.8 add_convert_fusion.2
  1066.8 11.1 add_convert_fusion
  1095.8 30.9 %collective-permute-done.125 = bf16[2,2,1,208,1600]{4,3,2,1,0:T(8,128)(2,1)} collective-permute-done((bf16[2,2,1,208,1600]{4,3,2,1,0:T(8,128)(2,1)}, bf16[2,2,1,208,1600]{4,3,2,1,0:T(8,128)(2,1)}, u32[]{:S(2)}, u32[]{:S(2)}) %collective-permute-start.125) | collective-permute-done | bytes 2662432 | tf_op jit(solution)/shard_map/ppermute | solution.py:156
  1130.9 52.9 %collective-permute-done.133 = bf16[2,2,1,200,1664]{4,3,2,1,0:T(8,128)(2,1)S(1)} collective-permute-done((bf16[2,2,1,200,1664]{4,3,2,1,0:T(8,128)(2,1)}, bf16[2,2,1,200,1664]{4,3,2,1,0:T(8,128)(2,1)S(1)}, u32[]{:S(2)}, u32[]{:S(2)}) %collective-permute-start.133) | collective-permute-done | bytes 2662432 | tf_op jit(solution)/shard_map/ppermute | solution.py:156
  1219.5 16.2 collective-permute-start.65
  1266.7 28.9 %collective-permute-done.127 = bf16[1,1,1,208,1600]{4,3,2,1,0:T(8,128)(2,1)S(1)} collective-permute-done((bf16[1,1,1,208,1600]{4,3,2,1,0:T(8,128)(2,1)S(1)}, bf16[1,1,1,208,1600]{4,3,2,1,0:T(8,128)(2,1)S(1)}, u32[]{:S(2)}, u32[]{:S(2)}) %collective-permute-start.127) | collective-permute-done | bytes 665632 | tf_op jit(solution)/shard_map/ppermute | solution.py:156
  1316.5 27.9 %attn_bwd.6 = bf16[1024,1408]{1,0:T(8,128)(2,1)S(1)} custom-call(s32[1]{0:T(128)} %get-tuple-element.442.len_ref, bf16[1024,1408]{1,0:T(8,128)(2,1)} %copy-done.16, bf16[1024,1408]{1,0:T(8,128)(2,1)} %copy-done.16, bf16[1024,512]{1,0:T(8,128)(2,1)S(1)} %fusion.216.g_ref), custom_call_target="tpu_custom_call" | custom-call | flops 18790481920 | bytes 8650752 | tf_op jit(solution)/shard_map/attn_bwd/pallas_call | solution.py:134
  1372.3 27.6 %attn_bwd.4 = bf16[1024,1408]{1,0:T(8,128)(2,1)S(1)} custom-call(s32[1]{0:T(128)} %get-tuple-element.441.len_ref, bf16[1024,1408]{1,0:T(8,128)(2,1)} %copy-done.15, bf16[1024,1408]{1,0:T(8,128)(2,1)} %copy-done.15, bf16[1024,512]{1,0:T(8,128)(2,1)S(1)} %fusion.214.g_ref), custom_call_target="tpu_custom_call" | custom-call | flops 18790481920 | bytes 8650752 | tf_op jit(solution)/shard_map/attn_bwd/pallas_call | solution.py:134
  1420.1 13.1 reshape.939
  1433.2 33.1 %broadcast_select_fusion = (bf16[16,104,1,832]{3,2,1,0:T(2,128)(2,1)}, f32[16,104,1,832]{3,2,1,0:T(1,128)}) fusion(pred[]{:T(512)S(6)} %eq.143, bf16[16,100,2,832]{3,2,1,0:T(2,128)(2,1)} %reshape.939), kind=kLoop, calls=%fused_computation.28 | loop fusion | flops 4153344 | bytes 13631489 | tf_op jit(solution)/shard_map/jit(_where)/select_n | solution.py:641
  1492.3 26.2 %collective-permute-done.69 = bf16[256,1600]{0,1:T(8,128)(2,1)S(1)} collective-permute-done((bf16[256,1600]{0,1:T(8,128)(2,1)}, bf16[256,1600]{0,1:T(8,128)(2,1)S(1)}, u32[]{:S(2)}, u32[]{:S(2)}) %collective-permute-start.69) | collective-permute-done | bytes 819232 | tf_op jit(solution)/shard_map/ppermute | solution.py:581
  1528.8 36.5 %collective-permute-done.90 = bf16[512,1664]{1,0:T(8,128)(2,1)S(1)} collective-permute-done((bf16[512,1664]{1,0:T(8,128)(2,1)S(1)}, bf16[512,1664]{1,0:T(8,128)(2,1)S(1)}, u32[]{:S(2)}, u32[]{:S(2)}) %collective-permute-start.90) | collective-permute-done | bytes 1703968 | tf_op jit(solution)/shard_map/ppermute | solution.py:156
  1606.5 14.9 collective-permute-start.99
  1645.5 15.8 convert_reduce_fusion.2
  1661.4 10.3 fusion.182
  1688.2 15.8 convert_reduce_fusion.3
  1717.0 10.3 add_convert_fusion.3
  1743.4 12.5 add_convert_fusion.1
  1768.6 34.9 %collective-permute-done.121 = bf16[2,2,1,208,1600]{4,3,2,1,0:T(8,128)(2,1)} collective-permute-done((bf16[2,2,1,208,1600]{4,3,2,1,0:T(8,128)(2,1)}, bf16[2,2,1,208,1600]{4,3,2,1,0:T(8,128)(2,1)}, u32[]{:S(2)}, u32[]{:S(2)}) %collective-permute-start.121) | collective-permute-done | bytes 2662432 | tf_op jit(solution)/shard_map/ppermute | solution.py:156
  1807.5 52.5 %collective-permute-done.130 = bf16[2,2,1,200,1664]{4,3,2,1,0:T(8,128)(2,1)S(1)} collective-permute-done((bf16[2,2,1,200,1664]{4,3,2,1,0:T(8,128)(2,1)S(1)}, bf16[2,2,1,200,1664]{4,3,2,1,0:T(8,128)(2,1)S(1)}, u32[]{:S(2)}, u32[]{:S(2)}) %collective-permute-start.130) | collective-permute-done | bytes 2662432 | tf_op jit(solution)/shard_map/ppermute | solution.py:156
  1897.2 21.9 collective-permute-done.131
  1924.3 28.2 %collective-permute-done.123 = bf16[1,1,1,208,1600]{4,3,2,1,0:T(8,128)(2,1)S(1)} collective-permute-done((bf16[1,1,1,208,1600]{4,3,2,1,0:T(8,128)(2,1)S(1)}, bf16[1,1,1,208,1600]{4,3,2,1,0:T(8,128)(2,1)S(1)}, u32[]{:S(2)}, u32[]{:S(2)}) %collective-permute-start.123) | collective-permute-done | bytes 665632 | tf_op jit(solution)/shard_map/ppermute | solution.py:156
  1952.9 29.8 %collective-permute-done.132 = bf16[1,1,1,200,1664]{4,3,2,1,0:T(8,128)(2,1)S(1)} collective-permute-done((bf16[1,1,1,200,1664]{4,3,2,1,0:T(8,128)(2,1)S(1)}, bf16[1,1,1,200,1664]{4,3,2,1,0:T(8,128)(2,1)S(1)}, u32[]{:S(2)}, u32[]{:S(2)}) %collective-permute-start.132) | collective-permute-done | bytes 665632 | tf_op jit(solution)/shard_map/ppermute | solution.py:156
  1992.8 27.6 %attn_bwd.5 = bf16[1024,1408]{1,0:T(8,128)(2,1)S(1)} custom-call(s32[1]{0:T(128)} %get-tuple-element.441.len_ref, bf16[1024,1408]{1,0:T(8,128)(2,1)} %copy-done.14, bf16[1024,1408]{1,0:T(8,128)(2,1)} %copy-done.14, bf16[1024,512]{1,0:T(8,128)(2,1)S(1)} %fusion.215.g_ref), custom_call_target="tpu_custom_call" | custom-call | flops 18790481920 | bytes 8650752 | tf_op jit(solution)/shard_map/attn_bwd/pallas_call | solution.py:134
  2032.1 27.6 %attn_bwd.7 = bf16[1024,1408]{1,0:T(8,128)(2,1)S(1)} custom-call(s32[1]{0:T(128)} %get-tuple-element.442.len_ref, bf16[1024,1408]{1,0:T(8,128)(2,1)} %copy-done.13, bf16[1024,1408]{1,0:T(8,128)(2,1)} %copy-done.13, bf16[1024,512]{1,0:T(8,128)(2,1)S(1)} %fusion.217.g_ref), custom_call_target="tpu_custom_call" | custom-call | flops 18790481920 | bytes 8650752 | tf_op jit(solution)/shard_map/attn_bwd/pallas_call | solution.py:134
  2069.6 12.0 fusion.196
  2111.3 13.5 reshape.937
  2124.8 32.9 %broadcast_select_fusion.2 = (bf16[16,104,1,832]{3,2,1,0:T(2,128)(2,1)S(1)}, f32[16,104,1,832]{3,2,1,0:T(1,128)}) fusion(pred[]{:T(512)S(6)} %eq.143, bf16[16,100,2,832]{3,2,1,0:T(2,128)(2,1)} %reshape.937), kind=kLoop, calls=%fused_computation.30 | loop fusion | flops 4153344 | bytes 13631489 | tf_op jit(solution)/shard_map/jit(_where)/select_n | solution.py:641
  2160.7 10.0 add_convert_fusion.5
  2213.7 11.2 collective-permute-done.84
  2224.9 36.5 %collective-permute-done.96 = bf16[512,1664]{1,0:T(8,128)(2,1)} collective-permute-done((bf16[512,1664]{1,0:T(8,128)(2,1)}, bf16[512,1664]{1,0:T(8,128)(2,1)}, u32[]{:S(2)}, u32[]{:S(2)}) %collective-permute-start.96) | collective-permute-done | bytes 1703968 | tf_op jit(solution)/shard_map/ppermute | solution.py:156
  2323.2 14.2 collective-permute-done.112
  2343.1 17.0 collective-permute-done.113
  2368.7 21.5 collective-permute-done.105
  2391.2 40.6 %collective-permute-done.101 = bf16[2,2,1,208,1408]{4,3,2,1,0:T(8,128)(2,1)S(1)} collective-permute-done((bf16[2,2,1,208,1408]{4,3,2,1,0:T(8,128)(2,1)S(1)}, bf16[2,2,1,208,1408]{4,3,2,1,0:T(8,128)(2,1)S(1)}, u32[]{:S(2)}, u32[]{:S(2)}) %collective-permute-start.101) | collective-permute-done | bytes 2342944 | tf_op jit(solution)/shard_map/ppermute | solution.py:156
  2435.5 36.0 %collective-permute-done.102 = bf16[2,1,1,208,1408]{4,3,2,1,0:T(8,128)(2,1)S(1)} collective-permute-done((bf16[2,1,1,208,1408]{4,3,2,1,0:T(8,128)(2,1)S(1)}, bf16[2,1,1,208,1408]{4,3,2,1,0:T(8,128)(2,1)S(1)}, u32[]{:S(2)}, u32[]{:S(2)}) %collective-permute-start.102) | collective-permute-done | bytes 1171488 | tf_op jit(solution)/shard_map/ppermute | solution.py:156
  2472.5 27.5 %collective-permute-done.103 = bf16[1,1,1,208,1408]{4,3,2,1,0:T(8,128)(2,1)S(1)} collective-permute-done((bf16[1,1,1,208,1408]{4,3,2,1,0:T(8,128)(2,1)S(1)}, bf16[1,1,1,208,1408]{4,3,2,1,0:T(8,128)(2,1)S(1)}, u32[]{:S(2)}, u32[]{:S(2)}) %collective-permute-start.103) | collective-permute-done | bytes 585760 | tf_op jit(solution)/shard_map/ppermute | solution.py:156
  (1628 shorter events, 1160.9 us)
Async XLA Ops:
  12.1 74.5 %collective-permute-start.3 = (bf16[2,104,1408]{2,1,0:T(8,128)(2,1)}, bf16[2,104,1408]{2,1,0:T(8,128)(2,1)}, u32[]{:S(2)}, u32[]{:S(2)}) collective-permute-start(bf16[2,104,1408]{2,1,0:T(8,128)(2,1)} %broadcast_select_fusion.142), channel_id=1, source_target_pairs={{0,16},{16,0},{1,17},{17,1},{2,18},{18,2},{3,19},{19,3},{4,20},{20... | collective-permute-start | bytes 1757192 | tf_op jit(solution)/shard_map/ppermute | solution.py:177
  16.9 72.7 %collective-permute-start.23 = (bf16[200,1664]{1,0:T(8,128)(2,1)}, bf16[200,1664]{1,0:T(8,128)(2,1)}, u32[]{:S(2)}, u32[]{:S(2)}) collective-permute-start(bf16[200,1664]{1,0:T(8,128)(2,1)} %broadcast_select_fusion.128), channel_id=1, source_target_pairs={{0,16},{16,0},{1,17},{17,1},{2,18},{18,2},{3,19},{19,3},{4,20},{20... | collective-permute-start | bytes 1996808 | tf_op jit(solution)/shard_map/ppermute | solution.py:177
  47.3 120.4 %collective-permute-start = (bf16[2,256,1600]{1,2,0:T(8,128)(2,1)}, bf16[2,256,1600]{1,2,0:T(8,128)(2,1)}, u32[]{:S(2)}, u32[]{:S(2)}) collective-permute-start(bf16[2,256,1600]{1,2,0:T(8,128)(2,1)} %pad_maximum_fusion.64), channel_id=1, source_target_pairs={{0,3},{1,2},{18,17},{19,16},{4,7},{5,6},{22,21},{23,20},{8,11},{9,... | collective-permute-start | bytes 4915208 | tf_op jit(solution)/shard_map/ppermute | solution.py:510
  85.1 83.9 %collective-permute-start.1 = (bf16[2,256,1600]{1,2,0:T(8,128)(2,1)S(1)}, bf16[2,256,1600]{1,2,0:T(8,128)(2,1)S(1)}, u32[]{:S(2)}, u32[]{:S(2)}) collective-permute-start(bf16[2,256,1600]{1,2,0:T(8,128)(2,1)S(1)} %copy-done.241), channel_id=1, source_target_pairs={{0,2},{1,3},{18,16},{19,17},{4,6},{5,7},{22,20},{23,21},{8,10},{9,... | collective-permute-start | bytes 4915208 | tf_op jit(solution)/shard_map/ppermute | solution.py:510
  86.5 82.5 %collective-permute-start.2 = (bf16[2,256,1600]{1,2,0:T(8,128)(2,1)S(1)}, bf16[2,256,1600]{1,2,0:T(8,128)(2,1)S(1)}, u32[]{:S(2)}, u32[]{:S(2)}) collective-permute-start(bf16[2,256,1600]{1,2,0:T(8,128)(2,1)S(1)} %copy-done.240), channel_id=1, source_target_pairs={{0,1},{1,0},{18,19},{19,18},{4,5},{5,4},{22,23},{23,22},{8,9},{9,8... | collective-permute-start | bytes 4915208 | tf_op jit(solution)/shard_map/ppermute | solution.py:510
  169.1 67.5 %collective-permute-start.25 = (bf16[2,1,1,200,1664]{4,3,2,1,0:T(8,128)(2,1)}, bf16[2,1,1,200,1664]{4,3,2,1,0:T(8,128)(2,1)}, u32[]{:S(2)}, u32[]{:S(2)}) collective-permute-start(bf16[2,1,1,200,1664]{4,3,2,1,0:T(8,128)(2,1)} %pad_maximum_fusion.84), channel_id=1, source_target_pairs={{0,4},{4,0},{8,12},{12,8},{1,5},{5,1},{9,13},{13,9},{2,6},{6,2},{1... | collective-permute-start | bytes 3993608 | tf_op jit(solution)/shard_map/ppermute | solution.py:156
  182.1 69.8 %collective-permute-start.13 = (bf16[2,2,1,2,104,832]{5,4,3,2,1,0:T(8,128)(2,1)}, bf16[2,2,1,2,104,832]{5,4,3,2,1,0:T(8,128)(2,1)}, u32[]{:S(2)}, u32[]{:S(2)}) collective-permute-start(bf16[2,2,1,2,104,832]{5,4,3,2,1,0:T(8,128)(2,1)} %pad_maximum_fusion.80), channel_id=1, source_target_pairs={{0,2},{1,3},{2,0},{3,1},{4,6},{5,7},{6,4},{7,5},{8,10},{9,11},{10,... | collective-permute-start | bytes 4153352 | tf_op jit(solution)/shard_map/ppermute | solution.py:156
  202.0 104.1 %collective-permute-start.73 = (bf16[512,1664]{1,0:T(8,128)(2,1)}, bf16[512,1664]{1,0:T(8,128)(2,1)}, u32[]{:S(2)}, u32[]{:S(2)}) collective-permute-start(bf16[512,1664]{1,0:T(8,128)(2,1)} %get-tuple-element.231), channel_id=1, source_target_pairs={{0,16},{16,0},{1,17},{17,1},{2,18},{18,2},{3,19},{19,3},{4,20},{20... | collective-permute-start | bytes 5111816 | tf_op jit(solution)/shard_map/ppermute | solution.py:177
  211.3 98.9 %collective-permute-start.85 = (bf16[512,1664]{1,0:T(8,128)(2,1)S(1)}, bf16[512,1664]{1,0:T(8,128)(2,1)S(1)}, u32[]{:S(2)}, u32[]{:S(2)}) collective-permute-start(bf16[512,1664]{1,0:T(8,128)(2,1)S(1)} %copy-done.96), channel_id=1, source_target_pairs={{0,16},{16,0},{1,17},{17,1},{2,18},{18,2},{3,19},{19,3},{4,20},{20... | collective-permute-start | bytes 5111816 | tf_op jit(solution)/shard_map/ppermute | solution.py:177
  236.6 101.9 %collective-permute-start.7 = (bf16[2,2,1,2,104,1408]{5,4,3,2,1,0:T(8,128)(2,1)S(1)}, bf16[2,2,1,2,104,1408]{5,4,3,2,1,0:T(8,128)(2,1)S(1)}, u32[]{:S(2)}, u32[]{:S(2)}) collective-permute-start(bf16[2,2,1,2,104,1408]{5,4,3,2,1,0:T(8,128)(2,1)S(1)} %pad_maximum_fusion.30), channel_id=1, source_target_pairs={{0,2},{1,3},{2,0},{3,1},{4,6},{5,7},{6,4},{7,5},{8,10},{9,11},{10,... | collective-permute-start | bytes 7028744 | tf_op jit(solution)/shard_map/ppermute | solution.py:156
  251.9 328.2 %collective-permute-start.26 = (bf16[2,2,1,200,1664]{4,3,2,1,0:T(8,128)(2,1)}, bf16[2,2,1,200,1664]{4,3,2,1,0:T(8,128)(2,1)}, u32[]{:S(2)}, u32[]{:S(2)}) collective-permute-start(bf16[2,2,1,200,1664]{4,3,2,1,0:T(8,128)(2,1)} %pad_maximum_fusion.28), channel_id=1, source_target_pairs={{0,2},{1,3},{2,0},{3,1},{4,6},{5,7},{6,4},{7,5},{8,10},{9,11},{10,... | collective-permute-start | bytes 7987208 | tf_op jit(solution)/shard_map/ppermute | solution.py:156
  310.2 170.9 %collective-permute-start.54 = (bf16[1,1,1,200,1664]{4,3,2,1,0:T(8,128)(2,1)}, bf16[1,1,1,200,1664]{4,3,2,1,0:T(8,128)(2,1)}, u32[]{:S(2)}, u32[]{:S(2)}) collective-permute-start(bf16[1,1,1,200,1664]{4,3,2,1,0:T(8,128)(2,1)} %bitcast.78), channel_id=1, source_target_pairs={{0,2},{1,3},{2,0},{3,1},{4,6},{5,7},{6,4},{7,5},{8,10},{9,11},{10,... | collective-permute-start | bytes 1996808 | tf_op jit(solution)/shard_map/ppermute | solution.py:156
  326.3 75.7 %collective-permute-start.45 = (bf16[2,2,1,2,104,832]{5,4,3,2,1,0:T(8,128)(2,1)}, bf16[2,2,1,2,104,832]{5,4,3,2,1,0:T(8,128)(2,1)}, u32[]{:S(2)}, u32[]{:S(2)}) collective-permute-start(bf16[2,2,1,2,104,832]{5,4,3,2,1,0:T(8,128)(2,1)} %pad_maximum_fusion.81), channel_id=1, source_target_pairs={{0,2},{1,3},{2,0},{3,1},{4,6},{5,7},{6,4},{7,5},{8,10},{9,11},{10,... | collective-permute-start | bytes 4153352 | tf_op jit(solution)/shard_map/ppermute | solution.py:156
  346.4 59.9 %collective-permute-start.29 = (bf16[512,1664]{1,0:T(8,128)(2,1)}, bf16[512,1664]{1,0:T(8,128)(2,1)S(1)}, u32[]{:S(2)}, u32[]{:S(2)}) collective-permute-start(bf16[512,1664]{1,0:T(8,128)(2,1)} %get-tuple-element.213), channel_id=1, source_target_pairs={{0,16},{16,0},{1,17},{17,1},{2,18},{18,2},{3,19},{19,3},{4,20},{20... | collective-permute-start | bytes 5111816 | tf_op jit(solution)/shard_map/ppermute | solution.py:177
  347.9 135.1 %collective-permute-start.38 = (bf16[1,1,1,2,104,1408]{5,4,3,2,1,0:T(8,128)(2,1)}, bf16[1,1,1,2,104,1408]{5,4,3,2,1,0:T(8,128)(2,1)}, u32[]{:S(2)}, u32[]{:S(2)}) collective-permute-start(bf16[1,1,1,2,104,1408]{5,4,3,2,1,0:T(8,128)(2,1)} %maximum_bitcast_fusion.6), channel_id=1, source_target_pairs={{0,8},{4,12},{8,0},{12,4},{1,9},{5,13},{9,1},{13,5},{2,10},{6,14},... | collective-permute-start | bytes 1757192 | tf_op jit(solution)/shard_map/ppermute | solution.py:156
  401.9 91.1 %collective-permute-start.51 = (bf16[1,1,1,2,104,1600]{5,4,3,2,1,0:T(8,128)(2,1)}, bf16[1,1,1,2,104,1600]{5,4,3,2,1,0:T(8,128)(2,1)}, u32[]{:S(2)}, u32[]{:S(2)}) collective-permute-start(bf16[1,1,1,2,104,1600]{5,4,3,2,1,0:T(8,128)(2,1)} %maximum_bitcast_fusion.4), channel_id=1, source_target_pairs={{0,8},{4,12},{8,0},{12,4},{1,9},{5,13},{9,1},{13,5},{2,10},{6,14},... | collective-permute-start | bytes 1996808 | tf_op jit(solution)/shard_map/ppermute | solution.py:156
  490.3 73.5 %collective-permute-start.16 = (bf16[512,1664]{1,0:T(8,128)(2,1)}, bf16[512,1664]{1,0:T(8,128)(2,1)}, u32[]{:S(2)}, u32[]{:S(2)}) collective-permute-start(bf16[512,1664]{1,0:T(8,128)(2,1)} %add_convert_fusion.43), channel_id=1, source_target_pairs={{0,1},{1,0},{2,3},{3,2},{4,5},{5,4},{6,7},{7,6},{8,9},{9,8},{10,11... | collective-permute-start | bytes 5111816 | tf_op jit(solution)/shard_map/ppermute | solution.py:156
  493.0 92.4 %collective-permute-start.22 = (bf16[2,2,1,2,104,1600]{5,4,3,2,1,0:T(8,128)(2,1)}, bf16[2,2,1,2,104,1600]{5,4,3,2,1,0:T(8,128)(2,1)}, u32[]{:S(2)}, u32[]{:S(2)}) collective-permute-start(bf16[2,2,1,2,104,1600]{5,4,3,2,1,0:T(8,128)(2,1)} %pad_maximum_fusion.26), channel_id=1, source_target_pairs={{0,2},{1,3},{2,0},{3,1},{4,6},{5,7},{6,4},{7,5},{8,10},{9,11},{10,... | collective-permute-start | bytes 7987208 | tf_op jit(solution)/shard_map/ppermute | solution.py:156
  514.4 131.1 %collective-permute-start.55 = (bf16[1,1,2,200,1664]{4,3,2,1,0:T(8,128)(2,1)}, bf16[1,1,2,200,1664]{4,3,2,1,0:T(8,128)(2,1)}, u32[]{:S(2)}, u32[]{:S(2)}) collective-permute-start(bf16[1,1,2,200,1664]{4,3,2,1,0:T(8,128)(2,1)} %pad_maximum_fusion.85), channel_id=1, source_target_pairs={{0,8},{4,12},{8,0},{12,4},{1,9},{5,13},{9,1},{13,5},{2,10},{6,14},... | collective-permute-start | bytes 3993608 | tf_op jit(solution)/shard_map/ppermute | solution.py:156
  643.9 96.4 %collective-permute-start.52 = (bf16[2,1,1,2,104,1600]{5,4,3,2,1,0:T(8,128)(2,1)}, bf16[2,1,1,2,104,1600]{5,4,3,2,1,0:T(8,128)(2,1)}, u32[]{:S(2)}, u32[]{:S(2)}) collective-permute-start(bf16[2,1,1,2,104,1600]{5,4,3,2,1,0:T(8,128)(2,1)} %pad_maximum_fusion.83), channel_id=1, source_target_pairs={{0,4},{4,0},{8,12},{12,8},{1,5},{5,1},{9,13},{13,9},{2,6},{6,2},{1... | collective-permute-start | bytes 3993608 | tf_op jit(solution)/shard_map/ppermute | solution.py:156
  656.0 71.4 %collective-permute-start.28 = (bf16[512,1664]{1,0:T(8,128)(2,1)}, bf16[512,1664]{1,0:T(8,128)(2,1)}, u32[]{:S(2)}, u32[]{:S(2)}) collective-permute-start(bf16[512,1664]{1,0:T(8,128)(2,1)} %add_convert_fusion.41), channel_id=1, source_target_pairs={{0,1},{1,0},{2,3},{3,2},{4,5},{5,4},{6,7},{7,6},{8,9},{9,8},{10,11... | collective-permute-start | bytes 5111816 | tf_op jit(solution)/shard_map/ppermute | solution.py:156
  659.2 145.9 %collective-permute-start.56 = (bf16[2,1,2,200,1664]{4,3,2,1,0:T(8,128)(2,1)}, bf16[2,1,2,200,1664]{4,3,2,1,0:T(8,128)(2,1)}, u32[]{:S(2)}, u32[]{:S(2)}) collective-permute-start(bf16[2,1,2,200,1664]{4,3,2,1,0:T(8,128)(2,1)} %pad_maximum_fusion.29), channel_id=1, source_target_pairs={{0,4},{4,0},{8,12},{12,8},{1,5},{5,1},{9,13},{13,9},{2,6},{6,2},{1... | collective-permute-start | bytes 7987208 | tf_op jit(solution)/shard_map/ppermute | solution.py:156
  745.1 167.2 %collective-permute-start.53 = (bf16[2,2,1,2,104,1600]{5,4,3,2,1,0:T(8,128)(2,1)}, bf16[2,2,1,2,104,1600]{5,4,3,2,1,0:T(8,128)(2,1)}, u32[]{:S(2)}, u32[]{:S(2)}) collective-permute-start(bf16[2,2,1,2,104,1600]{5,4,3,2,1,0:T(8,128)(2,1)} %pad_maximum_fusion.27), channel_id=1, source_target_pairs={{0,2},{1,3},{2,0},{3,1},{4,6},{5,7},{6,4},{7,5},{8,10},{9,11},{10,... | collective-permute-start | bytes 7987208 | tf_op jit(solution)/shard_map/ppermute | solution.py:156
  822.2 73.5 %collective-permute-start.48 = (bf16[512,1664]{1,0:T(8,128)(2,1)}, bf16[512,1664]{1,0:T(8,128)(2,1)}, u32[]{:S(2)}, u32[]{:S(2)}) collective-permute-start(bf16[512,1664]{1,0:T(8,128)(2,1)} %add_convert_fusion.35), channel_id=1, source_target_pairs={{0,1},{1,0},{2,3},{3,2},{4,5},{5,4},{6,7},{7,6},{8,9},{9,8},{10,11... | collective-permute-start | bytes 5111816 | tf_op jit(solution)/shard_map/ppermute | solution.py:156
  844.3 72.8 %collective-permute-start.36 = (bf16[2,256,1600]{1,2,0:T(8,128)(2,1)}, bf16[2,256,1600]{1,2,0:T(8,128)(2,1)}, u32[]{:S(2)}, u32[]{:S(2)}) collective-permute-start(bf16[2,256,1600]{1,2,0:T(8,128)(2,1)} %get-tuple-element.271), channel_id=1, source_target_pairs={{0,0},{1,1},{18,2},{19,3},{4,4},{5,5},{22,6},{23,7},{8,8},{9,9},{2... | collective-permute-start | bytes 4915208 | tf_op jit(solution)/shard_map/ppermute | solution.py:533
  846.1 70.9 %collective-permute-start.35 = (bf16[2,256,1600]{1,2,0:T(8,128)(2,1)}, bf16[2,256,1600]{1,2,0:T(8,128)(2,1)}, u32[]{:S(2)}, u32[]{:S(2)}) collective-permute-start(bf16[2,256,1600]{1,2,0:T(8,128)(2,1)} %get-tuple-element.270), channel_id=1, source_target_pairs={{2,0},{3,1},{16,2},{17,3},{6,4},{7,5},{20,6},{21,7},{10,8},{11,9},... | collective-permute-start | bytes 4915208 | tf_op jit(solution)/shard_map/ppermute | solution.py:533
  920.6 67.1 %collective-permute-start.49 = (bf16[512,1664]{1,0:T(8,128)(2,1)S(1)}, bf16[512,1664]{1,0:T(8,128)(2,1)S(1)}, u32[]{:S(2)}, u32[]{:S(2)}) collective-permute-start(bf16[512,1664]{1,0:T(8,128)(2,1)S(1)} %get-tuple-element.404), channel_id=1, source_target_pairs={{0,16},{16,0},{1,17},{17,1},{2,18},{18,2},{3,19},{19,3},{4,20},{20... | collective-permute-start | bytes 5111816 | tf_op jit(solution)/shard_map/ppermute | solution.py:177
  1009.9 71.9 %collective-permute-start.57 = (bf16[512,1664]{1,0:T(8,128)(2,1)}, bf16[512,1664]{1,0:T(8,128)(2,1)}, u32[]{:S(2)}, u32[]{:S(2)}) collective-permute-start(bf16[512,1664]{1,0:T(8,128)(2,1)} %broadcast_select_fusion.58), channel_id=1, source_target_pairs={{0,16},{16,0},{1,17},{17,1},{2,18},{18,2},{3,19},{19,3},{4,20},{20... | collective-permute-start | bytes 5111816 | tf_op jit(solution)/shard_map/ppermute | solution.py:177
  1011.8 73.2 %collective-permute-start.63 = (bf16[512,1664]{1,0:T(8,128)(2,1)}, bf16[512,1664]{1,0:T(8,128)(2,1)}, u32[]{:S(2)}, u32[]{:S(2)}) collective-permute-start(bf16[512,1664]{1,0:T(8,128)(2,1)} %broadcast_select_fusion.52), channel_id=1, source_target_pairs={{0,16},{16,0},{1,17},{17,1},{2,18},{18,2},{3,19},{19,3},{4,20},{20... | collective-permute-start | bytes 5111816 | tf_op jit(solution)/shard_map/ppermute | solution.py:177
  1065.3 61.4 %collective-permute-start.125 = (bf16[2,2,1,208,1600]{4,3,2,1,0:T(8,128)(2,1)}, bf16[2,2,1,208,1600]{4,3,2,1,0:T(8,128)(2,1)}, u32[]{:S(2)}, u32[]{:S(2)}) collective-permute-start(bf16[2,2,1,208,1600]{4,3,2,1,0:T(8,128)(2,1)} %broadcast_select_fusion.10), channel_id=1, source_target_pairs={{0,2},{1,3},{2,0},{3,1},{4,6},{5,7},{6,4},{7,5},{8,10},{9,11},{10,... | collective-permute-start | bytes 7987208 | tf_op jit(solution)/shard_map/ppermute | solution.py:156
  1081.8 102.0 %collective-permute-start.133 = (bf16[2,2,1,200,1664]{4,3,2,1,0:T(8,128)(2,1)}, bf16[2,2,1,200,1664]{4,3,2,1,0:T(8,128)(2,1)S(1)}, u32[]{:S(2)}, u32[]{:S(2)}) collective-permute-start(bf16[2,2,1,200,1664]{4,3,2,1,0:T(8,128)(2,1)} %broadcast_select_fusion.18), channel_id=1, source_target_pairs={{0,2},{1,3},{2,0},{3,1},{4,6},{5,7},{6,4},{7,5},{8,10},{9,11},{10,... | collective-permute-start | bytes 7987208 | tf_op jit(solution)/shard_map/ppermute | solution.py:156
  1085.1 102.6 %collective-permute-start.58 = (bf16[512,1664]{1,0:T(8,128)(2,1)S(1)}, bf16[512,1664]{1,0:T(8,128)(2,1)S(1)}, u32[]{:S(2)}, u32[]{:S(2)}) collective-permute-start(bf16[512,1664]{1,0:T(8,128)(2,1)S(1)} %add_convert_fusion.33), channel_id=1, source_target_pairs={{0,1},{1,0},{2,3},{3,2},{4,5},{5,4},{6,7},{7,6},{8,9},{9,8},{10,11... | collective-permute-start | bytes 5111816 | tf_op jit(solution)/shard_map/ppermute | solution.py:156
  1087.5 109.3 %collective-permute-start.64 = (bf16[512,1664]{1,0:T(8,128)(2,1)S(1)}, bf16[512,1664]{1,0:T(8,128)(2,1)S(1)}, u32[]{:S(2)}, u32[]{:S(2)}) collective-permute-start(bf16[512,1664]{1,0:T(8,128)(2,1)S(1)} %add_convert_fusion.29), channel_id=1, source_target_pairs={{0,1},{1,0},{2,3},{3,2},{4,5},{5,4},{6,7},{7,6},{8,9},{9,8},{10,11... | collective-permute-start | bytes 5111816 | tf_op jit(solution)/shard_map/ppermute | solution.py:156
  1092.2 127.2 %collective-permute-start.75 = (bf16[512,1664]{1,0:T(8,128)(2,1)}, bf16[512,1664]{1,0:T(8,128)(2,1)}, u32[]{:S(2)}, u32[]{:S(2)}) collective-permute-start(bf16[512,1664]{1,0:T(8,128)(2,1)} %add_convert_fusion.27), channel_id=1, source_target_pairs={{0,1},{1,0},{2,3},{3,2},{4,5},{5,4},{6,7},{7,6},{8,9},{9,8},{10,11... | collective-permute-start | bytes 5111816 | tf_op jit(solution)/shard_map/ppermute | solution.py:156
  1126.8 108.9 %collective-permute-start.87 = (bf16[512,1664]{1,0:T(8,128)(2,1)}, bf16[512,1664]{1,0:T(8,128)(2,1)}, u32[]{:S(2)}, u32[]{:S(2)}) collective-permute-start(bf16[512,1664]{1,0:T(8,128)(2,1)} %add_convert_fusion.23), channel_id=1, source_target_pairs={{0,1},{1,0},{2,3},{3,2},{4,5},{5,4},{6,7},{7,6},{8,9},{9,8},{10,11... | collective-permute-start | bytes 5111816 | tf_op jit(solution)/shard_map/ppermute | solution.py:156
  1183.8 75.8 %collective-permute-start.126 = (bf16[2,1,1,208,1600]{4,3,2,1,0:T(8,128)(2,1)}, bf16[2,1,1,208,1600]{4,3,2,1,0:T(8,128)(2,1)}, u32[]{:S(2)}, u32[]{:S(2)}) collective-permute-start(bf16[2,1,1,208,1600]{4,3,2,1,0:T(8,128)(2,1)} %broadcast_select_fusion.82), channel_id=1, source_target_pairs={{0,4},{4,0},{8,12},{12,8},{1,5},{5,1},{9,13},{13,9},{2,6},{6,2},{1... | collective-permute-start | bytes 3993608 | tf_op jit(solution)/shard_map/ppermute | solution.py:156
  1187.7 76.4 %collective-permute-start.134 = (bf16[2,1,1,200,1664]{4,3,2,1,0:T(8,128)(2,1)}, bf16[2,1,1,200,1664]{4,3,2,1,0:T(8,128)(2,1)}, u32[]{:S(2)}, u32[]{:S(2)}) collective-permute-start(bf16[2,1,1,200,1664]{4,3,2,1,0:T(8,128)(2,1)} %broadcast_select_fusion.90), channel_id=1, source_target_pairs={{0,4},{4,0},{8,12},{12,8},{1,5},{5,1},{9,13},{13,9},{2,6},{6,2},{1... | collective-permute-start | bytes 3993608 | tf_op jit(solution)/shard_map/ppermute | solution.py:156
  1218.2 87.5 %collective-permute-start.66 = (bf16[2,256,1600]{1,2,0:T(8,128)(2,1)}, bf16[2,256,1600]{1,2,0:T(8,128)(2,1)}, u32[]{:S(2)}, u32[]{:S(2)}) collective-permute-start(bf16[2,256,1600]{1,2,0:T(8,128)(2,1)} %get-tuple-element.266), channel_id=1, source_target_pairs={{0,16},{1,17},{18,18},{19,19},{4,20},{5,21},{22,22},{23,23},{8,24}... | collective-permute-start | bytes 4915208 | tf_op jit(solution)/shard_map/ppermute | solution.py:533
  1219.5 86.2 %collective-permute-start.65 = (bf16[2,256,1600]{1,2,0:T(8,128)(2,1)}, bf16[2,256,1600]{1,2,0:T(8,128)(2,1)}, u32[]{:S(2)}, u32[]{:S(2)}) collective-permute-start(bf16[2,256,1600]{1,2,0:T(8,128)(2,1)} %get-tuple-element.265), channel_id=1, source_target_pairs={{2,16},{3,17},{16,18},{17,19},{6,20},{7,21},{20,22},{21,23},{10,24... | collective-permute-start | bytes 4915208 | tf_op jit(solution)/shard_map/ppermute | solution.py:533
  1251.5 111.2 %collective-permute-start.76 = (bf16[512,1664]{1,0:T(8,128)(2,1)}, bf16[512,1664]{1,0:T(8,128)(2,1)}, u32[]{:S(2)}, u32[]{:S(2)}) collective-permute-start(bf16[512,1664]{1,0:T(8,128)(2,1)} %get-tuple-element.178), channel_id=1, source_target_pairs={{0,16},{16,0},{1,17},{17,1},{2,18},{18,2},{3,19},{19,3},{4,20},{20... | collective-permute-start | bytes 5111816 | tf_op jit(solution)/shard_map/ppermute | solution.py:177
  1311.4 179.3 %collective-permute-start.67 = (bf16[256,1600]{0,1:T(8,128)(2,1)}, bf16[256,1600]{0,1:T(8,128)(2,1)}, u32[]{:S(2)}, u32[]{:S(2)}) collective-permute-start(bf16[256,1600]{0,1:T(8,128)(2,1)} %get-tuple-element.293), channel_id=1, source_target_pairs={{0,12},{4,8},{8,4},{12,0},{1,13},{5,9},{9,5},{13,1},{2,14},{6,10},... | collective-permute-start | bytes 2457608 | tf_op jit(solution)/shard_map/ppermute | solution.py:581
  1312.9 178.0 %collective-permute-start.68 = (bf16[256,1600]{0,1:T(8,128)(2,1)}, bf16[256,1600]{0,1:T(8,128)(2,1)}, u32[]{:S(2)}, u32[]{:S(2)}) collective-permute-start(bf16[256,1600]{0,1:T(8,128)(2,1)} %get-tuple-element.294), channel_id=1, source_target_pairs={{0,8},{4,12},{8,0},{12,4},{1,9},{5,13},{9,1},{13,5},{2,10},{6,14},... | collective-permute-start | bytes 2457608 | tf_op jit(solution)/shard_map/ppermute | solution.py:581
  1410.9 72.5 %collective-permute-start.77 = (bf16[512,1664]{1,0:T(8,128)(2,1)}, bf16[512,1664]{1,0:T(8,128)(2,1)}, u32[]{:S(2)}, u32[]{:S(2)}) collective-permute-start(bf16[512,1664]{1,0:T(8,128)(2,1)} %broadcast_select_fusion.46), channel_id=1, source_target_pairs={{0,16},{16,0},{1,17},{17,1},{2,18},{18,2},{3,19},{19,3},{4,20},{20... | collective-permute-start | bytes 5111816 | tf_op jit(solution)/shard_map/ppermute | solution.py:177
  1414.3 73.6 %collective-permute-start.89 = (bf16[512,1664]{1,0:T(8,128)(2,1)}, bf16[512,1664]{1,0:T(8,128)(2,1)}, u32[]{:S(2)}, u32[]{:S(2)}) collective-permute-start(bf16[512,1664]{1,0:T(8,128)(2,1)} %broadcast_select_fusion.34), channel_id=1, source_target_pairs={{0,16},{16,0},{1,17},{17,1},{2,18},{18,2},{3,19},{19,3},{4,20},{20... | collective-permute-start | bytes 5111816 | tf_op jit(solution)/shard_map/ppermute | solution.py:177
  1487.9 464.9 %collective-permute-start.135 = (bf16[1,1,1,200,1664]{4,3,2,1,0:T(8,128)(2,1)}, bf16[1,1,1,200,1664]{4,3,2,1,0:T(8,128)(2,1)}, u32[]{:S(2)}, u32[]{:S(2)}) collective-permute-start(bf16[1,1,1,200,1664]{4,3,2,1,0:T(8,128)(2,1)} %broadcast_select_fusion.130), channel_id=1, source_target_pairs={{0,8},{4,12},{8,0},{12,4},{1,9},{5,13},{9,1},{13,5},{2,10},{6,14},... | collective-permute-start | bytes 1996808 | tf_op jit(solution)/shard_map/ppermute | solution.py:156
  1490.8 74.4 %collective-permute-start.90 = (bf16[512,1664]{1,0:T(8,128)(2,1)S(1)}, bf16[512,1664]{1,0:T(8,128)(2,1)S(1)}, u32[]{:S(2)}, u32[]{:S(2)}) collective-permute-start(bf16[512,1664]{1,0:T(8,128)(2,1)S(1)} %add_convert_fusion.22), channel_id=1, source_target_pairs={{0,1},{1,0},{2,3},{3,2},{4,5},{5,4},{6,7},{7,6},{8,9},{9,8},{10,11... | collective-permute-start | bytes 5111816 | tf_op jit(solution)/shard_map/ppermute | solution.py:156
  1527.5 94.0 %collective-permute-start.116 = (bf16[2,2,1,2,104,832]{5,4,3,2,1,0:T(8,128)(2,1)}, bf16[2,2,1,2,104,832]{5,4,3,2,1,0:T(8,128)(2,1)}, u32[]{:S(2)}, u32[]{:S(2)}) collective-permute-start(bf16[2,2,1,2,104,832]{5,4,3,2,1,0:T(8,128)(2,1)} %broadcast_select_fusion.76), channel_id=1, source_target_pairs={{0,2},{1,3},{2,0},{3,1},{4,6},{5,7},{6,4},{7,5},{8,10},{9,11},{10,... | collective-permute-start | bytes 4153352 | tf_op jit(solution)/shard_map/ppermute | solution.py:156
  1638.6 122.0 %collective-permute-start.118 = (bf16[1,1,1,2,104,832]{5,4,3,2,1,0:T(8,128)(2,1)}, bf16[1,1,1,2,104,832]{5,4,3,2,1,0:T(8,128)(2,1)}, u32[]{:S(2)}, u32[]{:S(2)}) collective-permute-start(bf16[1,1,1,2,104,832]{5,4,3,2,1,0:T(8,128)(2,1)} %broadcast_select_fusion.148), channel_id=1, source_target_pairs={{0,8},{4,12},{8,0},{12,4},{1,9},{5,13},{9,1},{13,5},{2,10},{6,14},... | collective-permute-start | bytes 1038344 | tf_op jit(solution)/shard_map/ppermute | solution.py:156
  1741.7 61.7 %collective-permute-start.121 = (bf16[2,2,1,208,1600]{4,3,2,1,0:T(8,128)(2,1)}, bf16[2,2,1,208,1600]{4,3,2,1,0:T(8,128)(2,1)}, u32[]{:S(2)}, u32[]{:S(2)}) collective-permute-start(bf16[2,2,1,208,1600]{4,3,2,1,0:T(8,128)(2,1)} %broadcast_select_fusion.11), channel_id=1, source_target_pairs={{0,2},{1,3},{2,0},{3,1},{4,6},{5,7},{6,4},{7,5},{8,10},{9,11},{10,... | collective-permute-start | bytes 7987208 | tf_op jit(solution)/shard_map/ppermute | solution.py:156
  1760.7 99.4 %collective-permute-start.130 = (bf16[2,2,1,200,1664]{4,3,2,1,0:T(8,128)(2,1)S(1)}, bf16[2,2,1,200,1664]{4,3,2,1,0:T(8,128)(2,1)S(1)}, u32[]{:S(2)}, u32[]{:S(2)}) collective-permute-start(bf16[2,2,1,200,1664]{4,3,2,1,0:T(8,128)(2,1)S(1)} %broadcast_select_fusion.19), channel_id=1, source_target_pairs={{0,2},{1,3},{2,0},{3,1},{4,6},{5,7},{6,4},{7,5},{8,10},{9,11},{10,... | collective-permute-start | bytes 7987208 | tf_op jit(solution)/shard_map/ppermute | solution.py:156
  1762.8 599.5 %collective-permute-start.119 = (bf16[1,1,1,1,104,832]{5,4,3,2,1,0:T(8,128)(2,1)}, bf16[1,1,1,1,104,832]{5,4,3,2,1,0:T(8,128)(2,1)}, u32[]{:S(2)}, u32[]{:S(2)}) collective-permute-start(bf16[1,1,1,1,104,832]{5,4,3,2,1,0:T(8,128)(2,1)} %broadcast_select_fusion.167), channel_id=1, source_target_pairs={{0,1},{1,0},{2,3},{3,2},{4,5},{5,4},{6,7},{7,6},{8,9},{9,8},{10,11... | collective-permute-start | bytes 519176 | tf_op jit(solution)/shard_map/ppermute | solution.py:156
  1765.4 98.6 %collective-permute-start.81 = (bf16[512,1664]{1,0:T(8,128)(2,1)S(1)}, bf16[512,1664]{1,0:T(8,128)(2,1)S(1)}, u32[]{:S(2)}, u32[]{:S(2)}) collective-permute-start(bf16[512,1664]{1,0:T(8,128)(2,1)S(1)} %add_convert_fusion.25), channel_id=1, source_target_pairs={{0,1},{1,0},{2,3},{3,2},{4,5},{5,4},{6,7},{7,6},{8,9},{9,8},{10,11... | collective-permute-start | bytes 5111816 | tf_op jit(solution)/shard_map/ppermute | solution.py:156
  1803.5 60.5 %collective-permute-start.93 = (bf16[512,1664]{1,0:T(8,128)(2,1)S(1)}, bf16[512,1664]{1,0:T(8,128)(2,1)S(1)}, u32[]{:S(2)}, u32[]{:S(2)}) collective-permute-start(bf16[512,1664]{1,0:T(8,128)(2,1)S(1)} %add_convert_fusion.21), channel_id=1, source_target_pairs={{0,1},{1,0},{2,3},{3,2},{4,5},{5,4},{6,7},{7,6},{8,9},{9,8},{10,11... | collective-permute-start | bytes 5111816 | tf_op jit(solution)/shard_map/ppermute | solution.py:156
  1879.5 107.7 %collective-permute-start.82 = (bf16[512,1664]{1,0:T(8,128)(2,1)}, bf16[512,1664]{1,0:T(8,128)(2,1)}, u32[]{:S(2)}, u32[]{:S(2)}) collective-permute-start(bf16[512,1664]{1,0:T(8,128)(2,1)} %get-tuple-element.168), channel_id=1, source_target_pairs={{0,16},{16,0},{1,17},{17,1},{2,18},{18,2},{3,19},{19,3},{4,20},{20... | collective-permute-start | bytes 5111816 | tf_op jit(solution)/shard_map/ppermute | solution.py:177
  1890.6 137.8 %collective-permute-start.94 = (bf16[512,1664]{1,0:T(8,128)(2,1)}, bf16[512,1664]{1,0:T(8,128)(2,1)S(1)}, u32[]{:S(2)}, u32[]{:S(2)}) collective-permute-start(bf16[512,1664]{1,0:T(8,128)(2,1)} %get-tuple-element.165), channel_id=1, source_target_pairs={{0,16},{16,0},{1,17},{17,1},{2,18},{18,2},{3,19},{19,3},{4,20},{20... | collective-permute-start | bytes 5111816 | tf_op jit(solution)/shard_map/ppermute | solution.py:177
  1985.4 185.3 %collective-permute-start.136 = (bf16[200,1664]{1,0:T(8,128)(2,1)}, bf16[200,1664]{1,0:T(8,128)(2,1)}, u32[]{:S(2)}, u32[]{:S(2)}) collective-permute-start(bf16[200,1664]{1,0:T(8,128)(2,1)} %get-tuple-element.154), channel_id=1, source_target_pairs={{0,16},{16,0},{1,17},{17,1},{2,18},{18,2},{3,19},{19,3},{4,20},{20... | collective-permute-start | bytes 1996808 | tf_op jit(solution)/shard_map/ppermute | solution.py:177
  1987.1 190.0 %collective-permute-start.129 = (bf16[2,104,1600]{2,1,0:T(8,128)(2,1)}, bf16[2,104,1600]{2,1,0:T(8,128)(2,1)}, u32[]{:S(2)}, u32[]{:S(2)}) collective-permute-start(bf16[2,104,1600]{2,1,0:T(8,128)(2,1)} %broadcast_select_fusion.114), channel_id=1, source_target_pairs={{0,16},{16,0},{1,17},{17,1},{2,18},{18,2},{3,19},{19,3},{4,20},{20... | collective-permute-start | bytes 1996808 | tf_op jit(solution)/shard_map/ppermute | solution.py:177
  2091.0 91.8 %collective-permute-start.83 = (bf16[512,1664]{1,0:T(8,128)(2,1)}, bf16[512,1664]{1,0:T(8,128)(2,1)}, u32[]{:S(2)}, u32[]{:S(2)}) collective-permute-start(bf16[512,1664]{1,0:T(8,128)(2,1)} %broadcast_select_fusion.40), channel_id=1, source_target_pairs={{0,16},{16,0},{1,17},{17,1},{2,18},{18,2},{3,19},{19,3},{4,20},{20... | collective-permute-start | bytes 5111816 | tf_op jit(solution)/shard_map/ppermute | solution.py:177
  2093.5 92.7 %collective-permute-start.95 = (bf16[512,1664]{1,0:T(8,128)(2,1)}, bf16[512,1664]{1,0:T(8,128)(2,1)}, u32[]{:S(2)}, u32[]{:S(2)}) collective-permute-start(bf16[512,1664]{1,0:T(8,128)(2,1)} %broadcast_select_fusion.28), channel_id=1, source_target_pairs={{0,16},{16,0},{1,17},{17,1},{2,18},{18,2},{3,19},{19,3},{4,20},{20... | collective-permute-start | bytes 5111816 | tf_op jit(solution)/shard_map/ppermute | solution.py:177
  2189.5 71.9 %collective-permute-start.96 = (bf16[512,1664]{1,0:T(8,128)(2,1)}, bf16[512,1664]{1,0:T(8,128)(2,1)}, u32[]{:S(2)}, u32[]{:S(2)}) collective-permute-start(bf16[512,1664]{1,0:T(8,128)(2,1)} %add_convert_fusion.20), channel_id=1, source_target_pairs={{0,1},{1,0},{2,3},{3,2},{4,5},{5,4},{6,7},{7,6},{8,9},{9,8},{10,11... | collective-permute-start | bytes 5111816 | tf_op jit(solution)/shard_map/ppermute | solution.py:156
  2210.1 110.4 %collective-permute-start.111 = (bf16[2,2,1,2,104,832]{5,4,3,2,1,0:T(8,128)(2,1)}, bf16[2,2,1,2,104,832]{5,4,3,2,1,0:T(8,128)(2,1)}, u32[]{:S(2)}, u32[]{:S(2)}) collective-permute-start(bf16[2,2,1,2,104,832]{5,4,3,2,1,0:T(8,128)(2,1)} %broadcast_select_fusion.77), channel_id=1, source_target_pairs={{0,2},{1,3},{2,0},{3,1},{4,6},{5,7},{6,4},{7,5},{8,10},{9,11},{10,... | collective-permute-start | bytes 4153352 | tf_op jit(solution)/shard_map/ppermute | solution.py:156
  2322.9 67.2 %collective-permute-start.105 = (bf16[2,2,1,208,1408]{4,3,2,1,0:T(8,128)(2,1)S(1)}, bf16[2,2,1,208,1408]{4,3,2,1,0:T(8,128)(2,1)S(1)}, u32[]{:S(2)}, u32[]{:S(2)}) collective-permute-start(bf16[2,2,1,208,1408]{4,3,2,1,0:T(8,128)(2,1)S(1)} %broadcast_select_fusion.22), channel_id=1, source_target_pairs={{0,2},{1,3},{2,0},{3,1},{4,6},{5,7},{6,4},{7,5},{8,10},{9,11},{10,... | collective-permute-start | bytes 7028744 | tf_op jit(solution)/shard_map/ppermute | solution.py:156
  2337.4 94.5 %collective-permute-start.101 = (bf16[2,2,1,208,1408]{4,3,2,1,0:T(8,128)(2,1)S(1)}, bf16[2,2,1,208,1408]{4,3,2,1,0:T(8,128)(2,1)S(1)}, u32[]{:S(2)}, u32[]{:S(2)}) collective-permute-start(bf16[2,2,1,208,1408]{4,3,2,1,0:T(8,128)(2,1)S(1)} %broadcast_select_fusion.23), channel_id=1, source_target_pairs={{0,2},{1,3},{2,0},{3,1},{4,6},{5,7},{6,4},{7,5},{8,10},{9,11},{10,... | collective-permute-start | bytes 7028744 | tf_op jit(solution)/shard_map/ppermute | solution.py:156
  2367.3 65.7 %collective-permute-start.120 = (bf16[104,832]{1,0:T(8,128)(2,1)S(1)}, bf16[104,832]{1,0:T(8,128)(2,1)S(1)}, u32[]{:S(2)}, u32[]{:S(2)}) collective-permute-start(bf16[104,832]{1,0:T(8,128)(2,1)S(1)} %select_bitcast_fusion.17), channel_id=1, source_target_pairs={{0,16},{16,0},{1,17},{17,1},{2,18},{18,2},{3,19},{19,3},{4,20},{20... | collective-permute-start | bytes 519176 | tf_op jit(solution)/shard_map/ppermute | solution.py:177
  (472 other events, 10478.2 us)

commit v2 on v1

v2 whole, which is shorter than its diff:
```python
import functools

import jax
import jax.numpy as jnp
from jax import lax
from jax.experimental import pallas as pl
from jax.experimental.pallas import tpu as pltpu
from jax.sharding import PartitionSpec as P

H = 25
HD = 64
QUARTERS = 4
HL = -(-H // QUARTERS)
HSTEP = (H - HL) // (QUARTERS - 1)
PAIRS = -(-HL // 2)
V_LANES = PAIRS * 2 * HD
P_LANES = 3 * V_LANES
ROW_BLOCK = 256
F32 = jnp.float32
BF16 = jnp.bfloat16


def round_up(value, by):
    return -(-value // by) * by


def lane_map_kernel(places, x_ref, o_ref):
    width, wide = x_ref.shape[1], o_ref.shape[1]
    for at in range(0, wide, 128):
        end = min(at + 128, wide)
        column = at + lax.broadcasted_iota(jnp.int32, (128, end - at), 1)
        source = places.of(column)
        total = None
        for low in sorted({p // 128 * 128 for p in (places(j) for j in range(at, end)) if p >= 0}):
            high = min(low + 128, width)
            row = low + lax.broadcasted_iota(jnp.int32, (high - low, end - at), 0)
            chosen = (row == source[: high - low]).astype(BF16)
            term = jnp.dot(x_ref[:, low:high], chosen, preferred_element_type=F32)
            total = term if total is None else total + term
        o_ref[:, at:end] = total.astype(o_ref.dtype)


class Spread:
    def __init__(self, part, part_pad):
        self.part, self.part_pad = part, part_pad

    def __call__(self, j):
        return j // self.part_pad * self.part + j % self.part_pad if j % self.part_pad < self.part else -1

    def of(self, j):
        inside = lax.rem(j, self.part_pad)
        return jnp.where(inside < self.part, lax.div(j, self.part_pad) * self.part + inside, -1)


class Gather:
    def __init__(self, part, part_pad):
        self.part, self.part_pad = part, part_pad

    def __call__(self, j):
        return j // self.part * self.part_pad + j % self.part

    def of(self, j):
        return lax.div(j, self.part) * self.part_pad + lax.rem(j, self.part)


def lane_map(value, places, wide, dtype=BF16):
    shape = value.shape[:-1] + (wide,)
    flat = value.reshape(-1, value.shape[-1])
    rows = flat.shape[0]
    block = rows if rows % 256 else 256
    result = pl.pallas_call(
        functools.partial(lane_map_kernel, places),
        grid=(rows // block,),
        in_specs=[pl.BlockSpec((block, flat.shape[1]), lambda i: (i, 0))],
        out_specs=pl.BlockSpec((block, wide), lambda i: (i, 0)),
        out_shape=jax.ShapeDtypeStruct((rows, wide), dtype),
        compiler_params=pltpu.CompilerParams(vmem_limit_bytes=32 * 2**20),
        cost_estimate=FREE,
        name="lane_map",
    )(flat)
    return result.reshape(shape)


NT = (((1,), (1,)), ((), ()))
TN = (((0,), (0,)), ((), ()))
FREE = pl.CostEstimate(flops=0, bytes_accessed=0, transcendentals=0)


def on_each_part(info_ref, parts, body):
    if parts == 1:
        body(0)
        return
    for part in range(parts):
        pl.when(info_ref[info_ref.shape[0] - 1] == part)(functools.partial(body, part))


def heads_of_pair(body):
    if HL % 2 == 0:
        body((0, 1))
        return
    last = pl.program_id(1) == PAIRS - 1
    pl.when(jnp.logical_not(last))(functools.partial(body, (0, 1)))
    pl.when(last)(functools.partial(body, (0,)))


def attn_fwd_kernel(info_ref, q_ref, k_ref, v_ref, o_ref, lse_ref):
    total, rows = k_ref.shape[0], o_ref.shape[0]
    length = info_ref[pl.program_id(0)]
    block = min(ROW_BLOCK, rows)
    lower = lax.broadcasted_iota(jnp.int32, (block, 2 * HD), 1) < HD
    keep = jnp.where(lax.broadcasted_iota(jnp.int32, (total, 1), 0) < length, 0.0, -1e30)

    def body(heads, half):
        for i in range(rows // block):
            first = half * rows + i * block
            end = first + block
            key = lax.broadcasted_iota(jnp.int32, (end, block), 0)
            query = lax.broadcasted_iota(jnp.int32, (end, block), 1) + first
            probs = []
            for a in heads:
                mine = lower if a == 0 else jnp.logical_not(lower)
                q = jnp.where(mine, q_ref[first:end, :] * jnp.asarray(HD**-0.5, BF16), jnp.zeros((), BF16))
                scores = lax.dot_general(k_ref[:end, :], q, NT, preferred_element_type=F32) + keep[:end]
                scores = jnp.where(key <= query, scores, -1e30)
                top = jnp.max(scores, axis=0, keepdims=True)
                weights = jnp.exp(scores - top)
                below = jnp.sum(weights, axis=0, keepdims=True)
                lse_ref[a : a + 1, i * block : (i + 1) * block] = top + jnp.log(below)
                probs.append((weights * (1.0 / below)).astype(BF16))
            parts = [lax.dot_general(p, v_ref[:end, :], TN, preferred_element_type=F32) for p in probs]
            upper = parts[1] if len(heads) == 2 else jnp.zeros_like(parts[0])
            o_ref[i * block : (i + 1) * block, :] = jnp.where(lower, parts[0], upper).astype(BF16)

    lse_ref[...] = jnp.zeros_like(lse_ref)
    heads_of_pair(lambda heads: on_each_part(info_ref, total // rows, functools.partial(body, heads)))


def pair_spec(rows, lanes, offset=0):
    return pl.BlockSpec((None, rows, lanes), lambda i, j: (i, 0, j + offset))


def stats_spec(rows):
    return pl.BlockSpec((None, None, 2, rows), lambda i, j: (i, j, 0, 0))


def attn_forward(packed, info, rows):
    count, total, _ = packed.shape
    return pl.pallas_call(
        attn_fwd_kernel,
        grid=(count, PAIRS),
        in_specs=[
            pl.BlockSpec(memory_space=pltpu.SMEM),
            pair_spec(total, 2 * HD),
            pair_spec(total, 2 * HD, PAIRS),
            pair_spec(total, 2 * HD, 2 * PAIRS),
        ],
        out_specs=[pair_spec(rows, 2 * HD), stats_spec(rows)],
        out_shape=[
            jax.ShapeDtypeStruct((count, rows, V_LANES), BF16),
            jax.ShapeDtypeStruct((count, PAIRS, 2, rows), F32),
        ],
        compiler_params=pltpu.CompilerParams(vmem_limit_bytes=48 * 2**20),
        cost_estimate=FREE,
        name="attn_fwd",
    )(info, packed, packed, packed)


def attn_bwd_kernel(info_ref, q_ref, k_ref, v_ref, g_ref, o_ref, lse_ref, out_ref):
    total, rows = k_ref.shape[0], g_ref.shape[0]
    block = min(2 * ROW_BLOCK, rows)
    count = total // block
    pair = pl.program_id(1)
    length = info_ref[pl.program_id(0)]
    lane = lax.broadcasted_iota(jnp.int32, (block, 2 * HD), 1)
    key = lax.broadcasted_iota(jnp.int32, (block, block), 0)
    query = lax.broadcasted_iota(jnp.int32, (block, block), 1)
    key_row = lax.broadcasted_iota(jnp.int32, (block, 1), 0)

    def body(heads, half):
        nothing = jnp.zeros((block, 2 * HD), F32)
        dq, dk, dv = {}, {}, {}
        for i in range(rows // block):
            at = slice(i * block, (i + 1) * block)
            place = half * rows // block + i
            g = g_ref[at, :]
            product = g.astype(F32) * o_ref[at, :].astype(F32)
            mine = {}
            for a in heads:
                lanes = (lane < HD) if a == 0 else (lane >= HD)
                inner = lax.dot_general(
                    jnp.ones((8, 2 * HD), F32),
                    jnp.where(lanes, product, 0.0),
                    NT,
                    preferred_element_type=F32,
                    precision=lax.Precision.HIGHEST,
                )[0:1]
                q = q_ref[place * block : (place + 1) * block, :] * jnp.asarray(HD**-0.5, BF16)
                q = jnp.where(lanes, q, jnp.zeros_like(q))
                mine[a] = (q, jnp.where(lanes, g, jnp.zeros_like(g)), inner, lse_ref[a : a + 1, at])
            for j in range(place + 1):
                keys = slice(j * block, (j + 1) * block)
                keep = jnp.where(key_row < length - j * block, 0.0, -1e30)
                for a in heads:
                    q, g_mine, inner, lse = mine[a]
                    k = k_ref[keys, :]
                    scores = lax.dot_general(k, q, NT, preferred_element_type=F32) + keep
                    if j == place:
                        scores = jnp.where(key <= query, scores, -1e30)
                    probs = jnp.exp(scores - lse)
                    gprobs = lax.dot_general(v_ref[keys, :], g_mine, NT, preferred_element_type=F32)
                    gscores = (probs * (gprobs - inner)).astype(BF16)
                    dq[a, place] = dq.get((a, place), 0.0) + lax.dot_general(
                        gscores, k, TN, preferred_element_type=F32
                    )
                    dk[a, j] = dk.get((a, j), 0.0) + jnp.dot(gscores, q, preferred_element_type=F32)
                    dv[j] = dv.get(j, 0.0) + jnp.dot(probs.astype(BF16), g_mine, preferred_element_type=F32)
        for j in range(count):
            at = slice(j * block, (j + 1) * block)
            low, high = heads[0], heads[-1]
            dq_both = jnp.where(lane < HD, dq.get((low, j), nothing), dq.get((high, j), nothing)) * HD**-0.5
            dk_both = jnp.where(lane < HD, dk.get((low, j), nothing), dk.get((high, j), nothing))
            for which, value in enumerate((dq_both, dk_both, dv.get(j, nothing))):
                start = pl.multiple_of(which * V_LANES + pair * 2 * HD, 2 * HD)
                out_ref[at, pl.ds(start, 2 * HD)] = value.astype(BF16)

    heads_of_pair(lambda heads: on_each_part(info_ref, total // rows, functools.partial(body, heads)))


def attn_backward(packed, grad, attended, lse, info):
    (count, total, _), rows = packed.shape, grad.shape[1]
    return pl.pallas_call(
        attn_bwd_kernel,
        grid=(count, PAIRS),
        in_specs=[
            pl.BlockSpec(memory_space=pltpu.SMEM),
            pair_spec(total, 2 * HD),
            pair_spec(total, 2 * HD, PAIRS),
            pair_spec(total, 2 * HD, 2 * PAIRS),
            pair_spec(rows, 2 * HD),
            pair_spec(rows, 2 * HD),
            stats_spec(rows),
        ],
        out_specs=pl.BlockSpec((None, total, P_LANES), lambda i, j: (i, 0, 0)),
        out_shape=jax.ShapeDtypeStruct((count, total, P_LANES), BF16),
        compiler_params=pltpu.CompilerParams(vmem_limit_bytes=56 * 2**20),
        cost_estimate=FREE,
        name="attn_bwd",
    )(info, packed, packed, packed, grad, attended, lse)


PAIR = "x"


def flip(value, axis):
    return lax.ppermute(value, axis, [(0, 1), (1, 0)])


def in_turn(mine, other, mine_at, axis):
    shape = [1] * mine.ndim
    shape[axis] = 2
    place = lax.broadcasted_iota(jnp.int32, tuple(shape), axis)
    return jnp.where(place == mine_at, mine, other)


def pick(value, at, axis=0):
    return lax.dynamic_slice_in_dim(value, at, 1, axis=axis)


def there(*tokens):
    result = None
    for leaf in jax.tree.leaves(tokens):
        first = lax.slice(leaf, (0,) * leaf.ndim, (1,) * leaf.ndim).reshape(())
        result = (first == first) if result is None else result & (first == first)
    return result


def tied(value, *tokens):
    if not jax.tree.leaves(tokens):
        return value
    return value + jnp.where(there(tokens), 0, 1).astype(value.dtype)


def rows_of_both(own):
    count, rows, width = own.shape
    both = in_turn(own[:, None], flip(own, "section")[:, None], lax.axis_index("section"), 1)
    return both.reshape(count, 2 * rows, width)


def chip_rows(partial):
    count, rows, width = partial.shape
    core = lax.axis_index("section")
    split = partial.reshape(count, 2, rows // 2, width)
    other = flip(pick(split, 1 - core, 1)[:, 0], "section")
    return (pick(split, core, 1)[:, 0].astype(F32) + other.astype(F32)).astype(BF16)


class PairSum:
    def __init__(self):
        self.before = ()

    def hold(self, value):
        self.before += (value,)

    def __call__(self, chip):
        arrived = flip(tied(chip, self.before), PAIR)
        self.before = (arrived,)
        return chip.astype(F32) + arrived.astype(F32)


def dot(a, b):
    flat = jnp.dot(a.reshape(-1, a.shape[-1]), b, preferred_element_type=F32)
    return flat.reshape(a.shape[:-1] + (b.shape[1],))


def dot_t(a, b):
    flat = lax.dot_general(a.reshape(-1, a.shape[-1]), b, NT, preferred_element_type=F32)
    return flat.reshape(a.shape[:-1] + (b.shape[0],))


def dot_0(a, b):
    return lax.dot_general(a.reshape(-1, a.shape[-1]), b.reshape(-1, b.shape[-1]), TN, preferred_element_type=F32)


def row_sum(value):
    return jnp.sum(value.astype(F32), axis=(0, 1))


def gelu_parts(u):
    t = jnp.tanh(0.7978845608 * (u + 0.044715 * u * u * u))
    return t


def gelu(u):
    return 0.5 * u * (1.0 + gelu_parts(u))


def gelu_slope(u):
    t = gelu_parts(u)
    return 0.5 * (1.0 + t) + 0.5 * u * (1.0 - t * t) * 0.7978845608 * (1.0 + 3 * 0.044715 * u * u)


def norm_stats(rows, mask, width):
    average = jnp.sum(rows, axis=-1, keepdims=True) / width
    centered = (rows - average) * mask
    variance = jnp.sum(centered * centered, axis=-1, keepdims=True) / width
    scale = lax.rsqrt(variance + 1e-05)
    return centered * scale, scale


def norm_back(grad, rows, gain, mask, width):
    hat, scale = norm_stats(rows, mask, width)
    inner = grad * gain
    mean_one = jnp.sum(inner, axis=-1, keepdims=True) / width
    mean_two = jnp.sum(inner * hat, axis=-1, keepdims=True) / width
    back = scale * (inner - mean_one - hat * mean_two) * mask
    return back, row_sum(grad * hat), row_sum(grad * mask)


def whole_sequence(packed):
    parts = lax.axis_size("y")
    if parts == 2:
        other = lax.ppermute(packed[..., V_LANES:], "y", [(0, 1)])
        other = jnp.pad(other, ((0, 0), (0, 0), (V_LANES, 0)))
        both = in_turn(packed[:, None], other[:, None], lax.axis_index("y"), 1)
    else:
        both = lax.all_gather(packed, "y", axis=1)
    return both.reshape(packed.shape[0], parts * packed.shape[1], packed.shape[2])


def own_rows(grad):
    parts = lax.axis_size("y")
    rows = grad.shape[1] // parts
    if parts != 2:
        return lax.psum_scatter(grad, "y", scatter_dimension=1, tiled=True)
    other = lax.ppermute(grad[:, :rows, V_LANES:], "y", [(1, 0)])
    other = jnp.pad(other, ((0, 0), (0, 0), (V_LANES, 0)))
    own = lax.dynamic_slice_in_dim(grad, lax.axis_index("y") * rows, rows, axis=1)
    return (own.astype(F32) + other.astype(F32)).astype(BF16)


def project_stage(rows, w, mask, width):
    hat, _ = norm_stats(rows.astype(F32), mask, width)
    normed = rows_of_both((hat * w["gain_one"] + w["shift_one"]).astype(BF16))
    packed = (dot(normed, w["qkv"]) + w["qkv_bias"]).astype(BF16)
    return normed, whole_sequence(packed)


def attend_stage(normed, packed, w, info):
    attended, lse = attn_forward(packed, info, normed.shape[1])
    return dot(attended, w["out"]).astype(BF16), (normed, packed, attended, lse)


def ffn_stage(middle, w, mask, width):
    hat, _ = norm_stats(middle, mask, width)
    normed = rows_of_both((hat * w["gain_two"] + w["shift_two"]).astype(BF16))
    upward = dot(normed, w["up"]) + w["up_bias"]
    hidden = gelu(upward).astype(BF16)
    partial = dot(hidden, w["down"]).astype(BF16)
    return partial, (normed, upward.astype(BF16), hidden)


def ffn_back_stage(grad_out, kept, w, token=()):
    normed, upward, hidden = kept
    grad_down = tied(grad_out.astype(BF16), token)
    b_down = row_sum(grad_down)
    grad_down = rows_of_both(grad_down)
    grad_up = (dot_t(grad_down, w["down"]) * gelu_slope(upward.astype(F32))).astype(BF16)
    b_up = row_sum(grad_up)
    partial = dot_t(grad_up, w["up"]).astype(BF16)
    return partial, {"down_bias": b_down, "up_bias": b_up}, {"down": (hidden, grad_down), "up": (normed, grad_up)}


def branch_stage(grad_middle, kept, token=()):
    grad_branch = tied(grad_middle.astype(BF16), token)
    return rows_of_both(grad_branch), {"out_bias": row_sum(grad_branch)}


def attend_back_stage(grad_branch, kept, w, info):
    normed, packed, attended, lse = kept
    grad_attended = dot_t(grad_branch, w["out"]).astype(BF16)
    return attn_backward(packed, grad_attended, attended, lse, info)


def project_back_stage(grad_packed, kept, w):
    grad_packed = own_rows(grad_packed)
    b_packed = row_sum(grad_packed)
    partial = dot_t(grad_packed, w["qkv"]).astype(BF16)
    return partial, {"packed": b_packed}, {"qkv": (kept[0], grad_packed)}


SMALL = ("b_qv", "out_bias", "up_bias", "down_bias", "gain_one", "shift_one", "gain_two", "shift_two")


def per_device(
    inputs,
    cotangent,
    lengths,
    dealing,
    query_key_value_weight,
    b_qv,
    attention_out_weight,
    attention_out_bias,
    up_weight,
    up_bias,
    down_weight,
    down_bias,
    gain_one,
    shift_one,
    gain_two,
    shift_two,
):
    micro, block_rows, width = inputs.shape
    dp_count, y_count = lax.axis_size("dp"), lax.axis_size("y")
    chips = 2 * dp_count * y_count
    all_groups = dp_count * y_count
    core, dp_index = lax.axis_index("section"), lax.axis_index("dp")
    x_index, y_index = lax.axis_index("x"), lax.axis_index("y")
    quarter = 2 * x_index + core
    part = query_key_value_weight.shape[1]
    part_pad = round_up(part + 1, 8)
    width_pad = chips * part_pad
    hid = down_weight.shape[1] // 2
    hid_pad = round_up(hid, 8)
    while all_groups * hid_pad % 128:
        hid_pad += 8

    lane = lax.broadcasted_iota(jnp.int32, (1, width_pad), 1)
    mask = (lane % part_pad < part).astype(F32)
    local = lax.broadcasted_iota(jnp.int32, (V_LANES, width_pad), 0)
    column = lax.broadcasted_iota(jnp.int32, (V_LANES, width_pad), 1)
    whole_row = local + quarter * HSTEP * HD
    own_local = (local < HL * HD) & ((local >= HD) | (quarter == 0))
    placed = ((column == whole_row // part * part_pad + whole_row % part) & own_local).astype(BF16)
    side = round_up(width_pad // 2, 128)
    far = width_pad - side

    def widen(value):
        return lane_map(value, Spread(part, part_pad), width_pad)

    def narrow(value, dtype=BF16):
        return lane_map(value.astype(BF16), Gather(part, part_pad), width, dtype)

    def pad_rows(value, rows):
        return jnp.pad(value, ((0, rows - value.shape[0]), (0, 0)))

    small_in = dict(
        zip(SMALL, (b_qv, attention_out_bias, up_bias, down_bias, gain_one, shift_one, gain_two, shift_two))
    )
    small_sizes = {name: value.shape[1] for name, value in small_in.items()}
    small_row = jnp.concatenate([small_in[name][0] for name in SMALL])
    small_total = small_row.shape[0]

    shard = query_key_value_weight[0].reshape(part, 3, H, HD)

    out_wide = pad_rows(widen(attention_out_weight[0]), part_pad)
    out_pieces = jnp.stack([jnp.stack([out_wide[:, at : at + side]] * 2) for at in (0, far)])

    def attn_piece(q):
        from_head = HSTEP * q
        heads = shard[:, :, from_head : from_head + HL]
        body = jnp.pad(heads.reshape(part, 3, HL * HD), ((0, 0), (0, 0), (0, V_LANES - HL * HD)))
        body = body.reshape(part, P_LANES)
        row = jnp.pad(small_row, (0, P_LANES - small_total))[None]
        return pad_rows(jnp.concatenate([body, row], axis=0), part_pad)

    up_shard = up_weight[0].reshape(part, all_groups, 2, 2, hid)

    def up_piece(q):
        body = up_shard[:, :, q // 2, q % 2]
        body = jnp.pad(body, ((0, 0), (0, 0), (0, hid_pad - hid))).reshape(part, all_groups * hid_pad)
        return pad_rows(body, part_pad)

    attn_pieces = jnp.stack([jnp.stack([attn_piece(2 * x + c) for x in range(2)]) for c in range(2)])
    up_pieces = jnp.stack([jnp.stack([up_piece(2 * x + c) for x in range(2)]) for c in range(2)])
    down_wide = widen(down_weight[0]).reshape(2, hid, width_pad)
    down_pieces = jnp.pad(down_wide, ((0, 0), (0, hid_pad - hid), (0, 0)))

    def by_layer(pieces):
        mine, other = pick(pieces, core)[0], flip(pick(pieces, 1 - core)[0], "section")
        return [jnp.where(core == 0, mine, other), jnp.where(core == 0, other, mine)]

    def across_pair(pieces):
        both = in_turn(pick(pieces, x_index), flip(pick(pieces, 1 - x_index), PAIR), x_index, 0)
        return both.reshape(2 * part_pad, both.shape[-1])

    groups = ("dp", "y")
    down_l = by_layer(down_pieces)
    attn_l = [across_pair(pieces) for pieces in by_layer(jnp.concatenate([attn_pieces, out_pieces], axis=-1))]
    up_l = [across_pair(pieces) for pieces in by_layer(up_pieces)]
    def gather(piece, *tokens):
        return lax.all_gather(tied(piece, tokens), groups, axis=0)

    down_first, attn_first = gather(down_l[0]), gather(attn_l[0])
    up_first = gather(up_l[0], down_first)
    weights = []

    def layer_of(attn_all, up_all, down_all):
        if attn_all is None:
            return {"down": down_all.reshape(all_groups * hid_pad, width_pad)}
        attn_all = attn_all.reshape(width_pad, P_LANES + side)
        qkv_all, out_all = attn_all[:, :P_LANES], attn_all[:, P_LANES:]
        small_all = qkv_all.reshape(chips, part_pad, P_LANES)[:, part, :small_total]
        pieces, at = {}, 0
        for name in SMALL:
            pieces[name] = small_all[:, at : at + small_sizes[name]]
            at += small_sizes[name]

        def feature(name):
            return jnp.pad(pieces[name].astype(F32), ((0, 0), (0, part_pad - part))).reshape(1, width_pad)

        qv = pieces["b_qv"].astype(F32).reshape(2, H * HD)
        own_qv = lax.dynamic_slice_in_dim(qv, quarter * HSTEP * HD, HL * HD, axis=1)
        own_qv = jnp.pad(own_qv, ((0, 0), (0, V_LANES - HL * HD)))
        qkv_bias = jnp.concatenate([own_qv[0], jnp.zeros((V_LANES,), F32), own_qv[1]])[None]
        ups = pieces["up_bias"].astype(F32).reshape(all_groups, 2, 2, hid)
        up_mine = lax.dynamic_index_in_dim(
            lax.dynamic_index_in_dim(ups, x_index, 1, keepdims=False), core, 1, keepdims=False
        )
        up_bias_row = jnp.pad(up_mine, ((0, 0), (0, hid_pad - hid))).reshape(1, all_groups * hid_pad)
        sides = in_turn(out_all[None], flip(out_all, "section")[None], core, 0)
        out_both = jnp.concatenate([sides[0], sides[1, :, side - far :]], axis=1)
        out_mine = dot(placed, out_both).astype(BF16)
        return {
                "qkv": qkv_all.reshape(width_pad, P_LANES),
                "qkv_bias": qkv_bias,
                "out": out_mine,
                "out_bias": feature("out_bias"),
                "up": up_all.reshape(width_pad, all_groups * hid_pad),
                "up_bias": up_bias_row,
                "down": None if down_all is None else down_all.reshape(all_groups * hid_pad, width_pad),
                "down_bias": feature("down_bias"),
                "gain_one": feature("gain_one"),
                "shift_one": feature("shift_one"),
                "gain_two": feature("gain_two"),
                "shift_two": feature("shift_two"),
        }

    rounds = [range(0, micro - micro // 2), range(micro - micro // 2, micro)]
    turns = range(len(rounds))
    CORE_X = ("section", "x")

    def to_rounds(value):
        rows = jnp.where(core == x_index, value, lax.ppermute(value, CORE_X, [(0, 1), (3, 2)]))
        rows = widen(rows)
        return [rows[r.start : r.stop] for r in rounds]

    def to_blocks(value, layer):
        rows = narrow(jnp.concatenate(value, axis=0))
        pairs = [(0, 2 * layer), (3, 2 * layer + 1), (1, 2 - 2 * layer), (2, 3 - 2 * layer)]
        return lax.ppermute(rows, CORE_X, pairs)

    own_lengths = lax.dynamic_slice_in_dim(lengths, dp_index * micro, micro)
    positions = (2 * y_index + core) * block_rows + jnp.arange(block_rows, dtype=jnp.int32)
    turn_info = [jnp.concatenate([own_lengths[r.start : r.stop], y_index[None].astype(jnp.int32)]) for r in rounds]

    start_rows = to_rounds(inputs)
    grad_rows = to_rounds(tied(cotangent, up_first))

    kept_attn = [[None] * len(rounds) for _ in range(2)]
    kept_ffn = [[None] * len(rounds) for _ in range(2)]
    middles = [[None] * len(rounds) for _ in range(2)]
    entering = [start_rows, None]
    pair_sum = PairSum()
    outputs = [None, None]
    layers = [layer_of(attn_first, up_first, down_first), None]
    for l in range(2):
        w = layers[l]
        partials, chip = [None] * len(rounds), [None] * len(rounds)
        projected = [None] * len(rounds)
        for turn in reversed(turns):
            projected[turn] = project_stage(entering[l][turn], w, mask, width)
        if l == 0:
            attn_second = gather(attn_l[1], projected[0][1], up_first)
        else:
            weights.append(gather(down_l[1], projected[0][1]))
            layers[1].update(layer_of(None, None, weights[-1]))
        for turn in turns:
            partials[turn], kept_attn[l][turn] = attend_stage(*projected[turn], w, turn_info[turn])
        for turn in turns:
            middles[l][turn] = entering[l][turn].astype(F32) + pair_sum(chip_rows(partials[turn])) + w["out_bias"]
            partials[turn], kept_ffn[l][turn] = ffn_stage(middles[l][turn], w, mask, width)
            if l == 0 and turn == 0:
                up_second = gather(up_l[1], partials[turn])
                layers[1] = layer_of(attn_second, up_second, None)
        outputs[l] = [
            (middles[l][turn] + pair_sum(chip_rows(partials[turn])) + w["down_bias"]).astype(BF16) for turn in turns
        ]
        if l == 0:
            entering[1] = outputs[0]

    def deal(token):
        acts_local = [to_blocks(outputs[l], l) for l in range(2)]
        acts_local = jnp.where(core == 0, acts_local[0], acts_local[1])
        total_seqs = dealing.shape[0]
        numbers = jnp.arange(total_seqs, dtype=jnp.int32)
        position = jnp.sum(jnp.where(dealing[:, None] == numbers[None, :], numbers[:, None], 0), axis=0)
        target = lax.dynamic_slice_in_dim(position, dp_index * micro, micro) // micro
        anchor = lax.dynamic_slice_in_dim(dealing, dp_index * micro, micro) // micro
        dealt = []
        for d in range(dp_count):
            dest = dp_index ^ d
            send = acts_local[0]
            for i in range(1, micro):
                send = jnp.where(target[i] == dest, acts_local[i], send)
            send = tied(send, token)
            if d:
                send = lax.ppermute(send, "dp", [(i, i ^ d) for i in range(dp_count)])
            dealt.append(send)
        result = []
        for j in range(micro):
            offset = anchor[j] ^ dp_index
            chosen = dealt[0]
            for d in range(1, dp_count):
                chosen = jnp.where(offset == d, dealt[d], chosen)
            result.append(chosen)
        return jnp.stack(result)

    def total(values):
        return functools.reduce(jnp.add, values)

    def product(operands):
        return total([dot_0(a, b) for a, b in operands]).astype(BF16)

    once = (x_index == 0).astype(F32)
    valid = [positions[None] < own_lengths[r.start : r.stop, None] for r in rounds]
    grads = [jnp.where(valid[turn][..., None], grad_rows[turn].astype(F32), 0.0) for turn in turns]

    def scattered(value, rows):
        value = value.reshape(all_groups, rows, value.shape[-1])
        return lax.psum_scatter(value, groups, scatter_dimension=0, tiled=False)

    finished = [None, None]
    token = ()
    sent_back = [None, None]
    for l in (1, 0):
        w = layers[l]
        smalls, operands, partials = [{} for _ in turns], [{} for _ in turns], [None] * len(rounds)
        for turn in turns:
            partials[turn], small, ops = ffn_back_stage(grads[turn], kept_ffn[l][turn], w, token)
            smalls[turn].update(small)
            operands[turn].update(ops)
        d_down = product([ops["down"] for ops in operands])
        d_up = product([ops["up"] for ops in operands])
        token = (d_down, d_up)
        down_done = scattered(d_down, hid_pad)
        up_done = scattered(d_up, 2 * part_pad)
        grad_middles = [None] * len(rounds)
        for turn in turns:
            if l == 0 and turn == 1:
                pair_sum.hold(finished[1]["up"])
            back, gain, shift = norm_back(
                pair_sum(chip_rows(partials[turn])), middles[l][turn], w["gain_two"], mask, width
            )
            smalls[turn].update({"gain_two": gain, "shift_two": shift})
            grad_middles[turn] = grads[turn] + back
        branches = [None] * len(rounds)
        for turn in turns:
            branches[turn], small = branch_stage(grad_middles[turn], kept_attn[l][turn], token)
            smalls[turn].update(small)
            operands[turn]["out"] = (kept_attn[l][turn][2], branches[turn])
        if l == 0:
            acts = deal(tuple(branches))
        d_out = dot_0(placed, product([ops["out"] for ops in operands])).astype(BF16)
        out_own = lax.dynamic_slice_in_dim(d_out, core * far, side, axis=1)
        out_other = flip(lax.dynamic_slice_in_dim(d_out, (1 - core) * far, side, axis=1), "section")
        d_out = (out_own.astype(F32) + out_other.astype(F32)).astype(BF16)
        out_done = scattered(d_out, 2 * part_pad)
        grad_packed, before = [None] * len(rounds), ()
        for turn in reversed(turns):
            grad_packed[turn] = attend_back_stage(
                branches[turn], kept_attn[l][turn], w, turn_info[turn] + jnp.where(there(before), 0, 1)
                if before
                else turn_info[turn]
            )
            before = (grad_packed[turn],)
        for turn in turns:
            partials[turn], small, ops = project_back_stage(grad_packed[turn], kept_attn[l][turn], w)
            smalls[turn].update(small)
            operands[turn].update(ops)
        d_qkv = product([ops["qkv"] for ops in operands])
        token = (d_qkv, out_done)
        returned = []
        for turn in turns:
            if l == 1 and turn == 1:
                pair_sum.hold(down_done)
            if l == 0 and turn == 1:
                pair_sum.hold((acts, finished[1]["qkv"]))
            back, gain, shift = norm_back(
                pair_sum(chip_rows(partials[turn])), entering[l][turn].astype(F32), w["gain_one"], mask, width
            )
            smalls[turn].update({"gain_one": gain, "shift_one": shift})
            returned.append((grad_middles[turn] + back).astype(BF16))
        sent_back[l] = returned
        if l == 1:
            grads = [r.astype(F32) for r in returned]
        sums = {name: total([small[name] for small in smalls]) for name in smalls[0]}

        def feature_sum(name):
            return sums[name].reshape(chips, part_pad)[:, :part] * once

        own_head = (jnp.arange(HL * HD) >= HD) | (quarter == 0)
        q_sum = sums["packed"][: HL * HD]
        v_sum = sums["packed"][2 * V_LANES : 2 * V_LANES + HL * HD]
        qv_sum = jnp.stack(
            [
                lax.dynamic_update_slice_in_dim(
                    jnp.zeros((H * HD,), F32), jnp.where(own_head, s, 0.0), quarter * HSTEP * HD, axis=0
                )
                for s in (q_sum, v_sum)
            ]
        ).reshape(chips, -1)
        up_sum = sums["up_bias"].reshape(all_groups, 1, 1, hid_pad)[..., :hid]
        at_x = jnp.arange(2)[None, :, None, None] == x_index
        at_c = jnp.arange(2)[None, None, :, None] == core
        up_sum = jnp.where(at_x & at_c, up_sum, 0.0).reshape(chips, -1)
        small_cols = jnp.concatenate(
            [qv_sum, feature_sum("out_bias"), up_sum]
            + [feature_sum(name) for name in ("down_bias", "gain_one", "shift_one", "gain_two", "shift_two")],
            axis=1,
        ).astype(BF16)
        small_cols = jnp.pad(small_cols, ((0, 0), (0, P_LANES - small_total)))[:, None, :]
        d_qkv = d_qkv.reshape(chips, part_pad, P_LANES)
        at_row = lax.broadcasted_iota(jnp.int32, (1, part_pad, 1), 1) == part
        d_qkv = jnp.where(at_row, small_cols, d_qkv)
        qkv_done = scattered(d_qkv, 2 * part_pad)
        finished[l] = {"up": up_done, "down": down_done, "qkv": qkv_done, "out": out_done}

    def back_across_pair(value):
        value = value.reshape(2, part_pad, value.shape[-1])
        return in_turn(pick(value, x_index), flip(pick(value, 1 - x_index), PAIR), x_index, 0)

    def own_layer(first, second):
        mine = jnp.where(core == 0, first, second)
        other = flip(jnp.where(core == 0, second, first), "section")
        return [jnp.where(core == 0, mine, other), jnp.where(core == 0, other, mine)]

    up_c = own_layer(*[back_across_pair(finished[l]["up"]) for l in range(2)])
    down_c = own_layer(*[finished[l]["down"].reshape(hid_pad, width_pad) for l in range(2)])
    qkv_c = own_layer(*[back_across_pair(finished[l]["qkv"]) for l in range(2)])
    out_c = own_layer(
        *[jnp.sum(back_across_pair(finished[l]["out"]).astype(F32), axis=0).astype(BF16) for l in range(2)]
    )

    def heads_sum(lanes_of):
        parts = []
        for x in range(2):
            for c in range(2):
                q = 2 * x + c
                piece = lanes_of(qkv_c[c][x, :part].astype(F32))
                own = jnp.arange(HL * HD) >= (0 if q == 0 else HD)
                piece = jnp.where(own[None], piece, 0.0)
                parts.append(jnp.pad(piece, ((0, 0), (HSTEP * q * HD, (H - HL - HSTEP * q) * HD))))
        return total(parts)

    def third(which):
        return lambda piece: piece[:, which * V_LANES : which * V_LANES + HL * HD]

    grad_w_qkv = jnp.concatenate([heads_sum(third(which)) for which in range(3)], axis=1)
    grad_w_out = narrow(jnp.concatenate([out_c[0], out_c[1][:, side - far :]], axis=1), F32)[:part]
    up_parts = jnp.stack(
        [
            jnp.stack(
                [
                    up_c[c][x, :part].reshape(part, all_groups, hid_pad)[..., :hid] for c in range(2)
                ],
                axis=2,
            )
            for x in range(2)
        ],
        axis=2,
    )
    grad_w_up = up_parts.astype(F32).reshape(part, -1)
    grad_w_down = narrow(jnp.concatenate([down_c[0][:hid], down_c[1][:hid]], axis=0), F32)
    small_sum = total([qkv_c[c][x, part, :small_total].astype(F32) for x in range(2) for c in range(2)])
    small_out, at = {}, 0
    for name in SMALL:
        small_out[name] = small_sum[at : at + small_sizes[name]]
        at += small_sizes[name]

    grads_local = [to_blocks(sent_back[l], l) for l in range(2)]
    input_grad = jnp.where(core == 0, grads_local[0], grads_local[1])
    return (
        acts[None],
        input_grad[None],
        grad_w_qkv[None],
        small_out["b_qv"][None],
        grad_w_out[None],
        small_out["out_bias"][None],
        grad_w_up[None],
        small_out["up_bias"][None],
        grad_w_down[None],
        small_out["down_bias"][None],
        small_out["gain_one"][None],
        small_out["shift_one"][None],
        small_out["gain_two"][None],
        small_out["shift_two"][None],
    )


def solution(mesh):
    sections, groups, positions = (mesh.shape[name] for name in ("section", "dp", "seq"))
    devices = mesh.devices.reshape(sections, groups, positions // 2, 2)
    split = jax.sharding.Mesh(devices, ("section", "dp", "y", "x"))
    seq = ("y", "x")
    wide = P("section", ("dp",) + seq, None)
    thin = P("section", ("dp",) + seq)
    rows = P("dp", seq, None)
    in_specs = (rows, rows, P(), P()) + (wide, thin) * 4 + (thin,) * 4
    out_specs = (P("section", "dp", seq, None),) * 2 + (wide, thin) * 4 + (thin,) * 4
    return jax.shard_map(per_device, mesh=split, in_specs=in_specs, out_specs=out_specs, check_vma=False)
```

time: 2550 us -> 2140 us (0.84)
  other arithmetic: 506 us -> 277 us
  matrix products: 478 us -> 354 us
  starting transfers between devices: 208 us -> 151 us
  between operations: 14.7 us -> 71.7 us
  Pallas kernels: 175 us -> 123 us
    ppermute x137 -> x86, waiting for transfers between devices: 905 us -> 625 us  [the longest x69 312 us: flip(): return lax.ppermute(value, axis, [(0, 1), (1, 0)])]
    all_gather x0 -> x6, waiting for transfers between devices: none -> 273 us  [gather(): return lax.all_gather(tied(piece, tokens), groups, axis=0)]
    select_n x119 -> x38, other arithmetic: 213 us -> 83.9 us  [the longest x26 69.8 us: in_turn(): return jnp.where(place == mine_at, mine, other)]
    dot_general x62 -> x50, matrix products: 478 us -> 354 us  [the longest x16 140 us: dot_0(): lax.dot_general(a.reshape(-1, a.shape[-1]), b.reshape(-1, b.shape[-1]), T...]
    ppermute x137 -> x86, starting transfers between devices: 208 us -> 148 us  [the longest x69 88.7 us: flip(): return lax.ppermute(value, axis, [(0, 1), (1, 0)])]
    convert_element_type x46 -> x16, other arithmetic: 94 us -> 35.7 us  [the longest x2 9.81 us: per_device(): returned.append((grad_middles[turn] + back).astype(BF16))]
    slice x24 -> x60, local copies, waits for them, and re-layouts: 6.02 us -> 59.9 us  [the longest x35 31.6 us: there(): first = lax.slice(leaf, (0,) * leaf.ndim, (1,) * leaf.ndim).reshape(())]
    pallas_call x8 -> x18, Pallas kernels: 175 us -> 123 us  [the longest x4 71.3 us: attn_backward(): pl.pallas_call(attn_bwd_kernel, grid=(count, PAIRS), in_specs=[pl.BlockSp...]
  transfers between devices with their start and end apart: 137 -> 100, of which waited for: 45 -> 40; matrix products, arithmetic and copies ran while one was open for 45% -> 39% of each run, Pallas kernels for 7% -> 6%
where the time goes in v2:
time: 2140 us; the launch traced here: 2130 us
  waiting for transfers between devices  916 us (43%)
  matrix products  354 us (17%)
  other arithmetic  277 us (13%)
  local copies, waits for them, and re-layouts  238 us (11%)
  starting transfers between devices  151 us (7%)
  Pallas kernels  123 us (6%)
  between operations  71.7 us (3%)
    ppermute x69, waiting for transfers between devices, flip(): return lax.ppermute(value, axis, [(0, 1), (1, 0)])  312 us
    all_gather x6, waiting for transfers between devices, gather(): return lax.all_gather(tied(piece, tokens), groups, axis=0)  273 us
    ppermute x4, waiting for transfers between devices, whole_sequence(): other = lax.ppermute(packed[..., V_LANES:], 'y', [(0, 1)])  147 us
    dot_general x16, matrix products, dot_0(): lax.dot_general(a.reshape(-1, a.shape[-1]), b.reshape(-1, b.shape[-1]), T...  140 us
    dot_general x18, matrix products, dot(): flat = jnp.dot(a.reshape(-1, a.shape[-1]), b, preferred_element_type=F32)  109 us
    dot_general x16, matrix products, dot_t(): lax.dot_general(a.reshape(-1, a.shape[-1]), b, NT, preferred_element_type...  104 us
    ppermute x4, waiting for transfers between devices, own_rows(): other = lax.ppermute(grad[:, :rows, V_LANES:], 'y', [(1, 0)])  93.8 us
    ppermute x69, starting transfers between devices, flip(): return lax.ppermute(value, axis, [(0, 1), (1, 0)])  88.7 us
  transfers between devices with their start and end apart: 100, of which 40 were waited for; matrix products, arithmetic and copies ran while one was open for 39% of the time, Pallas kernels for 6%

profile of v2, /device:TPU:1, one launch (start us, length us, event | category | flops | bytes accessed | tf_op | source)
XLA Modules:
  0.0 2130.6 jit_solution(5291979780945360637)
XLA Ops:
  27.0 11.0 collective-permute-done.2
  57.6 47.2 %all-gather.17.cloned.1.call-done = bf16[1664,1664]{1,0:T(8,128)(2,1)} async-done(((bf16[208,1664]{1,0:T(8,128)(2,1)}), bf16[1664,1664]{1,0:T(8,128)(2,1)}) %all-gather.17.cloned.1.call-update) | async-done | bytes 5537808 | tf_op jit(solution)/shard_map/all_gather | solution.py:531
  118.9 108.4 %all-gather.9.cloned.1.call-done = bf16[8,208,2432]{2,1,0:T(8,128)(2,1)} async-done(((bf16[1,208,2432]{2,1,0:T(8,128)(2,1)}), bf16[8,208,2432]{2,1,0:T(8,128)(2,1)}) %all-gather.9.cloned.1.call-update) | async-done | bytes 8093712 | tf_op jit(solution)/shard_map/all_gather | solution.py:531
  239.8 7.8 add_convert_fusion.11
  256.6 71.1 %collective-permute-done.4 = bf16[2,512,1024]{2,1,0:T(8,128)(2,1)} collective-permute-done((bf16[2,512,1024]{2,1,0:T(8,128)(2,1)}, bf16[2,512,1024]{2,1,0:T(8,128)(2,1)}, u32[]{:S(2)}, u32[]{:S(2)}) %collective-permute-start.4) | collective-permute-done | bytes 2097184 | tf_op jit(solution)/shard_map/ppermute | solution.py:362
  354.3 117.1 %all-gather.13.cloned.1.call-done = bf16[8,208,2432]{2,1,0:T(8,128)(2,1)} async-done(((bf16[1,208,2432]{2,1,0:T(8,128)(2,1)}), bf16[8,208,2432]{2,1,0:T(8,128)(2,1)}) %all-gather.13.cloned.1.call-update) | async-done | bytes 8093712 | tf_op jit(solution)/shard_map/all_gather | solution.py:531
  494.6 11.3 attn_fwd.4
  509.5 8.1 broadcast_select_fusion
  568.1 15.8 collective-permute-done.7
  599.3 17.8 collective-permute-done.16
  621.9 13.0 fusion.4
  660.3 26.0 %collective-permute-done.17 = bf16[2,256,1664]{2,1,0:T(8,128)(2,1)S(1)} collective-permute-done((bf16[2,256,1664]{2,1,0:T(8,128)(2,1)S(1)}, bf16[2,256,1664]{2,1,0:T(8,128)(2,1)S(1)}, u32[]{:S(2)}, u32[]{:S(2)}) %collective-permute-start.17) | collective-permute-done | bytes 1703968 | tf_op jit(solution)/shard_map/ppermute | solution.py:255
  700.8 14.7 collective-permute-done.20
  720.6 7.8 add_convert_fusion.10
  728.8 10.8 collective-permute-start.24
  752.7 60.6 %collective-permute-done.24 = bf16[2,512,1024]{2,1,0:T(8,128)(2,1)S(1)} collective-permute-done((bf16[2,512,1024]{2,1,0:T(8,128)(2,1)S(1)}, bf16[2,512,1024]{2,1,0:T(8,128)(2,1)S(1)}, u32[]{:S(2)}, u32[]{:S(2)}) %collective-permute-start.24) | collective-permute-done | bytes 2097184 | tf_op jit(solution)/shard_map/ppermute | solution.py:362
  819.0 11.6 attn_fwd.6
  842.4 11.3 collective-permute-start.32
  859.8 15.2 collective-permute-done.32
  896.7 18.9 collective-permute-done.27
  924.4 12.4 collective-permute-done.34
  960.4 7.8 fusion.285
  971.9 9.4 fusion.9
  981.3 11.3 add_convert_fusion.3
  996.9 10.3 fusion.65
  1009.1 14.2 convert_reduce_fusion.1
  1023.3 8.8 convolution_convert_fusion.3
  1049.3 23.0 %collective-permute-done.35 = bf16[2,256,1664]{2,1,0:T(8,128)(2,1)S(1)} collective-permute-done((bf16[2,256,1664]{2,1,0:T(8,128)(2,1)S(1)}, bf16[2,256,1664]{2,1,0:T(8,128)(2,1)S(1)}, u32[]{:S(2)}, u32[]{:S(2)}) %collective-permute-start.35) | collective-permute-done | bytes 1703968 | tf_op jit(solution)/shard_map/ppermute | solution.py:255
  1098.3 12.9 add_convert_fusion.2
  1113.1 22.1 %collective-permute-done.43 = bf16[2,256,1664]{2,1,0:T(8,128)(2,1)S(1)} collective-permute-done((bf16[2,256,1664]{2,1,0:T(8,128)(2,1)}, bf16[2,256,1664]{2,1,0:T(8,128)(2,1)S(1)}, u32[]{:S(2)}, u32[]{:S(2)}) %collective-permute-start.43) | collective-permute-done | bytes 1703968 | tf_op jit(solution)/shard_map/ppermute | solution.py:255
  1141.3 15.4 collective-permute-done.46
  1181.5 11.0 convolution_convert_fusion.1
  1211.9 13.0 attn_bwd.4
  1233.6 22.7 %attn_bwd.5 = bf16[2,1024,1536]{2,1,0:T(8,128)(2,1)} custom-call(s32[3]{0:T(128)} %broadcast_add_fusion.20.info_ref, bf16[2,1024,1536]{2,1,0:T(8,128)(2,1)} %bitcast_select_fusion.q_ref.k_ref.v_ref, bf16[2,1024,1536]{2,1,0:T(8,128)(2,1)} %bitcast_select_fusion.q_ref.k_ref.v_ref, bf16[2,1024,1536]{2,1,0:T(8,128)(2,1)} %bitcast_select_fusion.q_ref.k_ref.v_ref, ...), custom_call_target="tpu_custom_call" | custom-call | tf_op jit(solution)/shard_map/attn_bwd/pallas_call | solution.py:231
  1267.5 68.1 %collective-permute-done.49 = bf16[2,512,1024]{2,1,0:T(8,128)(2,1)} collective-permute-done((bf16[2,512,1024]{2,1,0:T(8,128)(2,1)}, bf16[2,512,1024]{2,1,0:T(8,128)(2,1)}, u32[]{:S(2)}, u32[]{:S(2)}) %collective-permute-start.49) | collective-permute-done | bytes 2097184 | tf_op jit(solution)/shard_map/ppermute | solution.py:375
  1339.3 9.0 fusion.59
  1352.4 20.5 collective-permute-done.52
  1386.7 8.4 add_convert_fusion.5
  1399.8 24.5 %collective-permute-done.51 = bf16[2,256,1664]{2,1,0:T(8,128)(2,1)S(1)} collective-permute-done((bf16[2,256,1664]{2,1,0:T(8,128)(2,1)}, bf16[2,256,1664]{2,1,0:T(8,128)(2,1)S(1)}, u32[]{:S(2)}, u32[]{:S(2)}) %collective-permute-start.51) | collective-permute-done | bytes 1703968 | tf_op jit(solution)/shard_map/ppermute | solution.py:255
  1432.4 14.3 collective-permute-done.57
  1469.1 13.6 convert_reduce_fusion
  1489.0 9.5 fusion.332
  1498.5 11.4 add_convert_fusion
  1550.8 19.6 collective-permute-done.39
  1590.4 10.9 collective-permute-start.74
  1604.5 9.7 convolution_convert_fusion.2
  1623.0 7.9 fusion.288
  1633.3 11.3 collective-permute-start.58
  1644.6 10.5 add_convert_fusion.1
  1659.9 22.2 %collective-permute-done.58 = bf16[2,256,1664]{2,1,0:T(8,128)(2,1)} collective-permute-done((bf16[2,256,1664]{2,1,0:T(8,128)(2,1)}, bf16[2,256,1664]{2,1,0:T(8,128)(2,1)}, u32[]{:S(2)}, u32[]{:S(2)}) %collective-permute-start.58) | collective-permute-done | bytes 1703968 | tf_op jit(solution)/shard_map/ppermute | solution.py:255
  1697.1 8.9 collective-permute-done.62
  1722.8 12.8 attn_bwd.6
  1744.9 22.8 %attn_bwd.7 = bf16[2,1024,1536]{2,1,0:T(8,128)(2,1)} custom-call(s32[3]{0:T(128)} %broadcast_add_fusion.19.info_ref, bf16[2,1024,1536]{2,1,0:T(8,128)(2,1)} %bitcast_select_fusion.1.q_ref.k_ref.v_ref, bf16[2,1024,1536]{2,1,0:T(8,128)(2,1)} %bitcast_select_fusion.1.q_ref.k_ref.v_ref, bf16[2,1024,1536]{2,1,0:T(8,128)(2,1)} %bitcast_select_fusion.1.q_ref.k_ref.v_ref, ...), custom_call_target="tpu_custom_call" | custom-call | tf_op jit(solution)/shard_map/attn_bwd/pallas_call | solution.py:231
  1798.2 10.6 convolution_convert_fusion
  1814.9 23.3 %collective-permute-done.66 = bf16[256,1600]{0,1:T(8,128)(2,1)} collective-permute-done((bf16[256,1600]{0,1:T(8,128)(2,1)}, bf16[256,1600]{0,1:T(8,128)(2,1)}, u32[]{:S(2)}, u32[]{:S(2)}) %collective-permute-start.66) | collective-permute-done | bytes 819232 | tf_op jit(solution)/shard_map/ppermute | solution.py:647
  1843.9 15.0 collective-permute-done.64
  1898.0 8.6 fusion.195
  1912.3 11.1 add_convert_fusion.4
  1926.1 23.6 %collective-permute-done.69 = bf16[2,256,1664]{2,1,0:T(8,128)(2,1)} collective-permute-done((bf16[2,256,1664]{2,1,0:T(8,128)(2,1)}, bf16[2,256,1664]{2,1,0:T(8,128)(2,1)}, u32[]{:S(2)}, u32[]{:S(2)}) %collective-permute-start.69) | collective-permute-done | bytes 1703968 | tf_op jit(solution)/shard_map/ppermute | solution.py:255
  1960.9 13.9 collective-permute-done.72
  2040.0 8.1 reshape.2767
  2048.1 8.7 collective-permute-done.73
  2070.0 10.8 collective-permute-start.81
  2080.8 18.9 reduce-scatter.17.cloned.1.call-done
  (1224 shorter events, 790.6 us)
Async XLA Ops:
  7.2 97.6 %all-gather.17.cloned.1.call-start = ((), (), s32[]{:S(2)}) async-start(), calls=%async_computation.20 | async-start | bytes 6230016 | tf_op jit(solution)/shard_map/all_gather | solution.py:531
  13.4 213.8 %all-gather.9.cloned.1.call-start = ((), (), s32[]{:S(2)}) async-start(), calls=%async_computation.8 | async-start | bytes 9105408 | tf_op jit(solution)/shard_map/all_gather | solution.py:531
  39.4 300.5 %all-gather.11.cloned.1.call-start = ((), (), s32[]{:S(2)}) async-start(), calls=%async_computation.9 | async-start | bytes 6230016 | tf_op jit(solution)/shard_map/all_gather | solution.py:531
  54.8 52.5 %collective-permute-start.10 = (bf16[1,104,1664]{2,1,0:T(8,128)(2,1)S(1)}, bf16[1,104,1664]{2,1,0:T(8,128)(2,1)S(1)}, u32[]{:S(2)}, u32[]{:S(2)}) collective-permute-start(bf16[1,104,1664]{2,1,0:T(8,128)(2,1)S(1)} %get-tuple-element.229), channel_id=1, source_target_pairs={{0,1},{1,0},{2,3},{3,2},{4,5},{5,4},{6,7},{7,6},{8,9},{9,8},{10,11... | collective-permute-start | bytes 1038344 | tf_op jit(solution)/shard_map/ppermute | solution.py:255
  56.3 52.7 %collective-permute-start = (bf16[3,256,1600]{1,2,0:T(8,128)(2,1)S(1)}, bf16[3,256,1600]{1,2,0:T(8,128)(2,1)}, u32[]{:S(2)}, u32[]{:S(2)}) collective-permute-start(bf16[3,256,1600]{1,2,0:T(8,128)(2,1)S(1)} %copy-done.120), channel_id=1, source_target_pairs={{0,1},{17,16},{2,3},{19,18},{4,5},{21,20},{6,7},{23,22},{8,9},{25,... | collective-permute-start | bytes 7372808 | tf_op jit(solution)/shard_map/ppermute | solution.py:583
  108.4 363.0 %all-gather.13.cloned.1.call-start = ((), (), s32[]{:S(2)}) async-start(), calls=%async_computation.10 | async-start | bytes 9105408 | tf_op jit(solution)/shard_map/all_gather | solution.py:531
  251.0 76.8 %collective-permute-start.4 = (bf16[2,512,1024]{2,1,0:T(8,128)(2,1)}, bf16[2,512,1024]{2,1,0:T(8,128)(2,1)}, u32[]{:S(2)}, u32[]{:S(2)}) collective-permute-start(bf16[2,512,1024]{2,1,0:T(8,128)(2,1)} %slice.676), channel_id=1, source_target_pairs={{0,2},{1,3},{4,6},{5,7},{8,10},{9,11},{12,14},{13,15},{16,18},{17,... | collective-permute-start | bytes 6291464 | tf_op jit(solution)/shard_map/ppermute | solution.py:362
  255.3 87.1 %collective-permute-start.22 = (bf16[1,104,2432]{2,1,0:T(8,128)(2,1)}, bf16[1,104,2432]{2,1,0:T(8,128)(2,1)}, u32[]{:S(2)}, u32[]{:S(2)}) collective-permute-start(bf16[1,104,2432]{2,1,0:T(8,128)(2,1)} %get-tuple-element.215), channel_id=1, source_target_pairs={{0,1},{1,0},{2,3},{3,2},{4,5},{5,4},{6,7},{7,6},{8,9},{9,8},{10,11... | collective-permute-start | bytes 1517576 | tf_op jit(solution)/shard_map/ppermute | solution.py:255
  344.8 608.8 %all-gather.15.cloned.1.call-start = ((), (), s32[]{:S(2)}) async-start(), calls=%async_computation.11 | async-start | bytes 6230016 | tf_op jit(solution)/shard_map/all_gather | solution.py:531
  353.1 156.4 %collective-permute-start.5 = (bf16[1664,896]{1,0:T(8,128)(2,1)}, bf16[1664,896]{1,0:T(8,128)(2,1)}, u32[]{:S(2)}, u32[]{:S(2)}) collective-permute-start(bf16[1664,896]{1,0:T(8,128)(2,1)} %slice.677), channel_id=1, source_target_pairs={{0,16},{16,0},{1,17},{17,1},{2,18},{18,2},{3,19},{19,3},{4,20},{20... | collective-permute-start | bytes 8945672 | tf_op jit(solution)/shard_map/ppermute | solution.py:255
  475.1 34.3 %collective-permute-start.25 = (bf16[1664,896]{1,0:T(8,128)(2,1)}, bf16[1664,896]{1,0:T(8,128)(2,1)}, u32[]{:S(2)}, u32[]{:S(2)}) collective-permute-start(bf16[1664,896]{1,0:T(8,128)(2,1)} %slice.703), channel_id=1, source_target_pairs={{0,16},{16,0},{1,17},{17,1},{2,18},{18,2},{3,19},{19,3},{4,20},{20... | collective-permute-start | bytes 8945672 | tf_op jit(solution)/shard_map/ppermute | solution.py:255
  480.2 217.9 %collective-permute-start.29 = (bf16[1,104,1664]{2,1,0:T(8,128)(2,1)}, bf16[1,104,1664]{2,1,0:T(8,128)(2,1)}, u32[]{:S(2)}, u32[]{:S(2)}) collective-permute-start(bf16[1,104,1664]{2,1,0:T(8,128)(2,1)} %get-tuple-element.227), channel_id=1, source_target_pairs={{0,1},{1,0},{2,3},{3,2},{4,5},{5,4},{6,7},{7,6},{8,9},{9,8},{10,11... | collective-permute-start | bytes 1038344 | tf_op jit(solution)/shard_map/ppermute | solution.py:255
  491.3 41.2 %collective-permute-start.14 = (bf16[1,512,1024]{2,1,0:T(8,128)(2,1)}, bf16[1,512,1024]{2,1,0:T(8,128)(2,1)}, u32[]{:S(2)}, u32[]{:S(2)}) collective-permute-start(bf16[1,512,1024]{2,1,0:T(8,128)(2,1)} %slice.690), channel_id=1, source_target_pairs={{0,2},{1,3},{4,6},{5,7},{8,10},{9,11},{12,14},{13,15},{16,18},{17,... | collective-permute-start | bytes 3145736 | tf_op jit(solution)/shard_map/ppermute | solution.py:362
  507.7 37.0 %collective-permute-start.40 = (bf16[3,256,1600]{1,2,0:T(8,128)(2,1)}, bf16[3,256,1600]{1,2,0:T(8,128)(2,1)}, u32[]{:S(2)}, u32[]{:S(2)}) collective-permute-start(bf16[3,256,1600]{1,2,0:T(8,128)(2,1)} %broadcast_add_fusion), channel_id=1, source_target_pairs={{0,1},{17,16},{2,3},{19,18},{4,5},{21,20},{6,7},{23,22},{8,9},{25,... | collective-permute-start | bytes 7372808 | tf_op jit(solution)/shard_map/ppermute | solution.py:583
  544.7 39.2 %collective-permute-start.7 = (bf16[2,256,1664]{2,1,0:T(8,128)(2,1)}, bf16[2,256,1664]{2,1,0:T(8,128)(2,1)}, u32[]{:S(2)}, u32[]{:S(2)}) collective-permute-start(bf16[2,256,1664]{2,1,0:T(8,128)(2,1)} %fusion.125), channel_id=1, source_target_pairs={{0,1},{1,0},{2,3},{3,2},{4,5},{5,4},{6,7},{7,6},{8,9},{9,8},{10,11... | collective-permute-start | bytes 5111816 | tf_op jit(solution)/shard_map/ppermute | solution.py:255
  559.5 188.6 %collective-permute-start.44 = (bf16[1,256,1664]{2,1,0:T(8,128)(2,1)}, bf16[1,256,1664]{2,1,0:T(8,128)(2,1)}, u32[]{:S(2)}, u32[]{:S(2)}) collective-permute-start(bf16[1,256,1664]{2,1,0:T(8,128)(2,1)} %bitcast.172), channel_id=1, source_target_pairs={{0,16},{16,0},{1,17},{17,1},{2,18},{18,2},{3,19},{19,3},{4,20},{20... | collective-permute-start | bytes 2555912 | tf_op jit(solution)/shard_map/ppermute | solution.py:255
  567.6 28.0 %collective-permute-start.15 = (bf16[1,256,1664]{2,1,0:T(8,128)(2,1)}, bf16[1,256,1664]{2,1,0:T(8,128)(2,1)}, u32[]{:S(2)}, u32[]{:S(2)}) collective-permute-start(bf16[1,256,1664]{2,1,0:T(8,128)(2,1)} %dynamic-slice_bitcast_fusion.16), channel_id=1, source_target_pairs={{0,16},{16,0},{1,17},{17,1},{2,18},{18,2},{3,19},{19,3},{4,20},{20... | collective-permute-start | bytes 2555912 | tf_op jit(solution)/shard_map/ppermute | solution.py:255
  648.0 38.3 %collective-permute-start.17 = (bf16[2,256,1664]{2,1,0:T(8,128)(2,1)S(1)}, bf16[2,256,1664]{2,1,0:T(8,128)(2,1)S(1)}, u32[]{:S(2)}, u32[]{:S(2)}) collective-permute-start(bf16[2,256,1664]{2,1,0:T(8,128)(2,1)S(1)} %broadcast_add_fusion.8), channel_id=1, source_target_pairs={{0,1},{1,0},{2,3},{3,2},{4,5},{5,4},{6,7},{7,6},{8,9},{9,8},{10,11... | collective-permute-start | bytes 5111816 | tf_op jit(solution)/shard_map/ppermute | solution.py:255
  659.5 33.8 %collective-permute-start.19 = (bf16[1,256,1664]{2,1,0:T(8,128)(2,1)S(1)}, bf16[1,256,1664]{2,1,0:T(8,128)(2,1)S(1)}, u32[]{:S(2)}, u32[]{:S(2)}) collective-permute-start(bf16[1,256,1664]{2,1,0:T(8,128)(2,1)S(1)} %dynamic-slice_bitcast_fusion.15), channel_id=1, source_target_pairs={{0,16},{16,0},{1,17},{17,1},{2,18},{18,2},{3,19},{19,3},{4,20},{20... | collective-permute-start | bytes 2555912 | tf_op jit(solution)/shard_map/ppermute | solution.py:255
  690.2 27.7 %collective-permute-start.23 = (bf16[2,256,1664]{2,1,0:T(8,128)(2,1)}, bf16[2,256,1664]{2,1,0:T(8,128)(2,1)}, u32[]{:S(2)}, u32[]{:S(2)}) collective-permute-start(bf16[2,256,1664]{2,1,0:T(8,128)(2,1)} %fusion.85), channel_id=1, source_target_pairs={{0,16},{16,0},{1,17},{17,1},{2,18},{18,2},{3,19},{19,3},{4,20},{20... | collective-permute-start | bytes 5111816 | tf_op jit(solution)/shard_map/ppermute | solution.py:255
  700.3 296.6 %all-gather.19.cloned.1.call-start = ((), (), s32[]{:S(2)}) async-start(), calls=%async_computation.21 | async-start | bytes 6230016 | tf_op jit(solution)/shard_map/all_gather | solution.py:531
  728.8 84.6 %collective-permute-start.24 = (bf16[2,512,1024]{2,1,0:T(8,128)(2,1)S(1)}, bf16[2,512,1024]{2,1,0:T(8,128)(2,1)S(1)}, u32[]{:S(2)}, u32[]{:S(2)}) collective-permute-start(bf16[2,512,1024]{2,1,0:T(8,128)(2,1)S(1)} %slice.702), channel_id=1, source_target_pairs={{0,2},{1,3},{4,6},{5,7},{8,10},{9,11},{12,14},{13,15},{16,18},{17,... | collective-permute-start | bytes 6291464 | tf_op jit(solution)/shard_map/ppermute | solution.py:362
  834.1 41.0 %collective-permute-start.26 = (bf16[2,256,1664]{2,1,0:T(8,128)(2,1)}, bf16[2,256,1664]{2,1,0:T(8,128)(2,1)S(1)}, u32[]{:S(2)}, u32[]{:S(2)}) collective-permute-start(bf16[2,256,1664]{2,1,0:T(8,128)(2,1)} %dynamic-slice_bitcast_fusion.5), channel_id=1, source_target_pairs={{0,16},{16,0},{1,17},{17,1},{2,18},{18,2},{3,19},{19,3},{4,20},{20... | collective-permute-start | bytes 5111816 | tf_op jit(solution)/shard_map/ppermute | solution.py:255
  842.4 32.6 %collective-permute-start.32 = (bf16[1,512,1024]{2,1,0:T(8,128)(2,1)}, bf16[1,512,1024]{2,1,0:T(8,128)(2,1)S(1)}, u32[]{:S(2)}, u32[]{:S(2)}) collective-permute-start(bf16[1,512,1024]{2,1,0:T(8,128)(2,1)} %slice.713), channel_id=1, source_target_pairs={{0,2},{1,3},{4,6},{5,7},{8,10},{9,11},{12,14},{13,15},{16,18},{17,... | collective-permute-start | bytes 3145736 | tf_op jit(solution)/shard_map/ppermute | solution.py:362
  855.4 112.9 %collective-permute-start.41 = (bf16[2,256,1664]{2,1,0:T(8,128)(2,1)}, bf16[2,256,1664]{2,1,0:T(8,128)(2,1)}, u32[]{:S(2)}, u32[]{:S(2)}) collective-permute-start(bf16[2,256,1664]{2,1,0:T(8,128)(2,1)} %select_convert_fusion.1), channel_id=1, source_target_pairs={{0,16},{16,0},{1,17},{17,1},{2,18},{18,2},{3,19},{19,3},{4,20},{20... | collective-permute-start | bytes 5111816 | tf_op jit(solution)/shard_map/ppermute | solution.py:255
  878.9 36.7 %collective-permute-start.27 = (bf16[2,256,1664]{2,1,0:T(8,128)(2,1)}, bf16[2,256,1664]{2,1,0:T(8,128)(2,1)}, u32[]{:S(2)}, u32[]{:S(2)}) collective-permute-start(bf16[2,256,1664]{2,1,0:T(8,128)(2,1)} %broadcast_add_fusion.7), channel_id=1, source_target_pairs={{0,1},{1,0},{2,3},{3,2},{4,5},{5,4},{6,7},{7,6},{8,9},{9,8},{10,11... | collective-permute-start | bytes 5111816 | tf_op jit(solution)/shard_map/ppermute | solution.py:255
  889.4 28.7 %collective-permute-start.33 = (bf16[1,256,1664]{2,1,0:T(8,128)(2,1)}, bf16[1,256,1664]{2,1,0:T(8,128)(2,1)}, u32[]{:S(2)}, u32[]{:S(2)}) collective-permute-start(bf16[1,256,1664]{2,1,0:T(8,128)(2,1)} %dynamic-slice_bitcast_fusion.14), channel_id=1, source_target_pairs={{0,16},{16,0},{1,17},{17,1},{2,18},{18,2},{3,19},{19,3},{4,20},{20... | collective-permute-start | bytes 2555912 | tf_op jit(solution)/shard_map/ppermute | solution.py:255
  896.3 366.6 %reduce-scatter.11.cloned.1.call-start = ((), (), s32[]{:S(2)}) async-start(), calls=%async_computation.13 | async-start | bytes 6230016 | tf_op jit(solution)/shard_map/reduce_scatter | solution.py:670
  996.8 451.3 %reduce-scatter.9.cloned.1.call-start = ((), (), s32[]{:S(2)}) async-start(), calls=%async_computation.12 | async-start | bytes 3354624 | tf_op jit(solution)/shard_map/reduce_scatter | solution.py:670
  1032.3 63.8 %collective-permute-start.42 = (bf16[2,256,1664]{2,1,0:T(8,128)(2,1)S(1)}, bf16[2,256,1664]{2,1,0:T(8,128)(2,1)S(1)}, u32[]{:S(2)}, u32[]{:S(2)}) collective-permute-start(bf16[2,256,1664]{2,1,0:T(8,128)(2,1)S(1)} %dynamic-slice_bitcast_fusion.3), channel_id=1, source_target_pairs={{0,16},{16,0},{1,17},{17,1},{2,18},{18,2},{3,19},{19,3},{4,20},{20... | collective-permute-start | bytes 5111816 | tf_op jit(solution)/shard_map/ppermute | solution.py:255
  1033.4 38.9 %collective-permute-start.35 = (bf16[2,256,1664]{2,1,0:T(8,128)(2,1)S(1)}, bf16[2,256,1664]{2,1,0:T(8,128)(2,1)S(1)}, u32[]{:S(2)}, u32[]{:S(2)}) collective-permute-start(bf16[2,256,1664]{2,1,0:T(8,128)(2,1)S(1)} %broadcast_add_fusion.6), channel_id=1, source_target_pairs={{0,1},{1,0},{2,3},{3,2},{4,5},{5,4},{6,7},{7,6},{8,9},{9,8},{10,11... | collective-permute-start | bytes 5111816 | tf_op jit(solution)/shard_map/ppermute | solution.py:255
  1041.0 33.2 %collective-permute-start.37 = (bf16[1,256,1664]{2,1,0:T(8,128)(2,1)S(1)}, bf16[1,256,1664]{2,1,0:T(8,128)(2,1)S(1)}, u32[]{:S(2)}, u32[]{:S(2)}) collective-permute-start(bf16[1,256,1664]{2,1,0:T(8,128)(2,1)S(1)} %dynamic-slice_bitcast_fusion.13), channel_id=1, source_target_pairs={{0,16},{16,0},{1,17},{17,1},{2,18},{18,2},{3,19},{19,3},{4,20},{20... | collective-permute-start | bytes 2555912 | tf_op jit(solution)/shard_map/ppermute | solution.py:255
  1082.6 54.4 %collective-permute-start.45 = (bf16[1,256,1664]{2,1,0:T(8,128)(2,1)}, bf16[1,256,1664]{2,1,0:T(8,128)(2,1)}, u32[]{:S(2)}, u32[]{:S(2)}) collective-permute-start(bf16[1,256,1664]{2,1,0:T(8,128)(2,1)} %dynamic-slice_bitcast_fusion.12), channel_id=1, source_target_pairs={{0,16},{16,0},{1,17},{17,1},{2,18},{18,2},{3,19},{19,3},{4,20},{20... | collective-permute-start | bytes 2555912 | tf_op jit(solution)/shard_map/ppermute | solution.py:255
  1097.9 37.3 %collective-permute-start.43 = (bf16[2,256,1664]{2,1,0:T(8,128)(2,1)}, bf16[2,256,1664]{2,1,0:T(8,128)(2,1)S(1)}, u32[]{:S(2)}, u32[]{:S(2)}) collective-permute-start(bf16[2,256,1664]{2,1,0:T(8,128)(2,1)} %get-tuple-element.175), channel_id=1, source_target_pairs={{0,1},{1,0},{2,3},{3,2},{4,5},{5,4},{6,7},{7,6},{8,9},{9,8},{10,11... | collective-permute-start | bytes 5111816 | tf_op jit(solution)/shard_map/ppermute | solution.py:255
  1207.1 371.3 %reduce-scatter.13.cloned.1.call-start = ((), (), s32[]{:S(2)}) async-start(), calls=%async_computation.14 | async-start | bytes 6230016 | tf_op jit(solution)/shard_map/reduce_scatter | solution.py:670
  1259.5 76.2 %collective-permute-start.49 = (bf16[2,512,1024]{2,1,0:T(8,128)(2,1)}, bf16[2,512,1024]{2,1,0:T(8,128)(2,1)}, u32[]{:S(2)}, u32[]{:S(2)}) collective-permute-start(bf16[2,512,1024]{2,1,0:T(8,128)(2,1)} %slice.728), channel_id=1, source_target_pairs={{2,0},{3,1},{6,4},{7,5},{10,8},{11,9},{14,12},{15,13},{18,16},{19,... | collective-permute-start | bytes 6291464 | tf_op jit(solution)/shard_map/ppermute | solution.py:375
  1262.8 660.7 %reduce-scatter.15.cloned.1.call-start = ((), (), s32[]{:S(2)}) async-start(), calls=%async_computation.15 | async-start | bytes 5750784 | tf_op jit(solution)/shard_map/reduce_scatter | solution.py:670
  1266.2 106.7 %collective-permute-start.52 = (bf16[1,512,1024]{2,1,0:T(8,128)(2,1)S(1)}, bf16[1,512,1024]{2,1,0:T(8,128)(2,1)S(1)}, u32[]{:S(2)}, u32[]{:S(2)}) collective-permute-start(bf16[1,512,1024]{2,1,0:T(8,128)(2,1)S(1)} %slice.730), channel_id=1, source_target_pairs={{2,0},{3,1},{6,4},{7,5},{10,8},{11,9},{14,12},{15,13},{18,16},{19,... | collective-permute-start | bytes 3145736 | tf_op jit(solution)/shard_map/ppermute | solution.py:375
  1348.5 35.5 %collective-permute-start.50 = (bf16[2,256,1664]{2,1,0:T(8,128)(2,1)S(1)}, bf16[2,256,1664]{2,1,0:T(8,128)(2,1)S(1)}, u32[]{:S(2)}, u32[]{:S(2)}) collective-permute-start(bf16[2,256,1664]{2,1,0:T(8,128)(2,1)S(1)} %dynamic-slice_bitcast_fusion.2), channel_id=1, source_target_pairs={{0,16},{16,0},{1,17},{17,1},{2,18},{18,2},{3,19},{19,3},{4,20},{20... | collective-permute-start | bytes 5111816 | tf_op jit(solution)/shard_map/ppermute | solution.py:255
  1377.1 49.1 %collective-permute-start.56 = (bf16[1,256,1664]{2,1,0:T(8,128)(2,1)}, bf16[1,256,1664]{2,1,0:T(8,128)(2,1)}, u32[]{:S(2)}, u32[]{:S(2)}) collective-permute-start(bf16[1,256,1664]{2,1,0:T(8,128)(2,1)} %dynamic-slice_bitcast_fusion.11), channel_id=1, source_target_pairs={{0,16},{16,0},{1,17},{17,1},{2,18},{18,2},{3,19},{19,3},{4,20},{20... | collective-permute-start | bytes 2555912 | tf_op jit(solution)/shard_map/ppermute | solution.py:255
  1386.4 38.0 %collective-permute-start.51 = (bf16[2,256,1664]{2,1,0:T(8,128)(2,1)}, bf16[2,256,1664]{2,1,0:T(8,128)(2,1)S(1)}, u32[]{:S(2)}, u32[]{:S(2)}) collective-permute-start(bf16[2,256,1664]{2,1,0:T(8,128)(2,1)} %get-tuple-element.171), channel_id=1, source_target_pairs={{0,1},{1,0},{2,3},{3,2},{4,5},{5,4},{6,7},{7,6},{8,9},{9,8},{10,11... | collective-permute-start | bytes 5111816 | tf_op jit(solution)/shard_map/ppermute | solution.py:255
  1488.8 513.9 %reduce-scatter.21.cloned.1.call-start = ((), (), s32[]{:S(2)}) async-start(), calls=%async_computation.18 | async-start | bytes 6230016 | tf_op jit(solution)/shard_map/reduce_scatter | solution.py:670
  1509.9 495.3 %reduce-scatter.23.cloned.1.call-start = ((), (), s32[]{:S(2)}) async-start(), calls=%async_computation.19 | async-start | bytes 6230016 | tf_op jit(solution)/shard_map/reduce_scatter | solution.py:670
  1514.8 31.5 %collective-permute-start.21 = (bf16[3,256,1600]{1,2,0:T(8,128)(2,1)}, bf16[3,256,1600]{1,2,0:T(8,128)(2,1)}, u32[]{:S(2)}, u32[]{:S(2)}) collective-permute-start(bf16[3,256,1600]{1,2,0:T(8,128)(2,1)} %copy.128), channel_id=1, source_target_pairs={{0,0},{17,1},{1,16},{16,17},{2,2},{19,3},{3,18},{18,19},{4,4},{21,... | collective-permute-start | bytes 7372808 | tf_op jit(solution)/shard_map/ppermute | solution.py:590
  1526.8 43.6 %collective-permute-start.39 = (bf16[3,256,1600]{1,2,0:T(8,128)(2,1)}, bf16[3,256,1600]{1,2,0:T(8,128)(2,1)}, u32[]{:S(2)}, u32[]{:S(2)}) collective-permute-start(bf16[3,256,1600]{1,2,0:T(8,128)(2,1)} %copy.132), channel_id=1, source_target_pairs={{0,16},{17,17},{1,0},{16,1},{2,18},{19,19},{3,2},{18,3},{4,20},{21... | collective-permute-start | bytes 7372808 | tf_op jit(solution)/shard_map/ppermute | solution.py:590
  1580.4 429.8 %collective-permute-start.83 = (bf16[1,104,1664]{2,1,0:T(8,128)(2,1)}, bf16[1,104,1664]{2,1,0:T(8,128)(2,1)}, u32[]{:S(2)}, u32[]{:S(2)}) collective-permute-start(bf16[1,104,1664]{2,1,0:T(8,128)(2,1)} %get-tuple-element.225), channel_id=1, source_target_pairs={{0,1},{1,0},{2,3},{3,2},{4,5},{5,4},{6,7},{7,6},{8,9},{9,8},{10,11... | collective-permute-start | bytes 1038344 | tf_op jit(solution)/shard_map/ppermute | solution.py:255
  1590.4 121.0 %collective-permute-start.74 = (bf16[3,256,1600]{1,2,0:T(8,128)(2,1)}, bf16[3,256,1600]{1,2,0:T(8,128)(2,1)}, u32[]{:S(2)}, u32[]{:S(2)}) collective-permute-start(bf16[3,256,1600]{1,2,0:T(8,128)(2,1)} %copy.153), channel_id=1, source_target_pairs={{0,16},{17,17},{1,0},{16,1},{2,18},{19,19},{3,2},{18,3},{4,20},{21... | collective-permute-start | bytes 7372808 | tf_op jit(solution)/shard_map/ppermute | solution.py:590
  1623.0 61.6 %collective-permute-start.61 = (bf16[1,256,1664]{2,1,0:T(8,128)(2,1)}, bf16[1,256,1664]{2,1,0:T(8,128)(2,1)}, u32[]{:S(2)}, u32[]{:S(2)}) collective-permute-start(bf16[1,256,1664]{2,1,0:T(8,128)(2,1)} %dynamic-slice_bitcast_fusion.10), channel_id=1, source_target_pairs={{0,16},{16,0},{1,17},{17,1},{2,18},{18,2},{3,19},{19,3},{4,20},{20... | collective-permute-start | bytes 2555912 | tf_op jit(solution)/shard_map/ppermute | solution.py:255
  1633.3 48.8 %collective-permute-start.58 = (bf16[2,256,1664]{2,1,0:T(8,128)(2,1)}, bf16[2,256,1664]{2,1,0:T(8,128)(2,1)}, u32[]{:S(2)}, u32[]{:S(2)}) collective-permute-start(bf16[2,256,1664]{2,1,0:T(8,128)(2,1)} %get-tuple-element.167), channel_id=1, source_target_pairs={{0,1},{1,0},{2,3},{3,2},{4,5},{5,4},{6,7},{7,6},{8,9},{9,8},{10,11... | collective-permute-start | bytes 5111816 | tf_op jit(solution)/shard_map/ppermute | solution.py:255
  1659.9 401.5 %reduce-scatter.19.cloned.1.call-start = ((), (), s32[]{:S(2)}) async-start(), calls=%async_computation.17 | async-start | bytes 3354624 | tf_op jit(solution)/shard_map/reduce_scatter | solution.py:670
  1695.5 42.6 %collective-permute-start.60 = (bf16[2,256,1664]{2,1,0:T(8,128)(2,1)}, bf16[2,256,1664]{2,1,0:T(8,128)(2,1)S(1)}, u32[]{:S(2)}, u32[]{:S(2)}) collective-permute-start(bf16[2,256,1664]{2,1,0:T(8,128)(2,1)} %get-tuple-element.146), channel_id=1, source_target_pairs={{0,16},{16,0},{1,17},{17,1},{2,18},{18,2},{3,19},{19,3},{4,20},{20... | collective-permute-start | bytes 5111816 | tf_op jit(solution)/shard_map/ppermute | solution.py:255
  1770.9 95.7 %collective-permute-start.67 = (bf16[2,512,1024]{2,1,0:T(8,128)(2,1)}, bf16[2,512,1024]{2,1,0:T(8,128)(2,1)}, u32[]{:S(2)}, u32[]{:S(2)}) collective-permute-start(bf16[2,512,1024]{2,1,0:T(8,128)(2,1)} %slice.745), channel_id=1, source_target_pairs={{2,0},{3,1},{6,4},{7,5},{10,8},{11,9},{14,12},{15,13},{18,16},{19,... | collective-permute-start | bytes 6291464 | tf_op jit(solution)/shard_map/ppermute | solution.py:375
  1780.4 57.9 %collective-permute-start.66 = (bf16[256,1600]{0,1:T(8,128)(2,1)}, bf16[256,1600]{0,1:T(8,128)(2,1)}, u32[]{:S(2)}, u32[]{:S(2)}) collective-permute-start(bf16[256,1600]{0,1:T(8,128)(2,1)} %copy.141), channel_id=1, source_target_pairs={{0,4},{4,0},{8,12},{12,8},{1,5},{5,1},{9,13},{13,9},{2,6},{6,2},{1... | collective-permute-start | bytes 2457608 | tf_op jit(solution)/shard_map/ppermute | solution.py:647
  1782.6 58.3 %collective-permute-start.65 = (bf16[256,1600]{0,1:T(8,128)(2,1)}, bf16[256,1600]{0,1:T(8,128)(2,1)}, u32[]{:S(2)}, u32[]{:S(2)}) collective-permute-start(bf16[256,1600]{0,1:T(8,128)(2,1)} %copy.140), channel_id=1, source_target_pairs={{0,8},{4,12},{8,0},{12,4},{1,9},{5,13},{9,1},{13,5},{2,10},{6,14},... | collective-permute-start | bytes 2457608 | tf_op jit(solution)/shard_map/ppermute | solution.py:647
  1785.0 73.9 %collective-permute-start.64 = (bf16[256,1600]{0,1:T(8,128)(2,1)}, bf16[256,1600]{0,1:T(8,128)(2,1)}, u32[]{:S(2)}, u32[]{:S(2)}) collective-permute-start(bf16[256,1600]{0,1:T(8,128)(2,1)} %copy.139), channel_id=1, source_target_pairs={{0,12},{4,8},{8,4},{12,0},{1,13},{5,9},{9,5},{13,1},{2,14},{6,10},... | collective-permute-start | bytes 2457608 | tf_op jit(solution)/shard_map/ppermute | solution.py:647
  1838.2 230.4 %collective-permute-start.80 = (bf16[1,104,896]{2,1,0:T(8,128)(2,1)}, bf16[1,104,896]{2,1,0:T(8,128)(2,1)}, u32[]{:S(2)}, u32[]{:S(2)}) collective-permute-start(bf16[1,104,896]{2,1,0:T(8,128)(2,1)} %get-tuple-element.253), channel_id=1, source_target_pairs={{0,1},{1,0},{2,3},{3,2},{4,5},{5,4},{6,7},{7,6},{8,9},{9,8},{10,11... | collective-permute-start | bytes 559112 | tf_op jit(solution)/shard_map/ppermute | solution.py:255
  1840.9 52.9 %collective-permute-start.78 = (bf16[1664,896]{1,0:T(8,128)(2,1)}, bf16[1664,896]{1,0:T(8,128)(2,1)}, u32[]{:S(2)}, u32[]{:S(2)}) collective-permute-start(bf16[1664,896]{1,0:T(8,128)(2,1)} %constant_dynamic-slice_fusion.4), channel_id=1, source_target_pairs={{0,16},{16,0},{1,17},{17,1},{2,18},{18,2},{3,19},{19,3},{4,20},{20... | collective-permute-start | bytes 8945672 | tf_op jit(solution)/shard_map/ppermute | solution.py:255
  1879.5 27.2 %collective-permute-start.68 = (bf16[2,256,1664]{2,1,0:T(8,128)(2,1)}, bf16[2,256,1664]{2,1,0:T(8,128)(2,1)}, u32[]{:S(2)}, u32[]{:S(2)}) collective-permute-start(bf16[2,256,1664]{2,1,0:T(8,128)(2,1)} %dynamic-slice_bitcast_fusion), channel_id=1, source_target_pairs={{0,16},{16,0},{1,17},{17,1},{2,18},{18,2},{3,19},{19,3},{4,20},{20... | collective-permute-start | bytes 5111816 | tf_op jit(solution)/shard_map/ppermute | solution.py:255
  1890.7 61.5 %collective-permute-start.71 = (bf16[1,256,1664]{2,1,0:T(8,128)(2,1)}, bf16[1,256,1664]{2,1,0:T(8,128)(2,1)}, u32[]{:S(2)}, u32[]{:S(2)}) collective-permute-start(bf16[1,256,1664]{2,1,0:T(8,128)(2,1)} %dynamic-slice_bitcast_fusion.9), channel_id=1, source_target_pairs={{0,16},{16,0},{1,17},{17,1},{2,18},{18,2},{3,19},{19,3},{4,20},{20... | collective-permute-start | bytes 2555912 | tf_op jit(solution)/shard_map/ppermute | solution.py:255
  1898.0 201.8 %reduce-scatter.17.cloned.1.call-start = ((), (), s32[]{:S(2)}) async-start(), calls=%async_computation.16 | async-start | bytes 5750784 | tf_op jit(solution)/shard_map/reduce_scatter | solution.py:670
  1910.6 39.1 %collective-permute-start.69 = (bf16[2,256,1664]{2,1,0:T(8,128)(2,1)}, bf16[2,256,1664]{2,1,0:T(8,128)(2,1)}, u32[]{:S(2)}, u32[]{:S(2)}) collective-permute-start(bf16[2,256,1664]{2,1,0:T(8,128)(2,1)} %get-tuple-element.161), channel_id=1, source_target_pairs={{0,1},{1,0},{2,3},{3,2},{4,5},{5,4},{6,7},{7,6},{8,9},{9,8},{10,11... | collective-permute-start | bytes 5111816 | tf_op jit(solution)/shard_map/ppermute | solution.py:255
  1994.1 108.0 %collective-permute-start.76 = (bf16[1,104,1536]{2,1,0:T(8,128)(2,1)}, bf16[1,104,1536]{2,1,0:T(8,128)(2,1)}, u32[]{:S(2)}, u32[]{:S(2)}) collective-permute-start(bf16[1,104,1536]{2,1,0:T(8,128)(2,1)} %get-tuple-element.249), channel_id=1, source_target_pairs={{0,1},{1,0},{2,3},{3,2},{4,5},{5,4},{6,7},{7,6},{8,9},{9,8},{10,11... | collective-permute-start | bytes 958472 | tf_op jit(solution)/shard_map/ppermute | solution.py:255
  2025.2 31.5 %collective-permute-start.73 = (bf16[3,256,1600]{1,2,0:T(8,128)(2,1)}, bf16[3,256,1600]{1,2,0:T(8,128)(2,1)}, u32[]{:S(2)}, u32[]{:S(2)}) collective-permute-start(bf16[3,256,1600]{1,2,0:T(8,128)(2,1)} %copy.152), channel_id=1, source_target_pairs={{0,0},{17,1},{1,16},{16,17},{2,2},{19,3},{3,18},{18,19},{4,4},{21,... | collective-permute-start | bytes 7372808 | tf_op jit(solution)/shard_map/ppermute | solution.py:590
  2070.0 32.1 %collective-permute-start.81 = (bf16[104,896]{1,0:T(8,128)(2,1)S(1)}, bf16[104,896]{1,0:T(8,128)(2,1)S(1)}, u32[]{:S(2)}, u32[]{:S(2)}) collective-permute-start(bf16[104,896]{1,0:T(8,128)(2,1)S(1)} %broadcast_select_fusion.27), channel_id=1, source_target_pairs={{0,16},{16,0},{1,17},{17,1},{2,18},{18,2},{3,19},{19,3},{4,20},{20... | collective-permute-start | bytes 559112 | tf_op jit(solution)/shard_map/ppermute | solution.py:255
  (279 other events, 6430.6 us)
Sparse Core Ops, SparseCore 0:
  13.5 91.1 all-gather.16
  107.5 119.7 all-gather.8
  229.4 97.5 all-gather.10
  345.0 126.4 all-gather.12
  700.4 105.3 all-gather.14
  896.4 92.4 all-gather.18
  996.9 105.7 reduce-scatter.10
  1207.2 72.1 reduce-scatter.8
  1283.4 121.4 reduce-scatter.12
  1488.9 97.4 reduce-scatter.14
  1590.3 106.6 reduce-scatter.20
  1700.8 161.5 reduce-scatter.22
  1898.1 86.8 reduce-scatter.18
  1988.6 111.1 reduce-scatter.16

commit v3 on v2

--- a/solution.py
+++ b/solution.py
@@ -537,8 +537,11 @@
     def layer_of(attn_all, up_all, down_all):
         if attn_all is None:
             return {"down": down_all.reshape(all_groups * hid_pad, width_pad)}
-        attn_all = attn_all.reshape(width_pad, P_LANES + side)
-        qkv_all, out_all = attn_all[:, :P_LANES], attn_all[:, P_LANES:]
+        if isinstance(attn_all, tuple):
+            qkv_all, out_all = (piece.reshape(width_pad, -1) for piece in attn_all)
+        else:
+            attn_all = attn_all.reshape(width_pad, P_LANES + side)
+            qkv_all, out_all = attn_all[:, :P_LANES], attn_all[:, P_LANES:]
         small_all = qkv_all.reshape(chips, part_pad, P_LANES)[:, part, :small_total]
         pieces, at = {}, 0
         for name in SMALL:
@@ -610,7 +613,8 @@
         for turn in reversed(turns):
             projected[turn] = project_stage(entering[l][turn], w, mask, width)
         if l == 0:
-            attn_second = gather(attn_l[1], projected[0][1], up_first)
+            out_second = gather(attn_l[1][:, P_LANES:], projected[0][1], up_first)
+            qkv_second = gather(attn_l[1][:, :P_LANES], projected[0][1], up_first)
         else:
             weights.append(gather(down_l[1], projected[0][1]))
             layers[1].update(layer_of(None, None, weights[-1]))
@@ -621,7 +625,7 @@
             partials[turn], kept_ffn[l][turn] = ffn_stage(middles[l][turn], w, mask, width)
             if l == 0 and turn == 0:
                 up_second = gather(up_l[1], partials[turn])
-                layers[1] = layer_of(attn_second, up_second, None)
+                layers[1] = layer_of((qkv_second, out_second), up_second, None)
         outputs[l] = [
             (middles[l][turn] + pair_sum(chip_rows(partials[turn])) + w["down_bias"]).astype(BF16) for turn in turns
         ]

time: 2140 us -> 2080 us (0.972)
  waiting for transfers between devices: 916 us -> 846 us
    all_gather x6 -> x7, waiting for transfers between devices: 273 us -> 203 us  [gather(): return lax.all_gather(tied(piece, tokens), groups, axis=0)]
    select_n x26 -> x27, other arithmetic: 69.8 us -> 76.3 us  [in_turn(): return jnp.where(place == mine_at, mine, other)]
    unnamed x496 -> x504, local copies, waits for them, and re-layouts: 43.7 us -> 44.9 us
  transfers between devices with their start and end apart: 100 -> 101, of which waited for: 40 -> 42; matrix products, arithmetic and copies ran while one was open for 39% -> 40% of each run, Pallas kernels for 6% -> 6%
where the time goes in v3:
time: 2080 us; the launch traced here: 2070 us
  waiting for transfers between devices  846 us (41%)
  matrix products  336 us (16%)
  other arithmetic  291 us (14%)
  local copies, waits for them, and re-layouts  239 us (11%)
  starting transfers between devices  163 us (8%)
  Pallas kernels  123 us (6%)
  between operations  71.4 us (3%)
    ppermute x69, waiting for transfers between devices, flip(): return lax.ppermute(value, axis, [(0, 1), (1, 0)])  322 us
    all_gather x7, waiting for transfers between devices, gather(): return lax.all_gather(tied(piece, tokens), groups, axis=0)  203 us
    dot_general x16, matrix products, dot_0(): lax.dot_general(a.reshape(-1, a.shape[-1]), b.reshape(-1, b.shape[-1]), T...  135 us
    ppermute x4, waiting for transfers between devices, whole_sequence(): other = lax.ppermute(packed[..., V_LANES:], 'y', [(0, 1)])  133 us
    dot_general x16, matrix products, dot_t(): lax.dot_general(a.reshape(-1, a.shape[-1]), b, NT, preferred_element_type...  102 us
    ppermute x69, starting transfers between devices, flip(): return lax.ppermute(value, axis, [(0, 1), (1, 0)])  99.3 us
    dot_general x18, matrix products, dot(): flat = jnp.dot(a.reshape(-1, a.shape[-1]), b, preferred_element_type=F32)  99.1 us
    ppermute x4, waiting for transfers between devices, own_rows(): other = lax.ppermute(grad[:, :rows, V_LANES:], 'y', [(1, 0)])  96.1 us
  transfers between devices with their start and end apart: 101, of which 42 were waited for; matrix products, arithmetic and copies ran while one was open for 40% of the time, Pallas kernels for 6%

profile of v3, /device:TPU:1, one launch (start us, length us, event | category | flops | bytes accessed | tf_op | source)
XLA Modules:
  0.0 2068.5 jit_solution(17389026784758499749)
XLA Ops:
  27.0 11.0 collective-permute-done.2
  57.5 47.2 %all-gather.18.cloned.1.call-done = bf16[1664,1664]{1,0:T(8,128)(2,1)} async-done(((bf16[208,1664]{1,0:T(8,128)(2,1)}), bf16[1664,1664]{1,0:T(8,128)(2,1)}) %all-gather.18.cloned.1.call-update) | async-done | bytes 5537808 | tf_op jit(solution)/shard_map/all_gather | solution.py:531
  120.8 106.5 %all-gather.12.cloned.1.call-done = bf16[8,208,2432]{2,1,0:T(8,128)(2,1)} async-done(((bf16[1,208,2432]{2,1,0:T(8,128)(2,1)}), bf16[8,208,2432]{2,1,0:T(8,128)(2,1)}) %all-gather.12.cloned.1.call-update) | async-done | bytes 8093712 | tf_op jit(solution)/shard_map/all_gather | solution.py:531
  239.8 7.8 add_convert_fusion.11
  256.8 11.4 collective-permute-done.22
  271.0 56.8 %collective-permute-done.4 = bf16[2,512,1024]{2,1,0:T(8,128)(2,1)} collective-permute-done((bf16[2,512,1024]{2,1,0:T(8,128)(2,1)}, bf16[2,512,1024]{2,1,0:T(8,128)(2,1)}, u32[]{:S(2)}, u32[]{:S(2)}) %collective-permute-start.4) | collective-permute-done | bytes 2097184 | tf_op jit(solution)/shard_map/ppermute | solution.py:362
  358.2 49.4 %all-gather.22.cloned.1.call-done = bf16[1664,896]{1,0:T(8,128)(2,1)} async-done(((bf16[208,896]{1,0:T(8,128)(2,1)}), bf16[1664,896]{1,0:T(8,128)(2,1)}) %all-gather.22.cloned.1.call-update) | async-done | bytes 2981904 | tf_op jit(solution)/shard_map/all_gather | solution.py:531
  427.7 11.3 attn_fwd.4
  446.7 7.6 broadcast_select_fusion
  500.8 27.6 %collective-permute-done.7 = bf16[2,256,1664]{2,1,0:T(8,128)(2,1)S(1)} collective-permute-done((bf16[2,256,1664]{2,1,0:T(8,128)(2,1)S(1)}, bf16[2,256,1664]{2,1,0:T(8,128)(2,1)S(1)}, u32[]{:S(2)}, u32[]{:S(2)}) %collective-permute-start.7) | collective-permute-done | bytes 1703968 | tf_op jit(solution)/shard_map/ppermute | solution.py:255
  556.1 9.0 fusion.4
  596.8 26.7 %collective-permute-done.17 = bf16[2,256,1664]{2,1,0:T(8,128)(2,1)S(1)} collective-permute-done((bf16[2,256,1664]{2,1,0:T(8,128)(2,1)S(1)}, bf16[2,256,1664]{2,1,0:T(8,128)(2,1)S(1)}, u32[]{:S(2)}, u32[]{:S(2)}) %collective-permute-start.17) | collective-permute-done | bytes 1703968 | tf_op jit(solution)/shard_map/ppermute | solution.py:255
  637.0 10.9 collective-permute-done.20
  663.2 11.3 collective-permute-start.24
  688.0 58.6 %collective-permute-done.24 = bf16[2,512,1024]{2,1,0:T(8,128)(2,1)S(1)} collective-permute-done((bf16[2,512,1024]{2,1,0:T(8,128)(2,1)S(1)}, bf16[2,512,1024]{2,1,0:T(8,128)(2,1)S(1)}, u32[]{:S(2)}, u32[]{:S(2)}) %collective-permute-start.24) | collective-permute-done | bytes 2097184 | tf_op jit(solution)/shard_map/ppermute | solution.py:362
  752.3 11.6 attn_fwd.6
  775.0 12.1 collective-permute-start.32
  789.9 17.6 collective-permute-done.32
  830.7 18.7 collective-permute-done.27
  864.4 11.2 collective-permute-done.34
  907.2 8.2 fusion.284
  915.4 9.5 fusion.9
  924.9 11.3 add_convert_fusion.3
  940.7 10.1 fusion.65
  952.7 14.2 convert_reduce_fusion.1
  966.9 8.8 convolution_convert_fusion.3
  984.8 7.8 convert_reduce_fusion.9
  992.6 22.2 %collective-permute-done.35 = bf16[2,256,1664]{2,1,0:T(8,128)(2,1)S(1)} collective-permute-done((bf16[2,256,1664]{2,1,0:T(8,128)(2,1)S(1)}, bf16[2,256,1664]{2,1,0:T(8,128)(2,1)S(1)}, u32[]{:S(2)}, u32[]{:S(2)}) %collective-permute-start.35) | collective-permute-done | bytes 1703968 | tf_op jit(solution)/shard_map/ppermute | solution.py:255
  1026.2 7.4 fusion.326
  1040.1 12.8 add_convert_fusion.2
  1054.9 22.0 %collective-permute-done.43 = bf16[2,256,1664]{2,1,0:T(8,128)(2,1)S(1)} collective-permute-done((bf16[2,256,1664]{2,1,0:T(8,128)(2,1)}, bf16[2,256,1664]{2,1,0:T(8,128)(2,1)S(1)}, u32[]{:S(2)}, u32[]{:S(2)}) %collective-permute-start.43) | collective-permute-done | bytes 1703968 | tf_op jit(solution)/shard_map/ppermute | solution.py:255
  1082.6 15.2 collective-permute-done.46
  1120.3 11.0 convolution_convert_fusion.1
  1150.0 13.0 attn_bwd.4
  1171.6 22.6 %attn_bwd.5 = bf16[2,1024,1536]{2,1,0:T(8,128)(2,1)} custom-call(s32[3]{0:T(128)} %broadcast_add_fusion.20.info_ref, bf16[2,1024,1536]{2,1,0:T(8,128)(2,1)} %bitcast_select_fusion.q_ref.k_ref.v_ref, bf16[2,1024,1536]{2,1,0:T(8,128)(2,1)} %bitcast_select_fusion.q_ref.k_ref.v_ref, bf16[2,1024,1536]{2,1,0:T(8,128)(2,1)} %bitcast_select_fusion.q_ref.k_ref.v_ref, ...), custom_call_target="tpu_custom_call" | custom-call | tf_op jit(solution)/shard_map/attn_bwd/pallas_call | solution.py:231
  1205.5 67.8 %collective-permute-done.49 = bf16[2,512,1024]{2,1,0:T(8,128)(2,1)} collective-permute-done((bf16[2,512,1024]{2,1,0:T(8,128)(2,1)}, bf16[2,512,1024]{2,1,0:T(8,128)(2,1)}, u32[]{:S(2)}, u32[]{:S(2)}) %collective-permute-start.49) | collective-permute-done | bytes 2097184 | tf_op jit(solution)/shard_map/ppermute | solution.py:375
  1287.2 21.9 %collective-permute-done.52 = bf16[1,512,1024]{2,1,0:T(8,128)(2,1)S(1)} collective-permute-done((bf16[1,512,1024]{2,1,0:T(8,128)(2,1)S(1)}, bf16[1,512,1024]{2,1,0:T(8,128)(2,1)S(1)}, u32[]{:S(2)}, u32[]{:S(2)}) %collective-permute-start.52) | collective-permute-done | bytes 1048608 | tf_op jit(solution)/shard_map/ppermute | solution.py:375
  1332.1 26.2 %collective-permute-done.51 = bf16[2,256,1664]{2,1,0:T(8,128)(2,1)S(1)} collective-permute-done((bf16[2,256,1664]{2,1,0:T(8,128)(2,1)}, bf16[2,256,1664]{2,1,0:T(8,128)(2,1)S(1)}, u32[]{:S(2)}, u32[]{:S(2)}) %collective-permute-start.51) | collective-permute-done | bytes 1703968 | tf_op jit(solution)/shard_map/ppermute | solution.py:255
  1366.1 14.8 collective-permute-done.57
  1404.3 13.6 convert_reduce_fusion
  1424.9 9.5 fusion.327
  1434.4 11.4 add_convert_fusion
  1486.9 19.2 collective-permute-done.39
  1526.1 10.5 collective-permute-start.74
  1539.9 9.7 convolution_convert_fusion.2
  1558.4 7.9 fusion.287
  1568.7 11.7 collective-permute-start.58
  1580.4 10.4 add_convert_fusion.1
  1595.6 22.2 %collective-permute-done.58 = bf16[2,256,1664]{2,1,0:T(8,128)(2,1)} collective-permute-done((bf16[2,256,1664]{2,1,0:T(8,128)(2,1)}, bf16[2,256,1664]{2,1,0:T(8,128)(2,1)}, u32[]{:S(2)}, u32[]{:S(2)}) %collective-permute-start.58) | collective-permute-done | bytes 1703968 | tf_op jit(solution)/shard_map/ppermute | solution.py:255
  1632.8 8.8 collective-permute-done.62
  1658.6 12.8 attn_bwd.6
  1680.7 22.7 %attn_bwd.7 = bf16[2,1024,1536]{2,1,0:T(8,128)(2,1)} custom-call(s32[3]{0:T(128)} %broadcast_add_fusion.19.info_ref, bf16[2,1024,1536]{2,1,0:T(8,128)(2,1)} %bitcast_select_fusion.1.q_ref.k_ref.v_ref, bf16[2,1024,1536]{2,1,0:T(8,128)(2,1)} %bitcast_select_fusion.1.q_ref.k_ref.v_ref, bf16[2,1024,1536]{2,1,0:T(8,128)(2,1)} %bitcast_select_fusion.1.q_ref.k_ref.v_ref, ...), custom_call_target="tpu_custom_call" | custom-call | tf_op jit(solution)/shard_map/attn_bwd/pallas_call | solution.py:231
  1734.0 10.7 convolution_convert_fusion
  1750.7 23.4 %collective-permute-done.66 = bf16[256,1600]{0,1:T(8,128)(2,1)} collective-permute-done((bf16[256,1600]{0,1:T(8,128)(2,1)}, bf16[256,1600]{0,1:T(8,128)(2,1)}, u32[]{:S(2)}, u32[]{:S(2)}) %collective-permute-start.66) | collective-permute-done | bytes 819232 | tf_op jit(solution)/shard_map/ppermute | solution.py:651
  1780.0 15.7 collective-permute-done.64
  1835.7 8.6 fusion.195
  1850.1 11.2 add_convert_fusion.4
  1864.0 23.4 %collective-permute-done.69 = bf16[2,256,1664]{2,1,0:T(8,128)(2,1)} collective-permute-done((bf16[2,256,1664]{2,1,0:T(8,128)(2,1)}, bf16[2,256,1664]{2,1,0:T(8,128)(2,1)}, u32[]{:S(2)}, u32[]{:S(2)}) %collective-permute-start.69) | collective-permute-done | bytes 1703968 | tf_op jit(solution)/shard_map/ppermute | solution.py:255
  1898.7 13.7 collective-permute-done.72
  1933.0 7.6 add_convert_fusion.15
  1977.6 8.1 reshape.2775
  1985.7 9.0 collective-permute-done.73
  2007.9 10.7 collective-permute-start.81
  2018.6 19.0 reduce-scatter.17.cloned.1.call-done
  (1235 shorter events, 814.4 us)
Async XLA Ops:
  7.2 97.6 %all-gather.18.cloned.1.call-start = ((), (), s32[]{:S(2)}) async-start(), calls=%async_computation.19 | async-start | bytes 6230016 | tf_op jit(solution)/shard_map/all_gather | solution.py:531
  13.4 213.9 %all-gather.12.cloned.1.call-start = ((), (), s32[]{:S(2)}) async-start(), calls=%async_computation.8 | async-start | bytes 9105408 | tf_op jit(solution)/shard_map/all_gather | solution.py:531
  39.4 300.6 %all-gather.14.cloned.1.call-start = ((), (), s32[]{:S(2)}) async-start(), calls=%async_computation.9 | async-start | bytes 6230016 | tf_op jit(solution)/shard_map/all_gather | solution.py:531
  54.8 52.5 %collective-permute-start.10 = (bf16[1,104,1664]{2,1,0:T(8,128)(2,1)}, bf16[1,104,1664]{2,1,0:T(8,128)(2,1)}, u32[]{:S(2)}, u32[]{:S(2)}) collective-permute-start(bf16[1,104,1664]{2,1,0:T(8,128)(2,1)} %get-tuple-element.229), channel_id=1, source_target_pairs={{0,1},{1,0},{2,3},{3,2},{4,5},{5,4},{6,7},{7,6},{8,9},{9,8},{10,11... | collective-permute-start | bytes 1038344 | tf_op jit(solution)/shard_map/ppermute | solution.py:255
  56.2 54.7 %collective-permute-start = (bf16[3,256,1600]{1,2,0:T(8,128)(2,1)S(1)}, bf16[3,256,1600]{1,2,0:T(8,128)(2,1)}, u32[]{:S(2)}, u32[]{:S(2)}) collective-permute-start(bf16[3,256,1600]{1,2,0:T(8,128)(2,1)S(1)} %copy-done.122), channel_id=1, source_target_pairs={{0,1},{17,16},{2,3},{19,18},{4,5},{21,20},{6,7},{23,22},{8,9},{25,... | collective-permute-start | bytes 7372808 | tf_op jit(solution)/shard_map/ppermute | solution.py:586
  110.4 297.2 %all-gather.22.cloned.1.call-start = ((), (), s32[]{:S(2)}) async-start(), calls=%async_computation.21 | async-start | bytes 3354624 | tf_op jit(solution)/shard_map/all_gather | solution.py:531
  250.9 76.8 %collective-permute-start.4 = (bf16[2,512,1024]{2,1,0:T(8,128)(2,1)}, bf16[2,512,1024]{2,1,0:T(8,128)(2,1)}, u32[]{:S(2)}, u32[]{:S(2)}) collective-permute-start(bf16[2,512,1024]{2,1,0:T(8,128)(2,1)} %slice.678), channel_id=1, source_target_pairs={{0,2},{1,3},{4,6},{5,7},{8,10},{9,11},{12,14},{13,15},{16,18},{17,... | collective-permute-start | bytes 6291464 | tf_op jit(solution)/shard_map/ppermute | solution.py:362
  344.2 202.3 %all-gather.20.cloned.1.call-start = ((), (), s32[]{:S(2)}) async-start(), calls=%async_computation.20 | async-start | bytes 5750784 | tf_op jit(solution)/shard_map/all_gather | solution.py:531
  349.8 284.5 %collective-permute-start.29 = (bf16[1,104,1664]{2,1,0:T(8,128)(2,1)}, bf16[1,104,1664]{2,1,0:T(8,128)(2,1)}, u32[]{:S(2)}, u32[]{:S(2)}) collective-permute-start(bf16[1,104,1664]{2,1,0:T(8,128)(2,1)} %get-tuple-element.227), channel_id=1, source_target_pairs={{0,1},{1,0},{2,3},{3,2},{4,5},{5,4},{6,7},{7,6},{8,9},{9,8},{10,11... | collective-permute-start | bytes 1038344 | tf_op jit(solution)/shard_map/ppermute | solution.py:255
  355.3 91.4 %collective-permute-start.5 = (bf16[1664,896]{1,0:T(8,128)(2,1)}, bf16[1664,896]{1,0:T(8,128)(2,1)}, u32[]{:S(2)}, u32[]{:S(2)}) collective-permute-start(bf16[1664,896]{1,0:T(8,128)(2,1)} %slice.679), channel_id=1, source_target_pairs={{0,16},{16,0},{1,17},{17,1},{2,18},{18,2},{3,19},{19,3},{4,20},{20... | collective-permute-start | bytes 8945672 | tf_op jit(solution)/shard_map/ppermute | solution.py:255
  407.6 39.1 %collective-permute-start.25 = (bf16[1664,896]{1,0:T(8,128)(2,1)}, bf16[1664,896]{1,0:T(8,128)(2,1)}, u32[]{:S(2)}, u32[]{:S(2)}) collective-permute-start(bf16[1664,896]{1,0:T(8,128)(2,1)} %all-gather.22.cloned.1.call-done), channel_id=1, source_target_pairs={{0,16},{16,0},{1,17},{17,1},{2,18},{18,2},{3,19},{19,3},{4,20},{20... | collective-permute-start | bytes 8945672 | tf_op jit(solution)/shard_map/ppermute | solution.py:255
  424.4 42.8 %collective-permute-start.14 = (bf16[1,512,1024]{2,1,0:T(8,128)(2,1)}, bf16[1,512,1024]{2,1,0:T(8,128)(2,1)}, u32[]{:S(2)}, u32[]{:S(2)}) collective-permute-start(bf16[1,512,1024]{2,1,0:T(8,128)(2,1)} %slice.692), channel_id=1, source_target_pairs={{0,2},{1,3},{4,6},{5,7},{8,10},{9,11},{12,14},{13,15},{16,18},{17,... | collective-permute-start | bytes 3145736 | tf_op jit(solution)/shard_map/ppermute | solution.py:362
  441.5 458.9 %all-gather.16.cloned.1.call-start = ((), (), s32[]{:S(2)}) async-start(), calls=%async_computation.10 | async-start | bytes 6230016 | tf_op jit(solution)/shard_map/all_gather | solution.py:531
  445.0 31.2 %collective-permute-start.40 = (bf16[3,256,1600]{1,2,0:T(8,128)(2,1)}, bf16[3,256,1600]{1,2,0:T(8,128)(2,1)}, u32[]{:S(2)}, u32[]{:S(2)}) collective-permute-start(bf16[3,256,1600]{1,2,0:T(8,128)(2,1)} %broadcast_add_fusion), channel_id=1, source_target_pairs={{0,1},{17,16},{2,3},{19,18},{4,5},{21,20},{6,7},{23,22},{8,9},{25,... | collective-permute-start | bytes 7372808 | tf_op jit(solution)/shard_map/ppermute | solution.py:586
  490.6 37.8 %collective-permute-start.7 = (bf16[2,256,1664]{2,1,0:T(8,128)(2,1)S(1)}, bf16[2,256,1664]{2,1,0:T(8,128)(2,1)S(1)}, u32[]{:S(2)}, u32[]{:S(2)}) collective-permute-start(bf16[2,256,1664]{2,1,0:T(8,128)(2,1)S(1)} %fusion.125), channel_id=1, source_target_pairs={{0,1},{1,0},{2,3},{3,2},{4,5},{5,4},{6,7},{7,6},{8,9},{9,8},{10,11... | collective-permute-start | bytes 5111816 | tf_op jit(solution)/shard_map/ppermute | solution.py:255
  492.2 158.2 %collective-permute-start.41 = (bf16[2,256,1664]{2,1,0:T(8,128)(2,1)}, bf16[2,256,1664]{2,1,0:T(8,128)(2,1)}, u32[]{:S(2)}, u32[]{:S(2)}) collective-permute-start(bf16[2,256,1664]{2,1,0:T(8,128)(2,1)} %select_convert_fusion.1), channel_id=1, source_target_pairs={{0,16},{16,0},{1,17},{17,1},{2,18},{18,2},{3,19},{19,3},{4,20},{20... | collective-permute-start | bytes 5111816 | tf_op jit(solution)/shard_map/ppermute | solution.py:255
  496.6 33.6 %collective-permute-start.15 = (bf16[1,256,1664]{2,1,0:T(8,128)(2,1)S(1)}, bf16[1,256,1664]{2,1,0:T(8,128)(2,1)S(1)}, u32[]{:S(2)}, u32[]{:S(2)}) collective-permute-start(bf16[1,256,1664]{2,1,0:T(8,128)(2,1)S(1)} %dynamic-slice_bitcast_fusion.16), channel_id=1, source_target_pairs={{0,16},{16,0},{1,17},{17,1},{2,18},{18,2},{3,19},{19,3},{4,20},{20... | collective-permute-start | bytes 2555912 | tf_op jit(solution)/shard_map/ppermute | solution.py:255
  498.6 185.4 %collective-permute-start.44 = (bf16[1,256,1664]{2,1,0:T(8,128)(2,1)}, bf16[1,256,1664]{2,1,0:T(8,128)(2,1)}, u32[]{:S(2)}, u32[]{:S(2)}) collective-permute-start(bf16[1,256,1664]{2,1,0:T(8,128)(2,1)} %bitcast.169), channel_id=1, source_target_pairs={{0,16},{16,0},{1,17},{17,1},{2,18},{18,2},{3,19},{19,3},{4,20},{20... | collective-permute-start | bytes 2555912 | tf_op jit(solution)/shard_map/ppermute | solution.py:255
  585.2 38.3 %collective-permute-start.17 = (bf16[2,256,1664]{2,1,0:T(8,128)(2,1)S(1)}, bf16[2,256,1664]{2,1,0:T(8,128)(2,1)S(1)}, u32[]{:S(2)}, u32[]{:S(2)}) collective-permute-start(bf16[2,256,1664]{2,1,0:T(8,128)(2,1)S(1)} %broadcast_add_fusion.8), channel_id=1, source_target_pairs={{0,1},{1,0},{2,3},{3,2},{4,5},{5,4},{6,7},{7,6},{8,9},{9,8},{10,11... | collective-permute-start | bytes 5111816 | tf_op jit(solution)/shard_map/ppermute | solution.py:255
  595.9 31.4 %collective-permute-start.19 = (bf16[1,256,1664]{2,1,0:T(8,128)(2,1)S(1)}, bf16[1,256,1664]{2,1,0:T(8,128)(2,1)S(1)}, u32[]{:S(2)}, u32[]{:S(2)}) collective-permute-start(bf16[1,256,1664]{2,1,0:T(8,128)(2,1)S(1)} %dynamic-slice_bitcast_fusion.15), channel_id=1, source_target_pairs={{0,16},{16,0},{1,17},{17,1},{2,18},{18,2},{3,19},{19,3},{4,20},{20... | collective-permute-start | bytes 2555912 | tf_op jit(solution)/shard_map/ppermute | solution.py:255
  636.5 304.1 %all-gather.24.cloned.1.call-start = ((), (), s32[]{:S(2)}) async-start(), calls=%async_computation.22 | async-start | bytes 6230016 | tf_op jit(solution)/shard_map/all_gather | solution.py:531
  663.2 83.4 %collective-permute-start.24 = (bf16[2,512,1024]{2,1,0:T(8,128)(2,1)S(1)}, bf16[2,512,1024]{2,1,0:T(8,128)(2,1)S(1)}, u32[]{:S(2)}, u32[]{:S(2)}) collective-permute-start(bf16[2,512,1024]{2,1,0:T(8,128)(2,1)S(1)} %slice.704), channel_id=1, source_target_pairs={{0,2},{1,3},{4,6},{5,7},{8,10},{9,11},{12,14},{13,15},{16,18},{17,... | collective-permute-start | bytes 6291464 | tf_op jit(solution)/shard_map/ppermute | solution.py:362
  767.4 41.4 %collective-permute-start.26 = (bf16[2,256,1664]{2,1,0:T(8,128)(2,1)}, bf16[2,256,1664]{2,1,0:T(8,128)(2,1)S(1)}, u32[]{:S(2)}, u32[]{:S(2)}) collective-permute-start(bf16[2,256,1664]{2,1,0:T(8,128)(2,1)} %dynamic-slice_bitcast_fusion.5), channel_id=1, source_target_pairs={{0,16},{16,0},{1,17},{17,1},{2,18},{18,2},{3,19},{19,3},{4,20},{20... | collective-permute-start | bytes 5111816 | tf_op jit(solution)/shard_map/ppermute | solution.py:255
  775.0 32.5 %collective-permute-start.32 = (bf16[1,512,1024]{2,1,0:T(8,128)(2,1)}, bf16[1,512,1024]{2,1,0:T(8,128)(2,1)}, u32[]{:S(2)}, u32[]{:S(2)}) collective-permute-start(bf16[1,512,1024]{2,1,0:T(8,128)(2,1)} %slice.715), channel_id=1, source_target_pairs={{0,2},{1,3},{4,6},{5,7},{8,10},{9,11},{12,14},{13,15},{16,18},{17,... | collective-permute-start | bytes 3145736 | tf_op jit(solution)/shard_map/ppermute | solution.py:362
  812.7 36.7 %collective-permute-start.27 = (bf16[2,256,1664]{2,1,0:T(8,128)(2,1)}, bf16[2,256,1664]{2,1,0:T(8,128)(2,1)}, u32[]{:S(2)}, u32[]{:S(2)}) collective-permute-start(bf16[2,256,1664]{2,1,0:T(8,128)(2,1)} %broadcast_add_fusion.7), channel_id=1, source_target_pairs={{0,1},{1,0},{2,3},{3,2},{4,5},{5,4},{6,7},{7,6},{8,9},{9,8},{10,11... | collective-permute-start | bytes 5111816 | tf_op jit(solution)/shard_map/ppermute | solution.py:255
  824.3 31.8 %collective-permute-start.33 = (bf16[1,256,1664]{2,1,0:T(8,128)(2,1)}, bf16[1,256,1664]{2,1,0:T(8,128)(2,1)}, u32[]{:S(2)}, u32[]{:S(2)}) collective-permute-start(bf16[1,256,1664]{2,1,0:T(8,128)(2,1)} %dynamic-slice_bitcast_fusion.14), channel_id=1, source_target_pairs={{0,16},{16,0},{1,17},{17,1},{2,18},{18,2},{3,19},{19,3},{4,20},{20... | collective-permute-start | bytes 2555912 | tf_op jit(solution)/shard_map/ppermute | solution.py:255
  830.2 370.5 %reduce-scatter.11.cloned.1.call-start = ((), (), s32[]{:S(2)}) async-start(), calls=%async_computation.12 | async-start | bytes 6230016 | tf_op jit(solution)/shard_map/reduce_scatter | solution.py:674
  860.8 35.4 %collective-permute-start.28 = (bf16[2,256,1664]{2,1,0:T(8,128)(2,1)}, bf16[2,256,1664]{2,1,0:T(8,128)(2,1)}, u32[]{:S(2)}, u32[]{:S(2)}) collective-permute-start(bf16[2,256,1664]{2,1,0:T(8,128)(2,1)} %add_convert_fusion.18), channel_id=1, source_target_pairs={{0,16},{16,0},{1,17},{17,1},{2,18},{18,2},{3,19},{19,3},{4,20},{20... | collective-permute-start | bytes 5111816 | tf_op jit(solution)/shard_map/ppermute | solution.py:255
  940.4 442.4 %reduce-scatter.9.cloned.1.call-start = ((), (), s32[]{:S(2)}) async-start(), calls=%async_computation.11 | async-start | bytes 3354624 | tf_op jit(solution)/shard_map/reduce_scatter | solution.py:674
  975.8 62.4 %collective-permute-start.42 = (bf16[2,256,1664]{2,1,0:T(8,128)(2,1)S(1)}, bf16[2,256,1664]{2,1,0:T(8,128)(2,1)S(1)}, u32[]{:S(2)}, u32[]{:S(2)}) collective-permute-start(bf16[2,256,1664]{2,1,0:T(8,128)(2,1)S(1)} %dynamic-slice_bitcast_fusion.3), channel_id=1, source_target_pairs={{0,16},{16,0},{1,17},{17,1},{2,18},{18,2},{3,19},{19,3},{4,20},{20... | collective-permute-start | bytes 5111816 | tf_op jit(solution)/shard_map/ppermute | solution.py:255
  976.5 38.4 %collective-permute-start.35 = (bf16[2,256,1664]{2,1,0:T(8,128)(2,1)S(1)}, bf16[2,256,1664]{2,1,0:T(8,128)(2,1)S(1)}, u32[]{:S(2)}, u32[]{:S(2)}) collective-permute-start(bf16[2,256,1664]{2,1,0:T(8,128)(2,1)S(1)} %broadcast_add_fusion.6), channel_id=1, source_target_pairs={{0,1},{1,0},{2,3},{3,2},{4,5},{5,4},{6,7},{7,6},{8,9},{9,8},{10,11... | collective-permute-start | bytes 5111816 | tf_op jit(solution)/shard_map/ppermute | solution.py:255
  984.6 32.2 %collective-permute-start.37 = (bf16[1,256,1664]{2,1,0:T(8,128)(2,1)S(1)}, bf16[1,256,1664]{2,1,0:T(8,128)(2,1)S(1)}, u32[]{:S(2)}, u32[]{:S(2)}) collective-permute-start(bf16[1,256,1664]{2,1,0:T(8,128)(2,1)S(1)} %dynamic-slice_bitcast_fusion.13), channel_id=1, source_target_pairs={{0,16},{16,0},{1,17},{17,1},{2,18},{18,2},{3,19},{19,3},{4,20},{20... | collective-permute-start | bytes 2555912 | tf_op jit(solution)/shard_map/ppermute | solution.py:255
  1024.5 54.2 %collective-permute-start.45 = (bf16[1,256,1664]{2,1,0:T(8,128)(2,1)}, bf16[1,256,1664]{2,1,0:T(8,128)(2,1)}, u32[]{:S(2)}, u32[]{:S(2)}) collective-permute-start(bf16[1,256,1664]{2,1,0:T(8,128)(2,1)} %dynamic-slice_bitcast_fusion.12), channel_id=1, source_target_pairs={{0,16},{16,0},{1,17},{17,1},{2,18},{18,2},{3,19},{19,3},{4,20},{20... | collective-permute-start | bytes 2555912 | tf_op jit(solution)/shard_map/ppermute | solution.py:255
  1040.1 36.8 %collective-permute-start.43 = (bf16[2,256,1664]{2,1,0:T(8,128)(2,1)}, bf16[2,256,1664]{2,1,0:T(8,128)(2,1)S(1)}, u32[]{:S(2)}, u32[]{:S(2)}) collective-permute-start(bf16[2,256,1664]{2,1,0:T(8,128)(2,1)} %get-tuple-element.175), channel_id=1, source_target_pairs={{0,1},{1,0},{2,3},{3,2},{4,5},{5,4},{6,7},{7,6},{8,9},{9,8},{10,11... | collective-permute-start | bytes 5111816 | tf_op jit(solution)/shard_map/ppermute | solution.py:255
  1146.0 368.1 %reduce-scatter.13.cloned.1.call-start = ((), (), s32[]{:S(2)}) async-start(), calls=%async_computation.13 | async-start | bytes 6230016 | tf_op jit(solution)/shard_map/reduce_scatter | solution.py:674
  1197.3 75.9 %collective-permute-start.49 = (bf16[2,512,1024]{2,1,0:T(8,128)(2,1)}, bf16[2,512,1024]{2,1,0:T(8,128)(2,1)}, u32[]{:S(2)}, u32[]{:S(2)}) collective-permute-start(bf16[2,512,1024]{2,1,0:T(8,128)(2,1)} %slice.730), channel_id=1, source_target_pairs={{2,0},{3,1},{6,4},{7,5},{10,8},{11,9},{14,12},{15,13},{18,16},{19,... | collective-permute-start | bytes 6291464 | tf_op jit(solution)/shard_map/ppermute | solution.py:375
  1200.7 660.7 %reduce-scatter.15.cloned.1.call-start = ((), (), s32[]{:S(2)}) async-start(), calls=%async_computation.14 | async-start | bytes 5750784 | tf_op jit(solution)/shard_map/reduce_scatter | solution.py:674
  1203.9 105.2 %collective-permute-start.52 = (bf16[1,512,1024]{2,1,0:T(8,128)(2,1)S(1)}, bf16[1,512,1024]{2,1,0:T(8,128)(2,1)S(1)}, u32[]{:S(2)}, u32[]{:S(2)}) collective-permute-start(bf16[1,512,1024]{2,1,0:T(8,128)(2,1)S(1)} %slice.732), channel_id=1, source_target_pairs={{2,0},{3,1},{6,4},{7,5},{10,8},{11,9},{14,12},{15,13},{18,16},{19,... | collective-permute-start | bytes 3145736 | tf_op jit(solution)/shard_map/ppermute | solution.py:375
  1283.4 34.5 %collective-permute-start.50 = (bf16[2,256,1664]{2,1,0:T(8,128)(2,1)S(1)}, bf16[2,256,1664]{2,1,0:T(8,128)(2,1)S(1)}, u32[]{:S(2)}, u32[]{:S(2)}) collective-permute-start(bf16[2,256,1664]{2,1,0:T(8,128)(2,1)S(1)} %dynamic-slice_bitcast_fusion.2), channel_id=1, source_target_pairs={{0,16},{16,0},{1,17},{17,1},{2,18},{18,2},{3,19},{19,3},{4,20},{20... | collective-permute-start | bytes 5111816 | tf_op jit(solution)/shard_map/ppermute | solution.py:255
  1313.2 47.1 %collective-permute-start.56 = (bf16[1,256,1664]{2,1,0:T(8,128)(2,1)}, bf16[1,256,1664]{2,1,0:T(8,128)(2,1)}, u32[]{:S(2)}, u32[]{:S(2)}) collective-permute-start(bf16[1,256,1664]{2,1,0:T(8,128)(2,1)} %dynamic-slice_bitcast_fusion.11), channel_id=1, source_target_pairs={{0,16},{16,0},{1,17},{17,1},{2,18},{18,2},{3,19},{19,3},{4,20},{20... | collective-permute-start | bytes 2555912 | tf_op jit(solution)/shard_map/ppermute | solution.py:255
  1320.4 38.0 %collective-permute-start.51 = (bf16[2,256,1664]{2,1,0:T(8,128)(2,1)}, bf16[2,256,1664]{2,1,0:T(8,128)(2,1)S(1)}, u32[]{:S(2)}, u32[]{:S(2)}) collective-permute-start(bf16[2,256,1664]{2,1,0:T(8,128)(2,1)} %get-tuple-element.171), channel_id=1, source_target_pairs={{0,1},{1,0},{2,3},{3,2},{4,5},{5,4},{6,7},{7,6},{8,9},{9,8},{10,11... | collective-permute-start | bytes 5111816 | tf_op jit(solution)/shard_map/ppermute | solution.py:255
  1424.8 515.8 %reduce-scatter.21.cloned.1.call-start = ((), (), s32[]{:S(2)}) async-start(), calls=%async_computation.17 | async-start | bytes 6230016 | tf_op jit(solution)/shard_map/reduce_scatter | solution.py:674
  1445.9 497.0 %reduce-scatter.23.cloned.1.call-start = ((), (), s32[]{:S(2)}) async-start(), calls=%async_computation.18 | async-start | bytes 6230016 | tf_op jit(solution)/shard_map/reduce_scatter | solution.py:674
  1450.7 31.5 %collective-permute-start.21 = (bf16[3,256,1600]{1,2,0:T(8,128)(2,1)}, bf16[3,256,1600]{1,2,0:T(8,128)(2,1)}, u32[]{:S(2)}, u32[]{:S(2)}) collective-permute-start(bf16[3,256,1600]{1,2,0:T(8,128)(2,1)} %copy.128), channel_id=1, source_target_pairs={{0,0},{17,1},{1,16},{16,17},{2,2},{19,3},{3,18},{18,19},{4,4},{21,... | collective-permute-start | bytes 7372808 | tf_op jit(solution)/shard_map/ppermute | solution.py:593
  1462.6 43.5 %collective-permute-start.39 = (bf16[3,256,1600]{1,2,0:T(8,128)(2,1)}, bf16[3,256,1600]{1,2,0:T(8,128)(2,1)}, u32[]{:S(2)}, u32[]{:S(2)}) collective-permute-start(bf16[3,256,1600]{1,2,0:T(8,128)(2,1)} %copy.132), channel_id=1, source_target_pairs={{0,16},{17,17},{1,0},{16,1},{2,18},{19,19},{3,2},{18,3},{4,20},{21... | collective-permute-start | bytes 7372808 | tf_op jit(solution)/shard_map/ppermute | solution.py:593
  1516.2 431.7 %collective-permute-start.83 = (bf16[1,104,1664]{2,1,0:T(8,128)(2,1)}, bf16[1,104,1664]{2,1,0:T(8,128)(2,1)}, u32[]{:S(2)}, u32[]{:S(2)}) collective-permute-start(bf16[1,104,1664]{2,1,0:T(8,128)(2,1)} %get-tuple-element.225), channel_id=1, source_target_pairs={{0,1},{1,0},{2,3},{3,2},{4,5},{5,4},{6,7},{7,6},{8,9},{9,8},{10,11... | collective-permute-start | bytes 1038344 | tf_op jit(solution)/shard_map/ppermute | solution.py:255
  1526.1 121.1 %collective-permute-start.74 = (bf16[3,256,1600]{1,2,0:T(8,128)(2,1)}, bf16[3,256,1600]{1,2,0:T(8,128)(2,1)}, u32[]{:S(2)}, u32[]{:S(2)}) collective-permute-start(bf16[3,256,1600]{1,2,0:T(8,128)(2,1)} %copy.153), channel_id=1, source_target_pairs={{0,16},{17,17},{1,0},{16,1},{2,18},{19,19},{3,2},{18,3},{4,20},{21... | collective-permute-start | bytes 7372808 | tf_op jit(solution)/shard_map/ppermute | solution.py:593
  1558.4 61.9 %collective-permute-start.61 = (bf16[1,256,1664]{2,1,0:T(8,128)(2,1)}, bf16[1,256,1664]{2,1,0:T(8,128)(2,1)}, u32[]{:S(2)}, u32[]{:S(2)}) collective-permute-start(bf16[1,256,1664]{2,1,0:T(8,128)(2,1)} %dynamic-slice_bitcast_fusion.10), channel_id=1, source_target_pairs={{0,16},{16,0},{1,17},{17,1},{2,18},{18,2},{3,19},{19,3},{4,20},{20... | collective-permute-start | bytes 2555912 | tf_op jit(solution)/shard_map/ppermute | solution.py:255
  1568.7 49.1 %collective-permute-start.58 = (bf16[2,256,1664]{2,1,0:T(8,128)(2,1)}, bf16[2,256,1664]{2,1,0:T(8,128)(2,1)}, u32[]{:S(2)}, u32[]{:S(2)}) collective-permute-start(bf16[2,256,1664]{2,1,0:T(8,128)(2,1)} %get-tuple-element.167), channel_id=1, source_target_pairs={{0,1},{1,0},{2,3},{3,2},{4,5},{5,4},{6,7},{7,6},{8,9},{9,8},{10,11... | collective-permute-start | bytes 5111816 | tf_op jit(solution)/shard_map/ppermute | solution.py:255
  1595.6 403.7 %reduce-scatter.19.cloned.1.call-start = ((), (), s32[]{:S(2)}) async-start(), calls=%async_computation.16 | async-start | bytes 3354624 | tf_op jit(solution)/shard_map/reduce_scatter | solution.py:674
  1631.2 42.7 %collective-permute-start.60 = (bf16[2,256,1664]{2,1,0:T(8,128)(2,1)}, bf16[2,256,1664]{2,1,0:T(8,128)(2,1)S(1)}, u32[]{:S(2)}, u32[]{:S(2)}) collective-permute-start(bf16[2,256,1664]{2,1,0:T(8,128)(2,1)} %get-tuple-element.146), channel_id=1, source_target_pairs={{0,16},{16,0},{1,17},{17,1},{2,18},{18,2},{3,19},{19,3},{4,20},{20... | collective-permute-start | bytes 5111816 | tf_op jit(solution)/shard_map/ppermute | solution.py:255
  1706.7 96.6 %collective-permute-start.67 = (bf16[2,512,1024]{2,1,0:T(8,128)(2,1)}, bf16[2,512,1024]{2,1,0:T(8,128)(2,1)}, u32[]{:S(2)}, u32[]{:S(2)}) collective-permute-start(bf16[2,512,1024]{2,1,0:T(8,128)(2,1)} %slice.747), channel_id=1, source_target_pairs={{2,0},{3,1},{6,4},{7,5},{10,8},{11,9},{14,12},{15,13},{18,16},{19,... | collective-permute-start | bytes 6291464 | tf_op jit(solution)/shard_map/ppermute | solution.py:375
  1715.5 58.7 %collective-permute-start.66 = (bf16[256,1600]{0,1:T(8,128)(2,1)}, bf16[256,1600]{0,1:T(8,128)(2,1)}, u32[]{:S(2)}, u32[]{:S(2)}) collective-permute-start(bf16[256,1600]{0,1:T(8,128)(2,1)} %copy.141), channel_id=1, source_target_pairs={{0,4},{4,0},{8,12},{12,8},{1,5},{5,1},{9,13},{13,9},{2,6},{6,2},{1... | collective-permute-start | bytes 2457608 | tf_op jit(solution)/shard_map/ppermute | solution.py:651
  1719.8 56.8 %collective-permute-start.65 = (bf16[256,1600]{0,1:T(8,128)(2,1)}, bf16[256,1600]{0,1:T(8,128)(2,1)}, u32[]{:S(2)}, u32[]{:S(2)}) collective-permute-start(bf16[256,1600]{0,1:T(8,128)(2,1)} %copy.140), channel_id=1, source_target_pairs={{0,8},{4,12},{8,0},{12,4},{1,9},{5,13},{9,1},{13,5},{2,10},{6,14},... | collective-permute-start | bytes 2457608 | tf_op jit(solution)/shard_map/ppermute | solution.py:651
  1722.6 73.1 %collective-permute-start.64 = (bf16[256,1600]{0,1:T(8,128)(2,1)}, bf16[256,1600]{0,1:T(8,128)(2,1)}, u32[]{:S(2)}, u32[]{:S(2)}) collective-permute-start(bf16[256,1600]{0,1:T(8,128)(2,1)} %copy.139), channel_id=1, source_target_pairs={{0,12},{4,8},{8,4},{12,0},{1,13},{5,9},{9,5},{13,1},{2,14},{6,10},... | collective-permute-start | bytes 2457608 | tf_op jit(solution)/shard_map/ppermute | solution.py:651
  1774.1 232.4 %collective-permute-start.80 = (bf16[1,104,896]{2,1,0:T(8,128)(2,1)}, bf16[1,104,896]{2,1,0:T(8,128)(2,1)}, u32[]{:S(2)}, u32[]{:S(2)}) collective-permute-start(bf16[1,104,896]{2,1,0:T(8,128)(2,1)} %get-tuple-element.253), channel_id=1, source_target_pairs={{0,1},{1,0},{2,3},{3,2},{4,5},{5,4},{6,7},{7,6},{8,9},{9,8},{10,11... | collective-permute-start | bytes 559112 | tf_op jit(solution)/shard_map/ppermute | solution.py:255
  1776.6 54.8 %collective-permute-start.78 = (bf16[1664,896]{1,0:T(8,128)(2,1)}, bf16[1664,896]{1,0:T(8,128)(2,1)}, u32[]{:S(2)}, u32[]{:S(2)}) collective-permute-start(bf16[1664,896]{1,0:T(8,128)(2,1)} %constant_dynamic-slice_fusion.4), channel_id=1, source_target_pairs={{0,16},{16,0},{1,17},{17,1},{2,18},{18,2},{3,19},{19,3},{4,20},{20... | collective-permute-start | bytes 8945672 | tf_op jit(solution)/shard_map/ppermute | solution.py:255
  1816.2 28.2 %collective-permute-start.68 = (bf16[2,256,1664]{2,1,0:T(8,128)(2,1)}, bf16[2,256,1664]{2,1,0:T(8,128)(2,1)}, u32[]{:S(2)}, u32[]{:S(2)}) collective-permute-start(bf16[2,256,1664]{2,1,0:T(8,128)(2,1)} %dynamic-slice_bitcast_fusion), channel_id=1, source_target_pairs={{0,16},{16,0},{1,17},{17,1},{2,18},{18,2},{3,19},{19,3},{4,20},{20... | collective-permute-start | bytes 5111816 | tf_op jit(solution)/shard_map/ppermute | solution.py:255
  1828.7 61.2 %collective-permute-start.71 = (bf16[1,256,1664]{2,1,0:T(8,128)(2,1)}, bf16[1,256,1664]{2,1,0:T(8,128)(2,1)}, u32[]{:S(2)}, u32[]{:S(2)}) collective-permute-start(bf16[1,256,1664]{2,1,0:T(8,128)(2,1)} %dynamic-slice_bitcast_fusion.9), channel_id=1, source_target_pairs={{0,16},{16,0},{1,17},{17,1},{2,18},{18,2},{3,19},{19,3},{4,20},{20... | collective-permute-start | bytes 2555912 | tf_op jit(solution)/shard_map/ppermute | solution.py:255
  1835.6 202.0 %reduce-scatter.17.cloned.1.call-start = ((), (), s32[]{:S(2)}) async-start(), calls=%async_computation.15 | async-start | bytes 5750784 | tf_op jit(solution)/shard_map/reduce_scatter | solution.py:674
  1848.3 39.1 %collective-permute-start.69 = (bf16[2,256,1664]{2,1,0:T(8,128)(2,1)}, bf16[2,256,1664]{2,1,0:T(8,128)(2,1)}, u32[]{:S(2)}, u32[]{:S(2)}) collective-permute-start(bf16[2,256,1664]{2,1,0:T(8,128)(2,1)} %get-tuple-element.161), channel_id=1, source_target_pairs={{0,1},{1,0},{2,3},{3,2},{4,5},{5,4},{6,7},{7,6},{8,9},{9,8},{10,11... | collective-permute-start | bytes 5111816 | tf_op jit(solution)/shard_map/ppermute | solution.py:255
  1931.8 108.3 %collective-permute-start.76 = (bf16[1,104,1536]{2,1,0:T(8,128)(2,1)}, bf16[1,104,1536]{2,1,0:T(8,128)(2,1)}, u32[]{:S(2)}, u32[]{:S(2)}) collective-permute-start(bf16[1,104,1536]{2,1,0:T(8,128)(2,1)} %get-tuple-element.249), channel_id=1, source_target_pairs={{0,1},{1,0},{2,3},{3,2},{4,5},{5,4},{6,7},{7,6},{8,9},{9,8},{10,11... | collective-permute-start | bytes 958472 | tf_op jit(solution)/shard_map/ppermute | solution.py:255
  1963.2 31.5 %collective-permute-start.73 = (bf16[3,256,1600]{1,2,0:T(8,128)(2,1)}, bf16[3,256,1600]{1,2,0:T(8,128)(2,1)}, u32[]{:S(2)}, u32[]{:S(2)}) collective-permute-start(bf16[3,256,1600]{1,2,0:T(8,128)(2,1)} %copy.152), channel_id=1, source_target_pairs={{0,0},{17,1},{1,16},{16,17},{2,2},{19,3},{3,18},{18,19},{4,4},{21,... | collective-permute-start | bytes 7372808 | tf_op jit(solution)/shard_map/ppermute | solution.py:593
  2007.9 32.1 %collective-permute-start.81 = (bf16[104,896]{1,0:T(8,128)(2,1)S(1)}, bf16[104,896]{1,0:T(8,128)(2,1)S(1)}, u32[]{:S(2)}, u32[]{:S(2)}) collective-permute-start(bf16[104,896]{1,0:T(8,128)(2,1)S(1)} %broadcast_select_fusion.27), channel_id=1, source_target_pairs={{0,16},{16,0},{1,17},{17,1},{2,18},{18,2},{3,19},{19,3},{4,20},{20... | collective-permute-start | bytes 559112 | tf_op jit(solution)/shard_map/ppermute | solution.py:255
  (283 other events, 5582.5 us)
Sparse Core Ops, SparseCore 0:
  13.5 91.1 all-gather.17
  107.5 119.7 all-gather.11
  230.0 97.5 all-gather.13
  344.3 63.2 all-gather.21
  441.6 87.2 all-gather.19
  636.7 106.6 all-gather.15
  830.3 92.7 all-gather.23
  940.5 106.9 reduce-scatter.10
  1146.1 73.7 reduce-scatter.8
  1223.7 120.5 reduce-scatter.12
  1424.9 99.4 reduce-scatter.14
  1528.2 106.6 reduce-scatter.20
  1638.9 160.3 reduce-scatter.22
  1835.8 87.2 reduce-scatter.18
  1926.6 110.9 reduce-scatter.16

commit v4 on v3

--- a/solution.py
+++ b/solution.py
@@ -674,6 +674,7 @@
         return lax.psum_scatter(value, groups, scatter_dimension=0, tiled=False)
 
     finished = [None, None]
+    small_rows = [None, None]
     token = ()
     sent_back = [None, None]
     for l in (1, 0):
@@ -723,6 +724,7 @@
             operands[turn].update(ops)
         d_qkv = product([ops["qkv"] for ops in operands])
         token = (d_qkv, out_done)
+        qkv_done = scattered(d_qkv, 2 * part_pad)
         returned = []
         for turn in turns:
             if l == 1 and turn == 1:
@@ -763,11 +765,19 @@
             axis=1,
         ).astype(BF16)
         small_cols = jnp.pad(small_cols, ((0, 0), (0, P_LANES - small_total)))[:, None, :]
-        d_qkv = d_qkv.reshape(chips, part_pad, P_LANES)
-        at_row = lax.broadcasted_iota(jnp.int32, (1, part_pad, 1), 1) == part
-        d_qkv = jnp.where(at_row, small_cols, d_qkv)
-        qkv_done = scattered(d_qkv, 2 * part_pad)
+        small_rows[l] = small_cols.reshape(all_groups, 2, P_LANES)
         finished[l] = {"up": up_done, "down": down_done, "qkv": qkv_done, "out": out_done}
+
+    small_done = jnp.concatenate(small_rows, axis=1).astype(F32)
+    for axis in groups:
+        count = lax.axis_size(axis)
+        for bit in range((count - 1).bit_length()):
+            small_done += lax.ppermute(small_done, axis, [(i, i ^ (1 << bit)) for i in range(count)])
+    small_done = pick(small_done, dp_index * y_count + y_index).astype(BF16).reshape(2, 2, 1, P_LANES)
+    spare = lax.broadcasted_iota(jnp.int32, (1, part_pad, 1), 1) == part
+    for l in range(2):
+        rows = finished[l]["qkv"].reshape(2, part_pad, P_LANES)
+        finished[l]["qkv"] = jnp.where(spare, small_done[l], rows).reshape(2 * part_pad, P_LANES)
 
     def back_across_pair(value):
         value = value.reshape(2, part_pad, value.shape[-1])

time: 2080 us -> 2080 us (level)
  waiting for transfers between devices: 846 us -> 814 us
  matrix products: 336 us -> 359 us
    ppermute x4, waiting for transfers between devices: 96.1 us -> 135 us  [own_rows(): other = lax.ppermute(grad[:, :rows, V_LANES:], 'y', [(1, 0)])]
    ppermute x4, waiting for transfers between devices: 33.1 us -> 0.01 us  [to_blocks(): return lax.ppermute(rows, CORE_X, pairs)]
    ppermute x3, waiting for transfers between devices: 39.1 us -> 17.7 us  [deal(): send = lax.ppermute(send, 'dp', [(i, i ^ d) for i in range(dp_count)])]
    unnamed x504 -> x524, local copies, waits for them, and re-layouts: 44.9 us -> 40 us
  transfers between devices with their start and end apart: 101 -> 104, of which waited for: 42 -> 40; matrix products, arithmetic and copies ran while one was open for 40% -> 41% of each run, Pallas kernels for 6% -> 6%
where the time goes in v4:
time: 2080 us; the launch traced here: 2070 us
  waiting for transfers between devices  814 us (39%)
  matrix products  359 us (17%)
  other arithmetic  290 us (14%)
  local copies, waits for them, and re-layouts  232 us (11%)
  starting transfers between devices  175 us (8%)
  Pallas kernels  123 us (6%)
  between operations  71.8 us (3%)
    ppermute x69, waiting for transfers between devices, flip(): return lax.ppermute(value, axis, [(0, 1), (1, 0)])  307 us
    all_gather x7, waiting for transfers between devices, gather(): return lax.all_gather(tied(piece, tokens), groups, axis=0)  203 us
    dot_general x16, matrix products, dot_0(): lax.dot_general(a.reshape(-1, a.shape[-1]), b.reshape(-1, b.shape[-1]), T...  144 us
    ppermute x4, waiting for transfers between devices, own_rows(): other = lax.ppermute(grad[:, :rows, V_LANES:], 'y', [(1, 0)])  135 us
    ppermute x4, waiting for transfers between devices, whole_sequence(): other = lax.ppermute(packed[..., V_LANES:], 'y', [(0, 1)])  133 us
    ppermute x69, starting transfers between devices, flip(): return lax.ppermute(value, axis, [(0, 1), (1, 0)])  117 us
    dot_general x16, matrix products, dot_t(): lax.dot_general(a.reshape(-1, a.shape[-1]), b, NT, preferred_element_type...  116 us
    dot_general x18, matrix products, dot(): flat = jnp.dot(a.reshape(-1, a.shape[-1]), b, preferred_element_type=F32)  98.9 us
  transfers between devices with their start and end apart: 104, of which 40 were waited for; matrix products, arithmetic and copies ran while one was open for 41% of the time, Pallas kernels for 6%

profile of v4, /device:TPU:1, one launch (start us, length us, event | category | flops | bytes accessed | tf_op | source)
XLA Modules:
  0.0 2066.0 jit_solution(4745733099068646276)
XLA Ops:
  27.0 11.0 collective-permute-done.2
  57.4 47.3 %all-gather.18.cloned.1.call-done = bf16[1664,1664]{1,0:T(8,128)(2,1)} async-done(((bf16[208,1664]{1,0:T(8,128)(2,1)}), bf16[1664,1664]{1,0:T(8,128)(2,1)}) %all-gather.18.cloned.1.call-update) | async-done | bytes 5537808 | tf_op jit(solution)/shard_map/all_gather | solution.py:531
  120.3 106.9 %all-gather.12.cloned.1.call-done = bf16[8,208,2432]{2,1,0:T(8,128)(2,1)} async-done(((bf16[1,208,2432]{2,1,0:T(8,128)(2,1)}), bf16[8,208,2432]{2,1,0:T(8,128)(2,1)}) %all-gather.12.cloned.1.call-update) | async-done | bytes 8093712 | tf_op jit(solution)/shard_map/all_gather | solution.py:531
  239.8 7.8 add_convert_fusion.11
  256.8 11.4 collective-permute-done.22
  271.0 56.8 %collective-permute-done.4 = bf16[2,512,1024]{2,1,0:T(8,128)(2,1)} collective-permute-done((bf16[2,512,1024]{2,1,0:T(8,128)(2,1)}, bf16[2,512,1024]{2,1,0:T(8,128)(2,1)}, u32[]{:S(2)}, u32[]{:S(2)}) %collective-permute-start.4) | collective-permute-done | bytes 2097184 | tf_op jit(solution)/shard_map/ppermute | solution.py:362
  358.5 49.1 %all-gather.22.cloned.1.call-done = bf16[1664,896]{1,0:T(8,128)(2,1)} async-done(((bf16[208,896]{1,0:T(8,128)(2,1)}), bf16[1664,896]{1,0:T(8,128)(2,1)}) %all-gather.22.cloned.1.call-update) | async-done | bytes 2981904 | tf_op jit(solution)/shard_map/all_gather | solution.py:531
  427.7 11.3 attn_fwd.4
  446.5 7.5 broadcast_select_fusion
  501.0 27.6 %collective-permute-done.7 = bf16[2,256,1664]{2,1,0:T(8,128)(2,1)S(1)} collective-permute-done((bf16[2,256,1664]{2,1,0:T(8,128)(2,1)S(1)}, bf16[2,256,1664]{2,1,0:T(8,128)(2,1)S(1)}, u32[]{:S(2)}, u32[]{:S(2)}) %collective-permute-start.7) | collective-permute-done | bytes 1703968 | tf_op jit(solution)/shard_map/ppermute | solution.py:255
  556.4 9.0 fusion.4
  597.0 26.7 %collective-permute-done.17 = bf16[2,256,1664]{2,1,0:T(8,128)(2,1)S(1)} collective-permute-done((bf16[2,256,1664]{2,1,0:T(8,128)(2,1)S(1)}, bf16[2,256,1664]{2,1,0:T(8,128)(2,1)S(1)}, u32[]{:S(2)}, u32[]{:S(2)}) %collective-permute-start.17) | collective-permute-done | bytes 1703968 | tf_op jit(solution)/shard_map/ppermute | solution.py:255
  636.8 11.3 collective-permute-done.20
  663.5 11.0 collective-permute-start.24
  688.0 58.7 %collective-permute-done.24 = bf16[2,512,1024]{2,1,0:T(8,128)(2,1)S(1)} collective-permute-done((bf16[2,512,1024]{2,1,0:T(8,128)(2,1)S(1)}, bf16[2,512,1024]{2,1,0:T(8,128)(2,1)S(1)}, u32[]{:S(2)}, u32[]{:S(2)}) %collective-permute-start.24) | collective-permute-done | bytes 2097184 | tf_op jit(solution)/shard_map/ppermute | solution.py:362
  752.3 11.9 attn_fwd.6
  775.3 12.1 collective-permute-start.32
  790.2 17.6 collective-permute-done.32
  830.7 18.9 collective-permute-done.27
  864.0 11.2 collective-permute-done.34
  906.7 8.3 fusion.286
  915.0 9.5 fusion.9
  924.5 11.3 add_convert_fusion.3
  940.5 10.1 fusion.65
  952.6 14.8 convert_reduce_fusion
  967.4 8.7 convolution_convert_fusion.3
  985.0 8.1 convert_reduce_fusion.6
  993.1 22.1 %collective-permute-done.35 = bf16[2,256,1664]{2,1,0:T(8,128)(2,1)S(1)} collective-permute-done((bf16[2,256,1664]{2,1,0:T(8,128)(2,1)S(1)}, bf16[2,256,1664]{2,1,0:T(8,128)(2,1)S(1)}, u32[]{:S(2)}, u32[]{:S(2)}) %collective-permute-start.35) | collective-permute-done | bytes 1703968 | tf_op jit(solution)/shard_map/ppermute | solution.py:255
  1040.5 13.1 add_convert_fusion.2
  1055.6 21.5 %collective-permute-done.43 = bf16[2,256,1664]{2,1,0:T(8,128)(2,1)S(1)} collective-permute-done((bf16[2,256,1664]{2,1,0:T(8,128)(2,1)}, bf16[2,256,1664]{2,1,0:T(8,128)(2,1)S(1)}, u32[]{:S(2)}, u32[]{:S(2)}) %collective-permute-start.43) | collective-permute-done | bytes 1703968 | tf_op jit(solution)/shard_map/ppermute | solution.py:255
  1083.6 14.5 collective-permute-done.46
  1121.7 10.6 convolution_convert_fusion.1
  1152.8 12.7 attn_bwd.4
  1173.8 22.7 %attn_bwd.5 = bf16[2,1024,1536]{2,1,0:T(8,128)(2,1)} custom-call(s32[3]{0:T(128)} %broadcast_add_fusion.20.info_ref, bf16[2,1024,1536]{2,1,0:T(8,128)(2,1)} %bitcast_select_fusion.q_ref.k_ref.v_ref, bf16[2,1024,1536]{2,1,0:T(8,128)(2,1)} %bitcast_select_fusion.q_ref.k_ref.v_ref, bf16[2,1024,1536]{2,1,0:T(8,128)(2,1)} %bitcast_select_fusion.q_ref.k_ref.v_ref, ...), custom_call_target="tpu_custom_call" | custom-call | tf_op jit(solution)/shard_map/attn_bwd/pallas_call | solution.py:231
  1200.8 74.8 %collective-permute-done.49 = bf16[2,512,1024]{2,1,0:T(8,128)(2,1)S(1)} collective-permute-done((bf16[2,512,1024]{2,1,0:T(8,128)(2,1)}, bf16[2,512,1024]{2,1,0:T(8,128)(2,1)S(1)}, u32[]{:S(2)}, u32[]{:S(2)}) %collective-permute-start.49) | collective-permute-done | bytes 2097184 | tf_op jit(solution)/shard_map/ppermute | solution.py:375
  1278.7 9.8 fusion.59
  1313.5 17.5 collective-permute-done.52
  1346.9 9.0 fusion.199
  1355.8 10.5 collective-permute-done.51
  1371.4 7.6 collective-permute-start.57
  1379.0 9.9 add_convert_fusion.5
  1396.7 15.5 collective-permute-done.57
  1443.8 12.9 convert_reduce_fusion.1
  1456.7 12.6 add_convert_fusion
  1517.6 9.9 convolution_convert_fusion.2
  1536.4 8.0 fusion.289
  1546.9 17.6 collective-permute-start.58
  1564.5 10.1 add_convert_fusion.1
  1579.7 22.1 %collective-permute-done.58 = bf16[2,256,1664]{2,1,0:T(8,128)(2,1)} collective-permute-done((bf16[2,256,1664]{2,1,0:T(8,128)(2,1)}, bf16[2,256,1664]{2,1,0:T(8,128)(2,1)}, u32[]{:S(2)}, u32[]{:S(2)}) %collective-permute-start.58) | collective-permute-done | bytes 1703968 | tf_op jit(solution)/shard_map/ppermute | solution.py:255
  1617.0 8.5 collective-permute-done.62
  1654.7 10.7 convolution_convert_fusion
  1692.5 13.1 attn_bwd.6
  1715.5 22.8 %attn_bwd.7 = bf16[2,1024,1536]{2,1,0:T(8,128)(2,1)} custom-call(s32[3]{0:T(128)} %broadcast_add_fusion.19.info_ref, bf16[2,1024,1536]{2,1,0:T(8,128)(2,1)} %bitcast_select_fusion.1.q_ref.k_ref.v_ref, bf16[2,1024,1536]{2,1,0:T(8,128)(2,1)} %bitcast_select_fusion.1.q_ref.k_ref.v_ref, bf16[2,1024,1536]{2,1,0:T(8,128)(2,1)} %bitcast_select_fusion.1.q_ref.k_ref.v_ref, ...), custom_call_target="tpu_custom_call" | custom-call | tf_op jit(solution)/shard_map/attn_bwd/pallas_call | solution.py:231
  1744.0 17.7 collective-permute-done.65
  1785.7 30.1 %collective-permute-done.67 = bf16[2,512,1024]{2,1,0:T(8,128)(2,1)} collective-permute-done((bf16[2,512,1024]{2,1,0:T(8,128)(2,1)}, bf16[2,512,1024]{2,1,0:T(8,128)(2,1)}, u32[]{:S(2)}, u32[]{:S(2)}) %collective-permute-start.67) | collective-permute-done | bytes 2097184 | tf_op jit(solution)/shard_map/ppermute | solution.py:375
  1819.6 10.0 fusion.56
  1835.7 12.4 collective-permute-done.70
  1859.5 8.0 fusion.195
  1873.0 11.5 add_convert_fusion.4
  1884.5 25.9 %collective-permute-done.69 = bf16[2,256,1664]{2,1,0:T(8,128)(2,1)} collective-permute-done((bf16[2,256,1664]{2,1,0:T(8,128)(2,1)}, bf16[2,256,1664]{2,1,0:T(8,128)(2,1)}, u32[]{:S(2)}, u32[]{:S(2)}) %collective-permute-start.69) | collective-permute-done | bytes 1703968 | tf_op jit(solution)/shard_map/ppermute | solution.py:255
  1934.0 8.4 collective-permute-done.85
  1970.3 14.8 collective-permute-done.76
  1998.0 8.2 reshape.2770
  2033.0 7.6 collective-permute-done.78
  (1261 shorter events, 823.5 us)
Async XLA Ops:
  7.2 97.6 %all-gather.18.cloned.1.call-start = ((), (), s32[]{:S(2)}) async-start(), calls=%async_computation.19 | async-start | bytes 6230016 | tf_op jit(solution)/shard_map/all_gather | solution.py:531
  13.4 213.8 %all-gather.12.cloned.1.call-start = ((), (), s32[]{:S(2)}) async-start(), calls=%async_computation.8 | async-start | bytes 9105408 | tf_op jit(solution)/shard_map/all_gather | solution.py:531
  39.3 300.5 %all-gather.14.cloned.1.call-start = ((), (), s32[]{:S(2)}) async-start(), calls=%async_computation.9 | async-start | bytes 6230016 | tf_op jit(solution)/shard_map/all_gather | solution.py:531
  54.7 52.5 %collective-permute-start.10 = (bf16[1,104,1664]{2,1,0:T(8,128)(2,1)}, bf16[1,104,1664]{2,1,0:T(8,128)(2,1)}, u32[]{:S(2)}, u32[]{:S(2)}) collective-permute-start(bf16[1,104,1664]{2,1,0:T(8,128)(2,1)} %get-tuple-element.229), channel_id=1, source_target_pairs={{0,1},{1,0},{2,3},{3,2},{4,5},{5,4},{6,7},{7,6},{8,9},{9,8},{10,11... | collective-permute-start | bytes 1038344 | tf_op jit(solution)/shard_map/ppermute | solution.py:255
  56.1 54.5 %collective-permute-start = (bf16[3,256,1600]{1,2,0:T(8,128)(2,1)S(1)}, bf16[3,256,1600]{1,2,0:T(8,128)(2,1)}, u32[]{:S(2)}, u32[]{:S(2)}) collective-permute-start(bf16[3,256,1600]{1,2,0:T(8,128)(2,1)S(1)} %copy-done.121), channel_id=1, source_target_pairs={{0,1},{17,16},{2,3},{19,18},{4,5},{21,20},{6,7},{23,22},{8,9},{25,... | collective-permute-start | bytes 7372808 | tf_op jit(solution)/shard_map/ppermute | solution.py:586
  110.3 297.3 %all-gather.22.cloned.1.call-start = ((), (), s32[]{:S(2)}) async-start(), calls=%async_computation.21 | async-start | bytes 3354624 | tf_op jit(solution)/shard_map/all_gather | solution.py:531
  250.9 76.8 %collective-permute-start.4 = (bf16[2,512,1024]{2,1,0:T(8,128)(2,1)}, bf16[2,512,1024]{2,1,0:T(8,128)(2,1)}, u32[]{:S(2)}, u32[]{:S(2)}) collective-permute-start(bf16[2,512,1024]{2,1,0:T(8,128)(2,1)} %slice.688), channel_id=1, source_target_pairs={{0,2},{1,3},{4,6},{5,7},{8,10},{9,11},{12,14},{13,15},{16,18},{17,... | collective-permute-start | bytes 6291464 | tf_op jit(solution)/shard_map/ppermute | solution.py:362
  344.1 202.6 %all-gather.20.cloned.1.call-start = ((), (), s32[]{:S(2)}) async-start(), calls=%async_computation.20 | async-start | bytes 5750784 | tf_op jit(solution)/shard_map/all_gather | solution.py:531
  350.0 284.4 %collective-permute-start.29 = (bf16[1,104,1664]{2,1,0:T(8,128)(2,1)}, bf16[1,104,1664]{2,1,0:T(8,128)(2,1)}, u32[]{:S(2)}, u32[]{:S(2)}) collective-permute-start(bf16[1,104,1664]{2,1,0:T(8,128)(2,1)} %get-tuple-element.227), channel_id=1, source_target_pairs={{0,1},{1,0},{2,3},{3,2},{4,5},{5,4},{6,7},{7,6},{8,9},{9,8},{10,11... | collective-permute-start | bytes 1038344 | tf_op jit(solution)/shard_map/ppermute | solution.py:255
  355.6 90.9 %collective-permute-start.5 = (bf16[1664,896]{1,0:T(8,128)(2,1)}, bf16[1664,896]{1,0:T(8,128)(2,1)}, u32[]{:S(2)}, u32[]{:S(2)}) collective-permute-start(bf16[1664,896]{1,0:T(8,128)(2,1)} %slice.689), channel_id=1, source_target_pairs={{0,16},{16,0},{1,17},{17,1},{2,18},{18,2},{3,19},{19,3},{4,20},{20... | collective-permute-start | bytes 8945672 | tf_op jit(solution)/shard_map/ppermute | solution.py:255
  407.6 38.9 %collective-permute-start.25 = (bf16[1664,896]{1,0:T(8,128)(2,1)}, bf16[1664,896]{1,0:T(8,128)(2,1)}, u32[]{:S(2)}, u32[]{:S(2)}) collective-permute-start(bf16[1664,896]{1,0:T(8,128)(2,1)} %all-gather.22.cloned.1.call-done), channel_id=1, source_target_pairs={{0,16},{16,0},{1,17},{17,1},{2,18},{18,2},{3,19},{19,3},{4,20},{20... | collective-permute-start | bytes 8945672 | tf_op jit(solution)/shard_map/ppermute | solution.py:255
  424.4 42.6 %collective-permute-start.14 = (bf16[1,512,1024]{2,1,0:T(8,128)(2,1)}, bf16[1,512,1024]{2,1,0:T(8,128)(2,1)}, u32[]{:S(2)}, u32[]{:S(2)}) collective-permute-start(bf16[1,512,1024]{2,1,0:T(8,128)(2,1)} %slice.702), channel_id=1, source_target_pairs={{0,2},{1,3},{4,6},{5,7},{8,10},{9,11},{12,14},{13,15},{16,18},{17,... | collective-permute-start | bytes 3145736 | tf_op jit(solution)/shard_map/ppermute | solution.py:362
  441.5 458.4 %all-gather.16.cloned.1.call-start = ((), (), s32[]{:S(2)}) async-start(), calls=%async_computation.10 | async-start | bytes 6230016 | tf_op jit(solution)/shard_map/all_gather | solution.py:531
  490.9 37.7 %collective-permute-start.7 = (bf16[2,256,1664]{2,1,0:T(8,128)(2,1)S(1)}, bf16[2,256,1664]{2,1,0:T(8,128)(2,1)S(1)}, u32[]{:S(2)}, u32[]{:S(2)}) collective-permute-start(bf16[2,256,1664]{2,1,0:T(8,128)(2,1)S(1)} %fusion.125), channel_id=1, source_target_pairs={{0,1},{1,0},{2,3},{3,2},{4,5},{5,4},{6,7},{7,6},{8,9},{9,8},{10,11... | collective-permute-start | bytes 5111816 | tf_op jit(solution)/shard_map/ppermute | solution.py:255
  492.5 158.2 %collective-permute-start.41 = (bf16[2,256,1664]{2,1,0:T(8,128)(2,1)}, bf16[2,256,1664]{2,1,0:T(8,128)(2,1)}, u32[]{:S(2)}, u32[]{:S(2)}) collective-permute-start(bf16[2,256,1664]{2,1,0:T(8,128)(2,1)} %select_convert_fusion.1), channel_id=1, source_target_pairs={{0,16},{16,0},{1,17},{17,1},{2,18},{18,2},{3,19},{19,3},{4,20},{20... | collective-permute-start | bytes 5111816 | tf_op jit(solution)/shard_map/ppermute | solution.py:255
  496.8 33.6 %collective-permute-start.15 = (bf16[1,256,1664]{2,1,0:T(8,128)(2,1)S(1)}, bf16[1,256,1664]{2,1,0:T(8,128)(2,1)S(1)}, u32[]{:S(2)}, u32[]{:S(2)}) collective-permute-start(bf16[1,256,1664]{2,1,0:T(8,128)(2,1)S(1)} %dynamic-slice_bitcast_fusion.16), channel_id=1, source_target_pairs={{0,16},{16,0},{1,17},{17,1},{2,18},{18,2},{3,19},{19,3},{4,20},{20... | collective-permute-start | bytes 2555912 | tf_op jit(solution)/shard_map/ppermute | solution.py:255
  498.8 185.2 %collective-permute-start.44 = (bf16[1,256,1664]{2,1,0:T(8,128)(2,1)}, bf16[1,256,1664]{2,1,0:T(8,128)(2,1)}, u32[]{:S(2)}, u32[]{:S(2)}) collective-permute-start(bf16[1,256,1664]{2,1,0:T(8,128)(2,1)} %bitcast.169), channel_id=1, source_target_pairs={{0,16},{16,0},{1,17},{17,1},{2,18},{18,2},{3,19},{19,3},{4,20},{20... | collective-permute-start | bytes 2555912 | tf_op jit(solution)/shard_map/ppermute | solution.py:255
  585.4 38.3 %collective-permute-start.17 = (bf16[2,256,1664]{2,1,0:T(8,128)(2,1)S(1)}, bf16[2,256,1664]{2,1,0:T(8,128)(2,1)S(1)}, u32[]{:S(2)}, u32[]{:S(2)}) collective-permute-start(bf16[2,256,1664]{2,1,0:T(8,128)(2,1)S(1)} %broadcast_add_fusion.8), channel_id=1, source_target_pairs={{0,1},{1,0},{2,3},{3,2},{4,5},{5,4},{6,7},{7,6},{8,9},{9,8},{10,11... | collective-permute-start | bytes 5111816 | tf_op jit(solution)/shard_map/ppermute | solution.py:255
  596.1 31.4 %collective-permute-start.19 = (bf16[1,256,1664]{2,1,0:T(8,128)(2,1)S(1)}, bf16[1,256,1664]{2,1,0:T(8,128)(2,1)S(1)}, u32[]{:S(2)}, u32[]{:S(2)}) collective-permute-start(bf16[1,256,1664]{2,1,0:T(8,128)(2,1)S(1)} %dynamic-slice_bitcast_fusion.15), channel_id=1, source_target_pairs={{0,16},{16,0},{1,17},{17,1},{2,18},{18,2},{3,19},{19,3},{4,20},{20... | collective-permute-start | bytes 2555912 | tf_op jit(solution)/shard_map/ppermute | solution.py:255
  636.6 303.9 %all-gather.24.cloned.1.call-start = ((), (), s32[]{:S(2)}) async-start(), calls=%async_computation.22 | async-start | bytes 6230016 | tf_op jit(solution)/shard_map/all_gather | solution.py:531
  663.5 83.1 %collective-permute-start.24 = (bf16[2,512,1024]{2,1,0:T(8,128)(2,1)S(1)}, bf16[2,512,1024]{2,1,0:T(8,128)(2,1)S(1)}, u32[]{:S(2)}, u32[]{:S(2)}) collective-permute-start(bf16[2,512,1024]{2,1,0:T(8,128)(2,1)S(1)} %slice.714), channel_id=1, source_target_pairs={{0,2},{1,3},{4,6},{5,7},{8,10},{9,11},{12,14},{13,15},{16,18},{17,... | collective-permute-start | bytes 6291464 | tf_op jit(solution)/shard_map/ppermute | solution.py:362
  767.7 41.4 %collective-permute-start.26 = (bf16[2,256,1664]{2,1,0:T(8,128)(2,1)}, bf16[2,256,1664]{2,1,0:T(8,128)(2,1)S(1)}, u32[]{:S(2)}, u32[]{:S(2)}) collective-permute-start(bf16[2,256,1664]{2,1,0:T(8,128)(2,1)} %dynamic-slice_bitcast_fusion.5), channel_id=1, source_target_pairs={{0,16},{16,0},{1,17},{17,1},{2,18},{18,2},{3,19},{19,3},{4,20},{20... | collective-permute-start | bytes 5111816 | tf_op jit(solution)/shard_map/ppermute | solution.py:255
  775.3 32.5 %collective-permute-start.32 = (bf16[1,512,1024]{2,1,0:T(8,128)(2,1)}, bf16[1,512,1024]{2,1,0:T(8,128)(2,1)}, u32[]{:S(2)}, u32[]{:S(2)}) collective-permute-start(bf16[1,512,1024]{2,1,0:T(8,128)(2,1)} %slice.725), channel_id=1, source_target_pairs={{0,2},{1,3},{4,6},{5,7},{8,10},{9,11},{12,14},{13,15},{16,18},{17,... | collective-permute-start | bytes 3145736 | tf_op jit(solution)/shard_map/ppermute | solution.py:362
  812.9 36.7 %collective-permute-start.27 = (bf16[2,256,1664]{2,1,0:T(8,128)(2,1)}, bf16[2,256,1664]{2,1,0:T(8,128)(2,1)}, u32[]{:S(2)}, u32[]{:S(2)}) collective-permute-start(bf16[2,256,1664]{2,1,0:T(8,128)(2,1)} %broadcast_add_fusion.7), channel_id=1, source_target_pairs={{0,1},{1,0},{2,3},{3,2},{4,5},{5,4},{6,7},{7,6},{8,9},{9,8},{10,11... | collective-permute-start | bytes 5111816 | tf_op jit(solution)/shard_map/ppermute | solution.py:255
  824.5 31.8 %collective-permute-start.33 = (bf16[1,256,1664]{2,1,0:T(8,128)(2,1)}, bf16[1,256,1664]{2,1,0:T(8,128)(2,1)}, u32[]{:S(2)}, u32[]{:S(2)}) collective-permute-start(bf16[1,256,1664]{2,1,0:T(8,128)(2,1)} %dynamic-slice_bitcast_fusion.14), channel_id=1, source_target_pairs={{0,16},{16,0},{1,17},{17,1},{2,18},{18,2},{3,19},{19,3},{4,20},{20... | collective-permute-start | bytes 2555912 | tf_op jit(solution)/shard_map/ppermute | solution.py:255
  830.5 473.5 %reduce-scatter.11.cloned.1.call-start = ((), (), s32[]{:S(2)}) async-start(), calls=%async_computation.12 | async-start | bytes 6230016 | tf_op jit(solution)/shard_map/reduce_scatter | solution.py:674
  860.5 35.4 %collective-permute-start.28 = (bf16[2,256,1664]{2,1,0:T(8,128)(2,1)}, bf16[2,256,1664]{2,1,0:T(8,128)(2,1)}, u32[]{:S(2)}, u32[]{:S(2)}) collective-permute-start(bf16[2,256,1664]{2,1,0:T(8,128)(2,1)} %add_convert_fusion.18), channel_id=1, source_target_pairs={{0,16},{16,0},{1,17},{17,1},{2,18},{18,2},{3,19},{19,3},{4,20},{20... | collective-permute-start | bytes 5111816 | tf_op jit(solution)/shard_map/ppermute | solution.py:255
  940.0 474.5 %reduce-scatter.9.cloned.1.call-start = ((), (), s32[]{:S(2)}) async-start(), calls=%async_computation.11 | async-start | bytes 3354624 | tf_op jit(solution)/shard_map/reduce_scatter | solution.py:674
  976.2 62.3 %collective-permute-start.42 = (bf16[2,256,1664]{2,1,0:T(8,128)(2,1)S(1)}, bf16[2,256,1664]{2,1,0:T(8,128)(2,1)S(1)}, u32[]{:S(2)}, u32[]{:S(2)}) collective-permute-start(bf16[2,256,1664]{2,1,0:T(8,128)(2,1)S(1)} %dynamic-slice_bitcast_fusion.3), channel_id=1, source_target_pairs={{0,16},{16,0},{1,17},{17,1},{2,18},{18,2},{3,19},{19,3},{4,20},{20... | collective-permute-start | bytes 5111816 | tf_op jit(solution)/shard_map/ppermute | solution.py:255
  976.9 38.4 %collective-permute-start.35 = (bf16[2,256,1664]{2,1,0:T(8,128)(2,1)S(1)}, bf16[2,256,1664]{2,1,0:T(8,128)(2,1)S(1)}, u32[]{:S(2)}, u32[]{:S(2)}) collective-permute-start(bf16[2,256,1664]{2,1,0:T(8,128)(2,1)S(1)} %broadcast_add_fusion.6), channel_id=1, source_target_pairs={{0,1},{1,0},{2,3},{3,2},{4,5},{5,4},{6,7},{7,6},{8,9},{9,8},{10,11... | collective-permute-start | bytes 5111816 | tf_op jit(solution)/shard_map/ppermute | solution.py:255
  984.9 32.2 %collective-permute-start.37 = (bf16[1,256,1664]{2,1,0:T(8,128)(2,1)S(1)}, bf16[1,256,1664]{2,1,0:T(8,128)(2,1)S(1)}, u32[]{:S(2)}, u32[]{:S(2)}) collective-permute-start(bf16[1,256,1664]{2,1,0:T(8,128)(2,1)S(1)} %dynamic-slice_bitcast_fusion.13), channel_id=1, source_target_pairs={{0,16},{16,0},{1,17},{17,1},{2,18},{18,2},{3,19},{19,3},{4,20},{20... | collective-permute-start | bytes 2555912 | tf_op jit(solution)/shard_map/ppermute | solution.py:255
  1024.9 54.1 %collective-permute-start.45 = (bf16[1,256,1664]{2,1,0:T(8,128)(2,1)}, bf16[1,256,1664]{2,1,0:T(8,128)(2,1)}, u32[]{:S(2)}, u32[]{:S(2)}) collective-permute-start(bf16[1,256,1664]{2,1,0:T(8,128)(2,1)} %dynamic-slice_bitcast_fusion.12), channel_id=1, source_target_pairs={{0,16},{16,0},{1,17},{17,1},{2,18},{18,2},{3,19},{19,3},{4,20},{20... | collective-permute-start | bytes 2555912 | tf_op jit(solution)/shard_map/ppermute | solution.py:255
  1040.4 36.8 %collective-permute-start.43 = (bf16[2,256,1664]{2,1,0:T(8,128)(2,1)}, bf16[2,256,1664]{2,1,0:T(8,128)(2,1)S(1)}, u32[]{:S(2)}, u32[]{:S(2)}) collective-permute-start(bf16[2,256,1664]{2,1,0:T(8,128)(2,1)} %get-tuple-element.175), channel_id=1, source_target_pairs={{0,1},{1,0},{2,3},{3,2},{4,5},{5,4},{6,7},{7,6},{8,9},{9,8},{10,11... | collective-permute-start | bytes 5111816 | tf_op jit(solution)/shard_map/ppermute | solution.py:255
  1147.0 350.5 %reduce-scatter.13.cloned.1.call-start = ((), (), s32[]{:S(2)}) async-start(), calls=%async_computation.13 | async-start | bytes 6230016 | tf_op jit(solution)/shard_map/reduce_scatter | solution.py:674
  1147.6 488.5 %reduce-scatter.15.cloned.1.call-start = ((), (), s32[]{:S(2)}) async-start(), calls=%async_computation.14 | async-start | bytes 5750784 | tf_op jit(solution)/shard_map/reduce_scatter | solution.py:674
  1199.5 76.1 %collective-permute-start.49 = (bf16[2,512,1024]{2,1,0:T(8,128)(2,1)}, bf16[2,512,1024]{2,1,0:T(8,128)(2,1)S(1)}, u32[]{:S(2)}, u32[]{:S(2)}) collective-permute-start(bf16[2,512,1024]{2,1,0:T(8,128)(2,1)} %slice.740), channel_id=1, source_target_pairs={{2,0},{3,1},{6,4},{7,5},{10,8},{11,9},{14,12},{15,13},{18,16},{19,... | collective-permute-start | bytes 6291464 | tf_op jit(solution)/shard_map/ppermute | solution.py:375
  1294.5 36.5 %collective-permute-start.52 = (bf16[1,512,1024]{2,1,0:T(8,128)(2,1)}, bf16[1,512,1024]{2,1,0:T(8,128)(2,1)}, u32[]{:S(2)}, u32[]{:S(2)}) collective-permute-start(bf16[1,512,1024]{2,1,0:T(8,128)(2,1)} %slice.742), channel_id=1, source_target_pairs={{2,0},{3,1},{6,4},{7,5},{10,8},{11,9},{14,12},{15,13},{18,16},{19,... | collective-permute-start | bytes 3145736 | tf_op jit(solution)/shard_map/ppermute | solution.py:375
  1301.8 180.0 %collective-permute-start.21 = (bf16[3,256,1600]{1,2,0:T(8,128)(2,1)}, bf16[3,256,1600]{1,2,0:T(8,128)(2,1)}, u32[]{:S(2)}, u32[]{:S(2)}) collective-permute-start(bf16[3,256,1600]{1,2,0:T(8,128)(2,1)} %copy.128), channel_id=1, source_target_pairs={{0,0},{17,1},{1,16},{16,17},{2,2},{19,3},{3,18},{18,19},{4,4},{21,... | collective-permute-start | bytes 7372808 | tf_op jit(solution)/shard_map/ppermute | solution.py:593
  1313.5 52.9 %collective-permute-start.51 = (bf16[2,256,1664]{2,1,0:T(8,128)(2,1)}, bf16[2,256,1664]{2,1,0:T(8,128)(2,1)}, u32[]{:S(2)}, u32[]{:S(2)}) collective-permute-start(bf16[2,256,1664]{2,1,0:T(8,128)(2,1)} %get-tuple-element.171), channel_id=1, source_target_pairs={{0,1},{1,0},{2,3},{3,2},{4,5},{5,4},{6,7},{7,6},{8,9},{9,8},{10,11... | collective-permute-start | bytes 5111816 | tf_op jit(solution)/shard_map/ppermute | solution.py:255
  1343.8 145.1 %collective-permute-start.39 = (bf16[3,256,1600]{1,2,0:T(8,128)(2,1)}, bf16[3,256,1600]{1,2,0:T(8,128)(2,1)}, u32[]{:S(2)}, u32[]{:S(2)}) collective-permute-start(bf16[3,256,1600]{1,2,0:T(8,128)(2,1)} %copy.132), channel_id=1, source_target_pairs={{0,16},{17,17},{1,0},{16,1},{2,18},{19,19},{3,2},{18,3},{4,20},{21... | collective-permute-start | bytes 7372808 | tf_op jit(solution)/shard_map/ppermute | solution.py:593
  1371.4 40.9 %collective-permute-start.57 = (bf16[1,256,1664]{2,1,0:T(8,128)(2,1)}, bf16[1,256,1664]{2,1,0:T(8,128)(2,1)}, u32[]{:S(2)}, u32[]{:S(2)}) collective-permute-start(bf16[1,256,1664]{2,1,0:T(8,128)(2,1)} %get-tuple-element.169), channel_id=1, source_target_pairs={{0,1},{1,0},{2,3},{3,2},{4,5},{5,4},{6,7},{7,6},{8,9},{9,8},{10,11... | collective-permute-start | bytes 2555912 | tf_op jit(solution)/shard_map/ppermute | solution.py:255
  1393.1 534.1 %reduce-scatter.21.cloned.1.call-start = ((), (), s32[]{:S(2)}) async-start(), calls=%async_computation.17 | async-start | bytes 6230016 | tf_op jit(solution)/shard_map/reduce_scatter | solution.py:674
  1469.4 460.2 %reduce-scatter.23.cloned.1.call-start = ((), (), s32[]{:S(2)}) async-start(), calls=%async_computation.18 | async-start | bytes 6230016 | tf_op jit(solution)/shard_map/reduce_scatter | solution.py:674
  1499.6 434.4 %collective-permute-start.86 = (bf16[1,104,1664]{2,1,0:T(8,128)(2,1)}, bf16[1,104,1664]{2,1,0:T(8,128)(2,1)}, u32[]{:S(2)}, u32[]{:S(2)}) collective-permute-start(bf16[1,104,1664]{2,1,0:T(8,128)(2,1)} %get-tuple-element.225), channel_id=1, source_target_pairs={{0,1},{1,0},{2,3},{3,2},{4,5},{5,4},{6,7},{7,6},{8,9},{9,8},{10,11... | collective-permute-start | bytes 1038344 | tf_op jit(solution)/shard_map/ppermute | solution.py:255
  1509.7 121.7 %collective-permute-start.74 = (bf16[3,256,1600]{1,2,0:T(8,128)(2,1)}, bf16[3,256,1600]{1,2,0:T(8,128)(2,1)}, u32[]{:S(2)}, u32[]{:S(2)}) collective-permute-start(bf16[3,256,1600]{1,2,0:T(8,128)(2,1)} %copy.153), channel_id=1, source_target_pairs={{0,16},{17,17},{1,0},{16,1},{2,18},{19,19},{3,2},{18,3},{4,20},{21... | collective-permute-start | bytes 7372808 | tf_op jit(solution)/shard_map/ppermute | solution.py:593
  1536.4 67.9 %collective-permute-start.61 = (bf16[1,256,1664]{2,1,0:T(8,128)(2,1)}, bf16[1,256,1664]{2,1,0:T(8,128)(2,1)}, u32[]{:S(2)}, u32[]{:S(2)}) collective-permute-start(bf16[1,256,1664]{2,1,0:T(8,128)(2,1)} %dynamic-slice_bitcast_fusion.10), channel_id=1, source_target_pairs={{0,16},{16,0},{1,17},{17,1},{2,18},{18,2},{3,19},{19,3},{4,20},{20... | collective-permute-start | bytes 2555912 | tf_op jit(solution)/shard_map/ppermute | solution.py:255
  1546.9 54.9 %collective-permute-start.58 = (bf16[2,256,1664]{2,1,0:T(8,128)(2,1)}, bf16[2,256,1664]{2,1,0:T(8,128)(2,1)}, u32[]{:S(2)}, u32[]{:S(2)}) collective-permute-start(bf16[2,256,1664]{2,1,0:T(8,128)(2,1)} %get-tuple-element.167), channel_id=1, source_target_pairs={{0,1},{1,0},{2,3},{3,2},{4,5},{5,4},{6,7},{7,6},{8,9},{9,8},{10,11... | collective-permute-start | bytes 5111816 | tf_op jit(solution)/shard_map/ppermute | solution.py:255
  1579.6 431.2 %reduce-scatter.19.cloned.1.call-start = ((), (), s32[]{:S(2)}) async-start(), calls=%async_computation.16 | async-start | bytes 3354624 | tf_op jit(solution)/shard_map/reduce_scatter | solution.py:674
  1615.2 33.8 %collective-permute-start.60 = (bf16[2,256,1664]{2,1,0:T(8,128)(2,1)}, bf16[2,256,1664]{2,1,0:T(8,128)(2,1)}, u32[]{:S(2)}, u32[]{:S(2)}) collective-permute-start(bf16[2,256,1664]{2,1,0:T(8,128)(2,1)} %get-tuple-element.146), channel_id=1, source_target_pairs={{0,16},{16,0},{1,17},{17,1},{2,18},{18,2},{3,19},{19,3},{4,20},{20... | collective-permute-start | bytes 5111816 | tf_op jit(solution)/shard_map/ppermute | solution.py:255
  1669.2 103.4 %collective-permute-start.81 = (bf16[1664,896]{1,0:T(8,128)(2,1)}, bf16[1664,896]{1,0:T(8,128)(2,1)}, u32[]{:S(2)}, u32[]{:S(2)}) collective-permute-start(bf16[1664,896]{1,0:T(8,128)(2,1)} %constant_dynamic-slice_fusion.4), channel_id=1, source_target_pairs={{0,16},{16,0},{1,17},{17,1},{2,18},{18,2},{3,19},{19,3},{4,20},{20... | collective-permute-start | bytes 8945672 | tf_op jit(solution)/shard_map/ppermute | solution.py:255
  1681.5 59.8 %collective-permute-start.66 = (bf16[256,1600]{0,1:T(8,128)(2,1)}, bf16[256,1600]{0,1:T(8,128)(2,1)}, u32[]{:S(2)}, u32[]{:S(2)}) collective-permute-start(bf16[256,1600]{0,1:T(8,128)(2,1)} %copy.141), channel_id=1, source_target_pairs={{0,4},{4,0},{8,12},{12,8},{1,5},{5,1},{9,13},{13,9},{2,6},{6,2},{1... | collective-permute-start | bytes 2457608 | tf_op jit(solution)/shard_map/ppermute | solution.py:651
  1684.5 77.2 %collective-permute-start.65 = (bf16[256,1600]{0,1:T(8,128)(2,1)}, bf16[256,1600]{0,1:T(8,128)(2,1)}, u32[]{:S(2)}, u32[]{:S(2)}) collective-permute-start(bf16[256,1600]{0,1:T(8,128)(2,1)} %copy.140), channel_id=1, source_target_pairs={{0,8},{4,12},{8,0},{12,4},{1,9},{5,13},{9,1},{13,5},{2,10},{6,14},... | collective-permute-start | bytes 2457608 | tf_op jit(solution)/shard_map/ppermute | solution.py:651
  1686.8 78.4 %collective-permute-start.64 = (bf16[256,1600]{0,1:T(8,128)(2,1)}, bf16[256,1600]{0,1:T(8,128)(2,1)}, u32[]{:S(2)}, u32[]{:S(2)}) collective-permute-start(bf16[256,1600]{0,1:T(8,128)(2,1)} %copy.139), channel_id=1, source_target_pairs={{0,12},{4,8},{8,4},{12,0},{1,13},{5,9},{9,5},{13,1},{2,14},{6,10},... | collective-permute-start | bytes 2457608 | tf_op jit(solution)/shard_map/ppermute | solution.py:651
  1741.3 283.1 %collective-permute-start.83 = (bf16[1,104,896]{2,1,0:T(8,128)(2,1)}, bf16[1,104,896]{2,1,0:T(8,128)(2,1)}, u32[]{:S(2)}, u32[]{:S(2)}) collective-permute-start(bf16[1,104,896]{2,1,0:T(8,128)(2,1)} %get-tuple-element.253), channel_id=1, source_target_pairs={{0,1},{1,0},{2,3},{3,2},{4,5},{5,4},{6,7},{7,6},{8,9},{9,8},{10,11... | collective-permute-start | bytes 559112 | tf_op jit(solution)/shard_map/ppermute | solution.py:255
  1761.7 54.1 %collective-permute-start.67 = (bf16[2,512,1024]{2,1,0:T(8,128)(2,1)}, bf16[2,512,1024]{2,1,0:T(8,128)(2,1)}, u32[]{:S(2)}, u32[]{:S(2)}) collective-permute-start(bf16[2,512,1024]{2,1,0:T(8,128)(2,1)} %slice.757), channel_id=1, source_target_pairs={{2,0},{3,1},{6,4},{7,5},{10,8},{11,9},{14,12},{15,13},{18,16},{19,... | collective-permute-start | bytes 6291464 | tf_op jit(solution)/shard_map/ppermute | solution.py:375
  1765.2 83.0 %collective-permute-start.70 = (bf16[1,512,1024]{2,1,0:T(8,128)(2,1)}, bf16[1,512,1024]{2,1,0:T(8,128)(2,1)}, u32[]{:S(2)}, u32[]{:S(2)}) collective-permute-start(bf16[1,512,1024]{2,1,0:T(8,128)(2,1)} %slice.759), channel_id=1, source_target_pairs={{2,0},{3,1},{6,4},{7,5},{10,8},{11,9},{14,12},{15,13},{18,16},{19,... | collective-permute-start | bytes 3145736 | tf_op jit(solution)/shard_map/ppermute | solution.py:375
  1777.9 251.8 %reduce-scatter.17.cloned.1.call-start = ((), (), s32[]{:S(2)}) async-start(), calls=%async_computation.15 | async-start | bytes 5750784 | tf_op jit(solution)/shard_map/reduce_scatter | solution.py:674
  1830.9 37.1 %collective-permute-start.68 = (bf16[2,256,1664]{2,1,0:T(8,128)(2,1)}, bf16[2,256,1664]{2,1,0:T(8,128)(2,1)}, u32[]{:S(2)}, u32[]{:S(2)}) collective-permute-start(bf16[2,256,1664]{2,1,0:T(8,128)(2,1)} %dynamic-slice_bitcast_fusion), channel_id=1, source_target_pairs={{0,16},{16,0},{1,17},{17,1},{2,18},{18,2},{3,19},{19,3},{4,20},{20... | collective-permute-start | bytes 5111816 | tf_op jit(solution)/shard_map/ppermute | solution.py:255
  1853.5 59.3 %collective-permute-start.71 = (bf16[1,256,1664]{2,1,0:T(8,128)(2,1)}, bf16[1,256,1664]{2,1,0:T(8,128)(2,1)}, u32[]{:S(2)}, u32[]{:S(2)}) collective-permute-start(bf16[1,256,1664]{2,1,0:T(8,128)(2,1)} %dynamic-slice_bitcast_fusion.9), channel_id=1, source_target_pairs={{0,16},{16,0},{1,17},{17,1},{2,18},{18,2},{3,19},{19,3},{4,20},{20... | collective-permute-start | bytes 2555912 | tf_op jit(solution)/shard_map/ppermute | solution.py:255
  1871.8 38.6 %collective-permute-start.69 = (bf16[2,256,1664]{2,1,0:T(8,128)(2,1)}, bf16[2,256,1664]{2,1,0:T(8,128)(2,1)}, u32[]{:S(2)}, u32[]{:S(2)}) collective-permute-start(bf16[2,256,1664]{2,1,0:T(8,128)(2,1)} %get-tuple-element.161), channel_id=1, source_target_pairs={{0,1},{1,0},{2,3},{3,2},{4,5},{5,4},{6,7},{7,6},{8,9},{9,8},{10,11... | collective-permute-start | bytes 5111816 | tf_op jit(solution)/shard_map/ppermute | solution.py:255
  1915.6 31.6 %collective-permute-start.72 = (bf16[1,256,1664]{2,1,0:T(8,128)(2,1)}, bf16[1,256,1664]{2,1,0:T(8,128)(2,1)}, u32[]{:S(2)}, u32[]{:S(2)}) collective-permute-start(bf16[1,256,1664]{2,1,0:T(8,128)(2,1)} %get-tuple-element.159), channel_id=1, source_target_pairs={{0,1},{1,0},{2,3},{3,2},{4,5},{5,4},{6,7},{7,6},{8,9},{9,8},{10,11... | collective-permute-start | bytes 2555912 | tf_op jit(solution)/shard_map/ppermute | solution.py:255
  1932.1 37.0 %collective-permute-start.88 = (bf16[208,1664]{1,0:T(8,128)(2,1)}, bf16[208,1664]{1,0:T(8,128)(2,1)}, u32[]{:S(2)}, u32[]{:S(2)}) collective-permute-start(bf16[208,1664]{1,0:T(8,128)(2,1)} %get-tuple-element.209), channel_id=1, source_target_pairs={{0,16},{16,0},{1,17},{17,1},{2,18},{18,2},{3,19},{19,3},{4,20},{20... | collective-permute-start | bytes 2076680 | tf_op jit(solution)/shard_map/ppermute | solution.py:255
  1945.0 45.2 %collective-permute-start.87 = (bf16[2,104,1664]{2,1,0:T(8,128)(2,1)}, bf16[2,104,1664]{2,1,0:T(8,128)(2,1)}, u32[]{:S(2)}, u32[]{:S(2)}) collective-permute-start(bf16[2,104,1664]{2,1,0:T(8,128)(2,1)} %select_select_fusion), channel_id=1, source_target_pairs={{0,16},{16,0},{1,17},{17,1},{2,18},{18,2},{3,19},{19,3},{4,20},{20... | collective-permute-start | bytes 2076680 | tf_op jit(solution)/shard_map/ppermute | solution.py:255
  1962.2 44.0 %collective-permute-start.73 = (bf16[3,256,1600]{1,2,0:T(8,128)(2,1)}, bf16[3,256,1600]{1,2,0:T(8,128)(2,1)}, u32[]{:S(2)}, u32[]{:S(2)}) collective-permute-start(bf16[3,256,1600]{1,2,0:T(8,128)(2,1)} %copy.152), channel_id=1, source_target_pairs={{0,0},{17,1},{1,16},{16,17},{2,2},{19,3},{3,18},{18,19},{4,4},{21,... | collective-permute-start | bytes 7372808 | tf_op jit(solution)/shard_map/ppermute | solution.py:593
  (296 other events, 5131.4 us)
Sparse Core Ops, SparseCore 0:
  13.5 91.1 all-gather.17
  107.5 119.7 all-gather.11
  230.0 97.5 all-gather.13
  344.3 63.2 all-gather.21
  441.7 87.3 all-gather.19
  636.7 106.4 all-gather.15
  830.6 92.4 all-gather.23
  940.1 106.6 reduce-scatter.10
  1147.1 73.6 reduce-scatter.8
  1224.6 121.6 reduce-scatter.12
  1393.2 100.7 reduce-scatter.14
  1497.8 106.6 reduce-scatter.20
  1608.5 155.6 reduce-scatter.22
  1778.0 97.2 reduce-scatter.18
  1884.6 104.3 reduce-scatter.16
